TPU v7x, 32 devices: a whole 2x2x4 slice. The times are simulated.
32 devices in a mesh: bl: 8 (over y, x, core), dir: 4 (over z).
Axes of the slice: x: 2, y: 2, z: 4, core: 2. Of those that a mesh axis runs over, the one named last changes fastest.
Arguments:
- visibilities: float32 [8, 16, 2048], P(None, 'dir', 'bl'), may hold values from -24 to 24
- coherencies: bfloat16 [32, 8, 16, 2048], P('dir', None, None, 'bl'), may hold values from -6 to 6
- gain_offsets: float32 [32, 8, 512], P(None, None, 'bl'), may hold values from -1.5 to 1.5
- stations: int32 [2, 2048], P(None, 'bl'), may hold values from 0 to 511, as said below
- solve_order: int32 [32], replicated, may hold values from 0 to 31, each once
- counts: int32 [32], replicated, may hold values from 1 to 2
- damping: int32 [32], replicated, may hold values from 1 to 8
Outputs:
- gains: float32 [32, 8, 512], P(None, None, 'bl')
- residual: float32 [8, 16, 2048], P(None, 'dir', 'bl')
Inputs may be any that keep to these rules, and one draw needn't show every extreme that they name: Each baseline names two different stations. `solve_order`: each direction appears once.
All inputs are finite; a program needn't handle non-finite values.
Results may differ from a plain program's by a relative error of at most 0.0003.
Values may be sent and summed in bfloat16 or wider, within the bound.
No kernel may reach another device: no remote copies, remote signals or barrier semaphores. Data moves between devices by JAX's collectives and lax.ppermute only.
A program may use at most 64 MiB of HBM per device.

v0:
```python
import functools

import jax
import jax.numpy as jnp
from jax import lax
from jax.experimental import pallas as pl
from jax.experimental.pallas import tpu as pltpu
from jax.sharding import PartitionSpec as P

LM_ITERS = 2
SOLVED = 4
F32 = jnp.float32
BF16 = jnp.bfloat16
VMEM_BYTES = 24 * 1024 * 1024
GRAM = [(u, v) for u in range(4) for v in range(u, 4)]
M_ROWS = 32
K_ROWS = 16
FIRST = 1


def mul(x, y):
    return (x[0] * y[0] - x[1] * y[1], x[0] * y[1] + x[1] * y[0])


def add(x, y):
    return (x[0] + y[0], x[1] + y[1])


def sub(x, y):
    return (x[0] - y[0], x[1] - y[1])


def conj(x):
    return (x[0], -x[1])


def total(terms):
    return functools.reduce(add, terms)


def mul_conj(x, y):
    return (x[0] * y[0] + x[1] * y[1], x[1] * y[0] - x[0] * y[1])


def matmul(left, right):
    return [add(mul(left[2 * i], right[j]), mul(left[2 * i + 1], right[2 + j])) for i in (0, 1) for j in (0, 1)]


def matmul_adj(left, right):
    return [
        add(mul_conj(left[2 * i], right[2 * j]), mul_conj(left[2 * i + 1], right[2 * j + 1]))
        for i in (0, 1)
        for j in (0, 1)
    ]


def apply_gains(gain_p, coher, gain_q):
    return matmul_adj(matmul(gain_p, coher), gain_q)


def as_matrix(parts):
    return [(parts[2 * e], parts[2 * e + 1]) for e in range(4)]


def split_rows(values):
    high = values.astype(BF16)
    low = (values - high.astype(F32)).astype(BF16)
    return jnp.concatenate([high, low], axis=0)


def one_hot(stations_p, stations_q, count):
    both = jnp.concatenate([stations_p, stations_q], axis=1)
    rows = lax.broadcasted_iota(jnp.int32, (count, both.shape[1]), 0)
    return jnp.where(rows == both, 1.0, 0.0).astype(BF16)


def pick(one_hots, values):
    count = values.shape[0]
    out = jnp.dot(split_rows(values), one_hots, preferred_element_type=F32)
    return out[:count] + out[count:]


def prep_kernel(order_ref, stations_ref, offs_ref, *refs, owned, per):
    *coher_refs, out_ref, first_ref, rest_ref = refs
    lane = lax.axis_index("dir")
    width = offs_ref.shape[2]
    station_rows = 2 * stations_ref.shape[1] // 128
    part_rows = out_ref.shape[0] - 8
    comp = lax.broadcasted_iota(jnp.int32, (8, width), 0)
    ident = jnp.where((comp == 0) | (comp == 6), 1.0, 0.0)
    places = [lane * owned + d for d in range(owned)] + [order_ref[i] for i in range(SOLVED)]
    blocks = [offs_ref[place] + ident for place in places]
    while len(blocks) * 8 < part_rows * per:
        blocks.append(jnp.zeros((8, width), F32))
    each = part_rows // 8
    columns = [jnp.concatenate(blocks[q * each : (q + 1) * each], axis=0) for q in range(per)]
    out_ref[:part_rows] = jnp.concatenate(columns, axis=1)
    out_ref[part_rows:] = jnp.zeros((8, 128), F32)
    for row in range(station_rows):
        end, tile = row // (station_rows // 2), row % (station_rows // 2)
        out_ref[part_rows + row : part_rows + row + 1] = stations_ref[end : end + 1, tile * 128 : tile * 128 + 128].astype(F32)
    for i in range(SOLVED):
        mine = order_ref[i] // owned == lane
        value = jnp.where(mine, coher_refs[i][0], jnp.zeros_like(coher_refs[i][0]))
        if i < FIRST:
            first_ref[i] = value
        else:
            rest_ref[i - FIRST] = value


def fill_table(blocks_ref, table, width):
    groups, rows, lanes = blocks_ref.shape
    part_rows = rows - 8
    per = lanes // width
    lane_of = lax.broadcasted_iota(jnp.int32, (part_rows, lanes), 1) // width
    for tile in range(groups * width // lanes):
        for q in range(per):
            tile_rows = jnp.zeros((part_rows, lanes), F32)
            for u in range(per):
                block = blocks_ref[per * tile + u, :part_rows]
                shift = ((u - q) * width) % lanes
                if shift:
                    block = pltpu.roll(block, shift, 1)
                tile_rows = jnp.where(lane_of == u, block, tile_rows)
            table[q * part_rows : (q + 1) * part_rows, tile * lanes : (tile + 1) * lanes] = tile_rows


def block_stations(blocks_ref, g, tiles, base):
    part_rows = blocks_ref.shape[1] - 8
    rows = blocks_ref[g, part_rows:, :].astype(jnp.int32) ^ base
    return [jnp.concatenate([rows[end * tiles + t : end * tiles + t + 1] for t in range(tiles)], axis=1) for end in (0, 1)]


def lookup_kernel(blocks_ref, hots_ref, ends_ref, start_ref, table, *, width, owned):
    groups = blocks_ref.shape[0]
    baselines = hots_ref.shape[2] // 2
    tiles = baselines // 128
    base = lax.axis_index("bl").astype(jnp.int32) * width
    fill_table(blocks_ref, table, width)
    start = table[owned * 8 : (owned + SOLVED) * 8, :]
    start_ref[...] = start
    split = split_rows(start)
    for g in range(groups):
        half = groups // 2
        rows_p, rows_q = block_stations(blocks_ref, 2 * (g % half) + g // half, tiles, base)
        hots_ref[g] = one_hot(rows_p, rows_q, groups * width)
        out = jnp.dot(split, hots_ref[g], preferred_element_type=F32)
        out = out[: SOLVED * 8] + out[SOLVED * 8 :]
        for i in range(SOLVED):
            for end in (0, 1):
                for t in range(tiles):
                    chunk, column = (g * tiles + t) * 8, (end * tiles + t) * 128
                    ends_ref[i, end, chunk : chunk + 8, :] = out[i * 8 : i * 8 + 8, column : column + 128]


def model_kernel(blocks_ref, coher_ref, vis_ref, part_ref, begin_ref, *refs, width):
    *piece_refs, table, ends = refs
    owned = coher_ref.shape[0]
    baselines = coher_ref.shape[3]
    channels = vis_ref.shape[1]
    lane = lax.axis_index("dir")
    base = lax.axis_index("bl").astype(jnp.int32) * width
    fill_table(blocks_ref, table, width)
    rows_p, rows_q = block_stations(blocks_ref, 0, baselines // 128, base)
    ends[...] = pick(one_hot(rows_p, rows_q, table.shape[1]), table[...])
    begin_ref[...] = ends[owned * 8 : (owned + SOLVED) * 8, :]

    for half in range(baselines // 128):
        at = pl.ds(half * 128, 128)
        at_q = pl.ds(baselines + half * 128, 128)

        def gain(row, where):
            block = ends[pl.ds(pl.multiple_of(row, 8), 8), where]
            return as_matrix([block[c : c + 1] for c in range(8)])

        def add_model(d, acc):
            coher = as_matrix([coher_ref[d, c, :, at].astype(F32) for c in range(8)])
            model = apply_gains(gain(d * 8, at), coher, gain(d * 8, at_q))
            return [sub(x, y) for x, y in zip(acc, model)]

        zeros = jnp.zeros((coher_ref.shape[2], 128), F32)
        acc = lax.fori_loop(0, owned, add_model, [(zeros, zeros)] * 4)
        for c in range(8):
            total_part = acc[c // 2][c % 2]
            lanes = [total_part[x * channels : (x + 1) * channels] for x in range(len(piece_refs))]
            vis = vis_ref[c, :, at]
            for k, piece_ref in enumerate(piece_refs):
                value = lanes[0]
                for x in range(1, len(lanes)):
                    value = jnp.where(lane ^ k == x, lanes[x], value)
                piece_ref[c, :, at] = value + vis if k == 0 else value
            part_ref[c, :, at] = jnp.concatenate([jnp.where(lane == x, y + vis, y) for x, y in enumerate(lanes)], axis=0)


def summed(values):
    return jnp.sum(values, axis=0, keepdims=True)


def target_kernel(order_ref, part_ref, solved_ref, begin_ref, m_ref, *, owned, low):
    baselines = part_ref.shape[2]
    lane = lax.axis_index("dir")
    for half in range(baselines // 128):
        at = pl.ds(half * 128, 128)
        for i in range(solved_ref.shape[0]):
            coher = as_matrix([solved_ref[i, c, :, at].astype(F32) for c in range(8)])
            row = (low + i) * 8
            gain_p, gain_q = [
                as_matrix([begin_ref[row + c : row + c + 1, pl.ds(end * baselines + half * 128, 128)] for c in range(8)])
                for end in (0, 1)
            ]
            model = apply_gains(gain_p, coher, gain_q)
            flag = (order_ref[low + i] // owned == lane).astype(F32)
            target = [
                (part_ref[2 * e, :, at] + flag * model[e][0], part_ref[2 * e + 1, :, at] + flag * model[e][1])
                for e in range(4)
            ]
            out = i * M_ROWS
            for u in range(4):
                for v in range(4):
                    value = mul_conj(target[u], coher[v])
                    m_ref[half, out : out + 1, :] = summed(value[0])
                    m_ref[half, out + 1 : out + 2, :] = summed(value[1])
                    out += 2


def pair_list(low):
    return [(m, i) for i in range(low, SOLVED) for m in range(i)]


def product_kernel(*refs, low):
    *solved_refs, kx_ref, own_ref = refs
    where = [(ref, i) for ref in solved_refs for i in range(ref.shape[0])]
    baselines = solved_refs[0].shape[3]
    channels = own_ref.shape[2]
    lane = lax.axis_index("dir")
    for half in range(baselines // 128):
        at = pl.ds(half * 128, 128)

        def load(i):
            ref, place = where[i]
            return [ref[place, c, :, at].astype(F32) for c in range(8)]

        out = 0
        for i in range(low, len(where)):
            parts = load(i)
            for c in range(8):
                mine = parts[c][:channels]
                for x in range(1, parts[c].shape[0] // channels):
                    mine = jnp.where(lane == x, parts[c][x * channels : (x + 1) * channels], mine)
                own_ref[i - low, c, :, at] = mine
            coher = as_matrix(parts)
            for u, v in GRAM:
                value = mul_conj(coher[u], coher[v])
                kx_ref[half, out : out + 1, :] = summed(value[0])
                out += 1
                if u != v:
                    kx_ref[half, out : out + 1, :] = summed(value[1])
                    out += 1
        if low == 0:
            continue
        for m, i in pair_list(low):
            coher, other = as_matrix(load(i)), as_matrix(load(m))
            for u in range(4):
                for v in range(4):
                    value = mul_conj(other[u], coher[v])
                    kx_ref[half, out : out + 1, :] = summed(value[0])
                    kx_ref[half, out + 1 : out + 2, :] = summed(value[1])
                    out += 2


def sweep_kernel(order_ref, counts_ref, damping_ref, *refs, low, high, tiles, factor, last):
    hots, begin, start_ref = refs[:3]
    near_m, far_m, near_kx, far_kx = refs[3:7]
    refs = refs[7:]
    if last:
        earlier, earlier_gains, earlier_after, offs_ref, own_a, own_b = refs[:6]
        pieces = refs[6:-8]
        gains_ref, out_ref = refs[-8:-6]
    else:
        solved_ref, moved_ref, after_ref = refs[:3]
    ends, values, state, m_now, k_now, moved = refs[-6:]
    groups, count = hots.shape[:2]
    chunks = groups * tiles
    kx_stride = near_kx.shape[0] // (chunks // 2)
    m_stride = near_m.shape[0] // (chunks // 2)
    x_start = kx_stride - M_ROWS * len(pair_list(low)) if low else 0
    k_start = 0 if low else high * M_ROWS

    def m_at(row):
        return jnp.concatenate([ref[pl.ds(row, chunks // 2, stride=m_stride), :] for ref in (near_m, far_m)], axis=0)

    def kx_at(row):
        return jnp.concatenate([ref[pl.ds(row, chunks // 2, stride=kx_stride), :] for ref in (near_kx, far_kx)], axis=0)

    def fetch(gain_now, only=None):
        split = split_rows(gain_now)
        for g in range(groups if only is None else only):
            out = jnp.dot(split, hots[g], preferred_element_type=F32)
            out = out[:8] + out[8:]
            for end in (0, 1):
                for t in range(tiles):
                    chunk, column = (g * tiles + t) * 8, (end * tiles + t) * 128
                    ends[end, chunk : chunk + 8, :] = out[:, column : column + 128]

    def gain_at(ref):
        return [as_matrix([ref[end, pl.ds(c, chunks, stride=8), :] for c in range(8)]) for end in (0, 1)]

    def load_m():
        return [[(m_now[(u * 4 + v) * 2], m_now[(u * 4 + v) * 2 + 1]) for v in range(4)] for u in range(4)]

    def load_k():
        row = 0
        gram = {}
        for u, v in GRAM:
            if u == v:
                gram[u, v] = (k_now[row], None)
                row += 1
            else:
                gram[u, v] = (k_now[row], k_now[row + 1])
                gram[v, u] = conj(gram[u, v])
                row += 2
        return gram

    def prepare(i):
        for row in range(K_ROWS):
            k_now[row] = kx_at(k_start + (i - low) * K_ROWS + row)
        for out in range(4):
            for w in range(4):
                row = (out * 4 + w) * 2
                value = (m_at((i - low) * M_ROWS + row), m_at((i - low) * M_ROWS + row + 1))
                for m in range(i):
                    base = x_start + pair_list(low).index((m, i)) * M_ROWS
                    source = moved.at[m - low] if m >= low else earlier.at[m]
                    for uv in range(4):
                        delta = (source[(out * 4 + uv) * 2], source[(out * 4 + uv) * 2 + 1])
                        at = base + (uv * 4 + w) * 2
                        value = add(value, mul(delta, (kx_at(at), kx_at(at + 1))))
                m_now[row] = value[0]
                m_now[row + 1] = value[1]

    def hermitian(gain):
        a = gain[0][0] ** 2 + gain[0][1] ** 2 + gain[2][0] ** 2 + gain[2][1] ** 2
        d = gain[1][0] ** 2 + gain[1][1] ** 2 + gain[3][0] ** 2 + gain[3][1] ** 2
        cross = add(mul_conj(gain[1], gain[0]), mul_conj(gain[3], gain[2]))
        return a, d, cross

    def normal_terms():
        gain_p, gain_q = gain_at(ends)
        m = load_m()
        k = load_k()
        for end, gain, other in ((0, gain_q, False), (1, gain_p, True)):
            row = 0
            for r in (0, 1):
                for c in (0, 1):
                    if other:
                        terms = [mul_conj(gain[2 * a + b], m[2 * a + r][2 * b + c]) for a in (0, 1) for b in (0, 1)]
                    else:
                        terms = [mul(gain[2 * a + b], m[2 * r + a][2 * c + b]) for a in (0, 1) for b in (0, 1)]
                    value = total(terms)
                    values[end, pl.ds(row, chunks, stride=16), :] = value[0]
                    values[end, pl.ds(row + 1, chunks, stride=16), :] = value[1]
                    row += 2
            a, d, cross = hermitian(gain)
            for r, c in ((0, 0), (1, 1), (0, 1)):
                if other:
                    kk = [[k[2 * x + r, 2 * y + c] for y in (0, 1)] for x in (0, 1)]
                    kk = [[(z[0], None if z[1] is None else -z[1]) for z in line] for line in kk]
                else:
                    kk = [[k[2 * r + x, 2 * c + y] for y in (0, 1)] for x in (0, 1)]
                real = a * kk[0][0][0] + d * kk[1][1][0]
                real += cross[0] * (kk[0][1][0] + kk[1][0][0])
                minus = None
                if kk[0][1][1] is not None:
                    minus = kk[1][0][1] - kk[0][1][1]
                    real += cross[1] * minus
                values[end, pl.ds(row, chunks, stride=16), :] = real
                row += 1
                if r != c:
                    imag = cross[1] * (kk[0][1][0] - kk[1][0][0])
                    if kk[0][0][1] is not None:
                        imag += a * kk[0][0][1]
                    if kk[1][1][1] is not None:
                        imag += d * kk[1][1][1]
                    if kk[0][1][1] is not None:
                        imag += cross[0] * kk[0][1][1]
                    if kk[1][0][1] is not None:
                        imag += cross[0] * kk[1][0][1]
                    values[end, pl.ds(row, chunks, stride=16), :] = imag
                    row += 1

    def station_sums():
        acc = jnp.zeros((32, count), F32)
        for g in range(groups):
            starts = [(end, (g * tiles + t) * 16) for end in (0, 1) for t in range(tiles)]
            split = split_rows(jnp.concatenate([values[end, at : at + 16, :] for end, at in starts], axis=1))
            acc += lax.dot_general(split, hots[g], (((1,), (1,)), ((), ())), preferred_element_type=F32)
        return acc[:16] + acc[16:]

    def solve(sums, gain_now, damp):
        numer = sums[:8] + damp * gain_now
        numer = as_matrix([numer[c : c + 1] for c in range(8)])
        diag_a = sums[8:9] + damp
        diag_d = sums[9:10] + damp
        cross_r = sums[10:11]
        cross_i = sums[11:12]
        scale = 1.0 / (diag_a * diag_d - cross_r * cross_r - cross_i * cross_i)
        rows = []
        for r in (0, 1):
            x, y = numer[2 * r], numer[2 * r + 1]
            low = mul(y, (cross_r, -cross_i))
            high = mul(x, (cross_r, cross_i))
            rows += [x[0] * diag_d - low[0], x[1] * diag_d - low[1]]
            rows += [y[0] * diag_a - high[0], y[1] * diag_a - high[1]]
        return jnp.concatenate([value * scale for value in rows], axis=0)

    def add_change(i, coher_ref, after):
        for tile in range(tiles):
            at = pl.ds(tile * 128, 128)
            coher = as_matrix([coher_ref[c, :, at] for c in range(8)])
            rows = [tile * 8 + c for c in range(8)]
            one = [as_matrix([begin[i, end, row : row + 1, :] for row in rows]) for end in (0, 1)]
            two = [as_matrix([after[end, row : row + 1, :] for row in rows]) for end in (0, 1)]
            before, now = apply_gains(one[0], coher, one[1]), apply_gains(two[0], coher, two[1])
            for e in range(4):
                change = sub(before[e], now[e])
                out_ref[2 * e, :, at] += change[0]
                out_ref[2 * e + 1, :, at] += change[1]

    width = offs_ref.shape[2] if last else None
    if last:
        comp = lax.broadcasted_iota(jnp.int32, (8, width), 0)
        gains_ref[...] = offs_ref[...] + jnp.where((comp == 0) | (comp == 6), 1.0, 0.0)[None]
        out_ref[...] = functools.reduce(lambda x, y: x + y, [piece[...] for piece in pieces])
        for i in range(low):
            gains_ref[order_ref[i]] = earlier_gains[i, :, :width]
            add_change(i, own_a.at[i], earlier_after.at[i])
    values[...] = jnp.zeros(values.shape, F32)
    for i in range(low, high):
        which = order_ref[i]
        damp = damping_ref[which].astype(F32) * factor
        state[...] = start_ref[i * 8 : i * 8 + 8, :]
        ends[...] = begin[i]
        prepare(i)

        def one_round():
            normal_terms()
            state[...] = solve(station_sums(), state[...], damp)

        def more(r, carry):
            one_round()
            fetch(state[...])
            return carry

        lax.fori_loop(0, jnp.minimum(counts_ref[which], LM_ITERS) - 1, more, jnp.int32(0))
        one_round()
        if last:
            gains_ref[which] = state[:, :width]
            fetch(state[...], 1 if i + 1 == high else None)
            add_change(i, own_b.at[i - low], ends)
        else:
            solved_ref[i - low] = state[...]
            fetch(state[...])
            after_ref[i - low] = ends[:, : tiles * 8, :]
        if i + 1 == SOLVED:
            break
        p0, q0 = gain_at(begin.at[i])
        p1, q1 = gain_at(ends)
        store = moved if last else moved_ref
        for a in (0, 1):
            for b in (0, 1):
                for u in (0, 1):
                    for v in (0, 1):
                        delta = sub(mul_conj(p0[2 * a + u], q0[2 * b + v]), mul_conj(p1[2 * a + u], q1[2 * b + v]))
                        row = ((2 * a + b) * 4 + 2 * u + v) * 2
                        store[i - low, row] = delta[0]
                        store[i - low, row + 1] = delta[1]


def exchange(block, axis, mask):
    return lax.ppermute(block, axis, [(i, i ^ mask) for i in range(lax.axis_size(axis))])


def butterfly_sum(value, axis):
    mask = 1
    while mask < lax.axis_size(axis):
        value = value + exchange(value, axis, mask)
        mask *= 2
    return value


def chip_blocks(block, axis):
    chips = lax.axis_size(axis) // 2
    if chips <= 4:
        return jnp.stack([block] + [exchange(block, axis, 2 * j) for j in range(1, chips)])
    parts = block[None]
    while parts.shape[0] < chips:
        parts = jnp.concatenate([parts, exchange(parts, axis, 2 * parts.shape[0])], axis=0)
    return parts


def on_device(visibilities, coherencies, gain_offsets, stations, solve_order, counts, damping):
    groups = lax.axis_size("bl")
    owned, _, channel_count, baselines = coherencies.shape
    channels = visibilities.shape[1]
    width = gain_offsets.shape[2]
    count = groups * width
    tiles = baselines // 128
    lanes = lax.axis_size("dir")
    params = pltpu.CompilerParams(vmem_limit_bytes=VMEM_BYTES)
    rest = SOLVED - FIRST

    def call(kernel, name, shapes, scalars, arrays, scratch=(), **static):
        return pl.pallas_call(
            functools.partial(kernel, **static),
            out_shape=[jax.ShapeDtypeStruct(*shape) for shape in shapes],
            in_specs=[pl.BlockSpec(memory_space=pltpu.SMEM)] * len(scalars)
            + [pl.BlockSpec(memory_space=pltpu.VMEM)] * len(arrays),
            out_specs=[pl.BlockSpec(memory_space=pltpu.VMEM)] * len(shapes),
            scratch_shapes=[pltpu.VMEM(*shape) for shape in scratch],
            compiler_params=params,
            name=name,
        )(*scalars, *arrays)

    per = 128 // width
    part_rows = -(-(owned + SOLVED) // per) * 8
    block = coherencies.shape[1:]
    whole = lambda shape: pl.BlockSpec(shape, lambda g, order: (0,) * len(shape))
    picked = lambda i: pl.BlockSpec((1,) + block, lambda g, order: (order[i] % owned, 0, 0, 0))
    shapes = [(part_rows + 8, 128), (FIRST,) + block, (rest,) + block]
    packed, chosen_first, chosen_rest = pl.pallas_call(
        functools.partial(prep_kernel, owned=owned, per=per),
        out_shape=[jax.ShapeDtypeStruct(shape, dtype) for shape, dtype in zip(shapes, (F32, BF16, BF16))],
        grid_spec=pltpu.PrefetchScalarGridSpec(
            num_scalar_prefetch=1,
            grid=(1,),
            in_specs=[whole(stations.shape), whole(gain_offsets.shape)] + [picked(i) for i in range(SOLVED)],
            out_specs=[whole(shape) for shape in shapes],
        ),
        compiler_params=params,
        name="prepare",
    )(solve_order, stations, gain_offsets, *[coherencies] * SOLVED)

    near = chip_blocks(packed, "bl")
    blocks = jnp.stack([near, exchange(near, "bl", 1)], axis=1).reshape(groups, part_rows + 8, 128)
    shared_first = butterfly_sum(chosen_first, "dir")
    shared_rest = butterfly_sum(chosen_rest, "dir")

    table = ((part_rows * per, count), F32)
    part, begin, *pieces = call(
        model_kernel,
        "first_model",
        [((8, channel_count, baselines), F32), ((SOLVED * 8, 2 * baselines), F32)] + [(visibilities.shape, F32)] * lanes,
        [],
        [blocks, coherencies, visibilities],
        [table, ((part_rows * per, 2 * baselines), F32)],
        width=width,
    )
    [m_first] = call(
        target_kernel, "first_target", [((tiles, FIRST * M_ROWS, 128), F32)], [solve_order],
        [part, shared_first, begin], owned=owned, low=0,
    )
    k_first, own_first = call(
        product_kernel, "first_products",
        [((tiles, FIRST * K_ROWS, 128), F32), ((FIRST, 8, channels, baselines), F32)], [], [shared_first], low=0,
    )
    hots, ends, start = call(
        lookup_kernel, "lookup",
        [
            ((groups, count, 2 * baselines), BF16),
            ((SOLVED, 2, groups * tiles * 8, 128), F32),
            ((SOLVED * 8, count), F32),
        ],
        [], [blocks], [table], width=width, owned=owned,
    )
    [m_rest] = call(
        target_kernel, "other_targets", [((tiles, rest * M_ROWS, 128), F32)], [solve_order],
        [part, shared_rest, begin], owned=owned, low=FIRST,
    )
    kx_rows = rest * K_ROWS + len(pair_list(FIRST)) * M_ROWS
    kx_rest, own_rest = call(
        product_kernel, "other_products",
        [((tiles, kx_rows, 128), F32), ((rest, 8, channels, baselines), F32)], [], [shared_first, shared_rest], low=FIRST,
    )

    first_near = chip_blocks(jnp.concatenate([butterfly_sum(m_first, "dir"), k_first], axis=1), "bl")
    first_far = exchange(first_near, "bl", 1)
    pieces = [pieces[0]] + [exchange(piece, "dir", k) for k, piece in enumerate(pieces) if k]
    kx_near = chip_blocks(kx_rest, "bl")
    kx_far = exchange(kx_near, "bl", 1)
    m_near = chip_blocks(butterfly_sum(m_rest, "dir"), "bl")
    m_far = exchange(m_near, "bl", 1)

    chunks = groups * tiles
    static = dict(tiles=tiles, factor=baselines * groups * channel_count / count)
    scratch = [
        ((2, chunks * 8, 128), F32),
        ((2, chunks * 16, 128), F32),
        ((8, count), F32),
        ((M_ROWS, chunks, 128), F32),
        ((K_ROWS, chunks, 128), F32),
    ]
    flat = lambda *arrays: [array.reshape(-1, 128) for array in arrays]
    scalars = [solve_order, counts, damping]
    solved_first, moved_first, after_first = call(
        sweep_kernel, "first_sweep",
        [((FIRST, 8, count), F32), ((FIRST, M_ROWS, chunks, 128), F32), ((FIRST, 2, tiles * 8, 128), F32)],
        scalars,
        [hots, ends, start] + flat(first_near, first_far, first_near, first_far),
        scratch + [((1, 8, 128), F32)],
        low=0, high=FIRST, last=False, **static,
    )
    gains, residual = call(
        sweep_kernel, "other_sweeps",
        [(gain_offsets.shape, F32), (visibilities.shape, F32)],
        scalars,
        [hots, ends, start] + flat(m_near, m_far, kx_near, kx_far)
        + [moved_first, solved_first, after_first, gain_offsets, own_first, own_rest] + pieces,
        scratch + [((rest, M_ROWS, chunks, 128), F32)],
        low=FIRST, high=SOLVED, last=True, **static,
    )
    return gains, residual


def solution(mesh):
    return jax.shard_map(
        on_device,
        mesh=mesh,
        in_specs=(
            P(None, "dir", "bl"),
            P("dir", None, None, "bl"),
            P(None, None, "bl"),
            P(None, "bl"),
            P(),
            P(),
            P(),
        ),
        out_specs=(P(None, None, "bl"), P(None, "dir", "bl")),
        check_vma=False,
    )
```

profile of v0, /device:TPU:0, one launch (start us, length us, event | category | flops | bytes accessed | tf_op | source)
XLA Modules:
  0.0 99.7 jit_solution(6883485863780032121)
XLA Ops:
  4.6 3.1 %collective-permute-start.4 = (bf16[3,8,16,256]{3,2,1,0:T(8,128)(2,1)S(1)}, bf16[3,8,16,256]{3,2,1,0:T(8,128)(2,1)S(1)}, u32[]{:S(2)}, u32[]{:S(2)}) collective-permute-start(bf16[3,8,16,256]{3,2,1,0:T(8,128)(2,1)S(1)} %get-tuple-element.26), channel_id=1, source_target_pairs={{0,1},{1,0},{2,3},{3,2},{4,5},{5,4},{6,7},{7,6},{8,9},{9,8},{10,11... | collective-permute-start | bytes 589832 | tf_op jit(solution)/shard_map/ppermute | solution.py:480
  7.6 4.9 %collective-permute-done.4 = bf16[3,8,16,256]{3,2,1,0:T(8,128)(2,1)S(1)} collective-permute-done((bf16[3,8,16,256]{3,2,1,0:T(8,128)(2,1)S(1)}, bf16[3,8,16,256]{3,2,1,0:T(8,128)(2,1)S(1)}, u32[]{:S(2)}, u32[]{:S(2)}) %collective-permute-start.4) | collective-permute-done | bytes 196640 | tf_op jit(solution)/shard_map/ppermute | solution.py:480
  12.6 2.8 %collective-permute-start.5 = (bf16[3,8,16,256]{3,2,1,0:T(8,128)(2,1)S(1)}, bf16[3,8,16,256]{3,2,1,0:T(8,128)(2,1)S(1)}, u32[]{:S(2)}, u32[]{:S(2)}) collective-permute-start(bf16[3,8,16,256]{3,2,1,0:T(8,128)(2,1)S(1)} %add.24), channel_id=1, source_target_pairs={{0,2},{1,3},{2,0},{3,1},{4,6},{5,7},{6,4},{7,5},{8,10},{9,11},{10,... | collective-permute-start | bytes 589832 | tf_op jit(solution)/shard_map/ppermute | solution.py:480
  15.4 1.6 %collective-permute-start.12 = (bf16[1,8,16,256]{3,2,1,0:T(8,128)(2,1)S(1)}, bf16[1,8,16,256]{3,2,1,0:T(8,128)(2,1)S(1)}, u32[]{:S(2)}, u32[]{:S(2)}) collective-permute-start(bf16[1,8,16,256]{3,2,1,0:T(8,128)(2,1)S(1)} %get-tuple-element.28), channel_id=1, source_target_pairs={{0,1},{1,0},{2,3},{3,2},{4,5},{5,4},{6,7},{7,6},{8,9},{9,8},{10,11... | collective-permute-start | bytes 196616 | tf_op jit(solution)/shard_map/ppermute | solution.py:480
  17.0 3.2 %collective-permute-done.12 = bf16[1,8,16,256]{3,2,1,0:T(8,128)(2,1)S(1)} collective-permute-done((bf16[1,8,16,256]{3,2,1,0:T(8,128)(2,1)S(1)}, bf16[1,8,16,256]{3,2,1,0:T(8,128)(2,1)S(1)}, u32[]{:S(2)}, u32[]{:S(2)}) %collective-permute-start.12) | collective-permute-done | bytes 65568 | tf_op jit(solution)/shard_map/ppermute | solution.py:480
  20.2 2.4 %collective-permute-start.13 = (bf16[1,8,16,256]{3,2,1,0:T(8,128)(2,1)S(1)}, bf16[1,8,16,256]{3,2,1,0:T(8,128)(2,1)S(1)}, u32[]{:S(2)}, u32[]{:S(2)}) collective-permute-start(bf16[1,8,16,256]{3,2,1,0:T(8,128)(2,1)S(1)} %add.28), channel_id=1, source_target_pairs={{0,2},{1,3},{2,0},{3,1},{4,6},{5,7},{6,4},{7,5},{8,10},{9,11},{10,... | collective-permute-start | bytes 196616 | tf_op jit(solution)/shard_map/ppermute | solution.py:480
  22.6 3.3 %collective-permute-done.13 = bf16[1,8,16,256]{3,2,1,0:T(8,128)(2,1)S(1)} collective-permute-done((bf16[1,8,16,256]{3,2,1,0:T(8,128)(2,1)S(1)}, bf16[1,8,16,256]{3,2,1,0:T(8,128)(2,1)S(1)}, u32[]{:S(2)}, u32[]{:S(2)}) %collective-permute-start.13) | collective-permute-done | bytes 65568 | tf_op jit(solution)/shard_map/ppermute | solution.py:480
  27.0 1.4 %collective-permute-start.14 = (f32[2,240,128]{2,1,0:T(8,128)S(1)}, f32[2,240,128]{2,1,0:T(8,128)S(1)}, u32[]{:S(2)}, u32[]{:S(2)}) collective-permute-start(f32[2,240,128]{2,1,0:T(8,128)S(1)} %get-tuple-element.29), channel_id=1, source_target_pairs={{0,8},{4,12},{8,0},{12,4},{16,24},{20,28},{24,16},{28,20},{1,9},{5... | collective-permute-start | bytes 737288 | tf_op jit(solution)/shard_map/ppermute | solution.py:480
  28.4 1.5 %collective-permute-start.15 = (f32[2,240,128]{2,1,0:T(8,128)S(1)}, f32[2,240,128]{2,1,0:T(8,128)S(1)}, u32[]{:S(2)}, u32[]{:S(2)}) collective-permute-start(f32[2,240,128]{2,1,0:T(8,128)S(1)} %get-tuple-element.29), channel_id=1, source_target_pairs={{0,16},{4,20},{8,24},{12,28},{16,0},{20,4},{24,8},{28,12},{1,17},{... | collective-permute-start | bytes 737288 | tf_op jit(solution)/shard_map/ppermute | solution.py:480
  30.6 1.3 %collective-permute-start = (f32[56,128]{1,0:T(8,128)S(1)}, f32[56,128]{1,0:T(8,128)S(1)}, u32[]{:S(2)}, u32[]{:S(2)}) collective-permute-start(f32[56,128]{1,0:T(8,128)S(1)} %get-tuple-element.21), channel_id=1, source_target_pairs={{0,8},{4,12},{8,0},{12,4},{16,24},{20,28},{24,16},{28,20},{1,9},{5... | collective-permute-start | bytes 86024 | tf_op jit(solution)/shard_map/ppermute | solution.py:480
  31.9 1.5 %collective-permute-start.1 = (f32[56,128]{1,0:T(8,128)S(1)}, f32[56,128]{1,0:T(8,128)S(1)}, u32[]{:S(2)}, u32[]{:S(2)}) collective-permute-start(f32[56,128]{1,0:T(8,128)S(1)} %get-tuple-element.21), channel_id=1, source_target_pairs={{0,16},{4,20},{8,24},{12,28},{16,0},{20,4},{24,8},{28,12},{1,17},{... | collective-permute-start | bytes 86024 | tf_op jit(solution)/shard_map/ppermute | solution.py:480
  33.4 6.5 %collective-permute-done = f32[56,128]{1,0:T(8,128)S(1)} collective-permute-done((f32[56,128]{1,0:T(8,128)S(1)}, f32[56,128]{1,0:T(8,128)S(1)}, u32[]{:S(2)}, u32[]{:S(2)}) %collective-permute-start) | collective-permute-done | bytes 28704 | tf_op jit(solution)/shard_map/ppermute | solution.py:480
  39.9 2.1 %collective-permute-start.2 = (f32[56,128]{1,0:T(8,128)S(1)}, f32[56,128]{1,0:T(8,128)S(1)}, u32[]{:S(2)}, u32[]{:S(2)}) collective-permute-start(f32[56,128]{1,0:T(8,128)S(1)} %get-tuple-element.21), channel_id=1, source_target_pairs={{0,24},{4,28},{8,16},{12,20},{16,8},{20,12},{24,0},{28,4},{1,25},{... | collective-permute-start | bytes 86024 | tf_op jit(solution)/shard_map/ppermute | solution.py:480
  42.1 2.6 %collective-permute-done.2 = f32[56,128]{1,0:T(8,128)S(1)} collective-permute-done((f32[56,128]{1,0:T(8,128)S(1)}, f32[56,128]{1,0:T(8,128)S(1)}, u32[]{:S(2)}, u32[]{:S(2)}) %collective-permute-start.2) | collective-permute-done | bytes 28704 | tf_op jit(solution)/shard_map/ppermute | solution.py:480
  46.2 1.0 %first_model.1 = (f32[8,16,256]{2,1,0:T(8,128)S(1)}, f32[32,512]{1,0:T(8,128)S(1)}, f32[8,4,256]{2,1,0:T(4,128)S(1)}, f32[8,4,256]{2,1,0:T(4,128)S(1)}, f32[8,4,...) custom-call(f32[8,56,128]{2,1,0:T(8,128)S(1)} %bitcast.28, bf16[8,8,16,256]{3,2,1,0:T(8,128)(2,1)S(1)} %copy-done.1, ...), custom_call_target="tpu_custom_call" | custom-call | tf_op jit(solution)/shard_map/first_model/pallas_call | solution.py:513
  47.2 1.1 %other_targets.1 = f32[2,96,128]{2,1,0:T(8,128)S(1)} custom-call(s32[32]{0:T(128)S(1)} %copy-done.6, f32[8,16,256]{2,1,0:T(8,128)S(1)} %get-tuple-element.25.part_ref, bf16[3,8,16,256]{3,2,1,0:T(8,128)(2,1)S(1)} %add.25.solved_ref.refs_1_, f32[32,512]{1,0:T(8,128)S(1)} %get-tuple-element.27.begin_ref), custom_call_target="tpu_custom_call" | custom-call | tf_op jit(solution)/shard_map/other_targets/pallas_call | solution.py:513
  48.4 2.2 %collective-permute-start.6 = (f32[2,96,128]{2,1,0:T(8,128)S(1)}, f32[2,96,128]{2,1,0:T(8,128)S(1)}, u32[]{:S(2)}, u32[]{:S(2)}) collective-permute-start(f32[2,96,128]{2,1,0:T(8,128)S(1)} %other_targets.1), channel_id=1, source_target_pairs={{0,1},{1,0},{2,3},{3,2},{4,5},{5,4},{6,7},{7,6},{8,9},{9,8},{10,11... | collective-permute-start | bytes 294920 | tf_op jit(solution)/shard_map/ppermute | solution.py:480
  50.6 3.1 %collective-permute-done.6 = f32[2,96,128]{2,1,0:T(8,128)S(1)} collective-permute-done((f32[2,96,128]{2,1,0:T(8,128)S(1)}, f32[2,96,128]{2,1,0:T(8,128)S(1)}, u32[]{:S(2)}, u32[]{:S(2)}) %collective-permute-start.6) | collective-permute-done | bytes 98336 | tf_op jit(solution)/shard_map/ppermute | solution.py:480
  53.7 3.4 %collective-permute-start.7 = (f32[2,96,128]{2,1,0:T(8,128)S(1)}, f32[2,96,128]{2,1,0:T(8,128)S(1)}, u32[]{:S(2)}, u32[]{:S(2)}) collective-permute-start(f32[2,96,128]{2,1,0:T(8,128)S(1)} %add.26), channel_id=1, source_target_pairs={{0,2},{1,3},{2,0},{3,1},{4,6},{5,7},{6,4},{7,5},{8,10},{9,11},{10,... | collective-permute-start | bytes 294920 | tf_op jit(solution)/shard_map/ppermute | solution.py:480
  57.9 1.8 %collective-permute-start.18 = (f32[2,32,128]{2,1,0:T(8,128)S(1)}, f32[2,32,128]{2,1,0:T(8,128)S(1)}, u32[]{:S(2)}, u32[]{:S(2)}) collective-permute-start(f32[2,32,128]{2,1,0:T(8,128)S(1)} %first_target.1), channel_id=1, source_target_pairs={{0,1},{1,0},{2,3},{3,2},{4,5},{5,4},{6,7},{7,6},{8,9},{9,8},{10,11... | collective-permute-start | bytes 98312 | tf_op jit(solution)/shard_map/ppermute | solution.py:480
  59.7 2.5 %collective-permute-done.18 = f32[2,32,128]{2,1,0:T(8,128)S(1)} collective-permute-done((f32[2,32,128]{2,1,0:T(8,128)S(1)}, f32[2,32,128]{2,1,0:T(8,128)S(1)}, u32[]{:S(2)}, u32[]{:S(2)}) %collective-permute-start.18) | collective-permute-done | bytes 32800 | tf_op jit(solution)/shard_map/ppermute | solution.py:480
  62.3 4.7 %collective-permute-done.19 = f32[2,32,128]{2,1,0:T(8,128)S(1)} collective-permute-done((f32[2,32,128]{2,1,0:T(8,128)S(1)}, f32[2,32,128]{2,1,0:T(8,128)S(1)}, u32[]{:S(2)}, u32[]{:S(2)}) %collective-permute-start.19) | collective-permute-done | bytes 32800 | tf_op jit(solution)/shard_map/ppermute | solution.py:480
  67.1 2.5 %collective-permute-start.10 = (f32[2,96,128]{2,1,0:T(8,128)S(1)}, f32[2,96,128]{2,1,0:T(8,128)S(1)}, u32[]{:S(2)}, u32[]{:S(2)}) collective-permute-start(f32[2,96,128]{2,1,0:T(8,128)S(1)} %add.27), channel_id=1, source_target_pairs={{0,24},{4,28},{8,16},{12,20},{16,8},{20,12},{24,0},{28,4},{1,25},{... | collective-permute-start | bytes 294920 | tf_op jit(solution)/shard_map/ppermute | solution.py:480
  70.6 1.5 %collective-permute-start.20 = (f32[2,48,128]{2,1,0:T(8,128)S(1)}, f32[2,48,128]{2,1,0:T(8,128)S(1)}, u32[]{:S(2)}, u32[]{:S(2)}) collective-permute-start(f32[2,48,128]{2,1,0:T(8,128)S(1)} %get-tuple-element.43), channel_id=1, source_target_pairs={{0,8},{4,12},{8,0},{12,4},{16,24},{20,28},{24,16},{28,20},{1,9},{5... | collective-permute-start | bytes 147464 | tf_op jit(solution)/shard_map/ppermute | solution.py:480
  72.8 1.8 %collective-permute-start.21 = (f32[2,48,128]{2,1,0:T(8,128)S(1)}, f32[2,48,128]{2,1,0:T(8,128)S(1)}, u32[]{:S(2)}, u32[]{:S(2)}) collective-permute-start(f32[2,48,128]{2,1,0:T(8,128)S(1)} %get-tuple-element.43), channel_id=1, source_target_pairs={{0,16},{4,20},{8,24},{12,28},{16,0},{20,4},{24,8},{28,12},{1,17},{... | collective-permute-start | bytes 147464 | tf_op jit(solution)/shard_map/ppermute | solution.py:480
  74.6 1.1 %collective-permute-start.22 = (f32[2,48,128]{2,1,0:T(8,128)S(1)}, f32[2,48,128]{2,1,0:T(8,128)S(1)}, u32[]{:S(2)}, u32[]{:S(2)}) collective-permute-start(f32[2,48,128]{2,1,0:T(8,128)S(1)} %get-tuple-element.43), channel_id=1, source_target_pairs={{0,24},{4,28},{8,16},{12,20},{16,8},{20,12},{24,0},{28,4},{1,25},{... | collective-permute-start | bytes 147464 | tf_op jit(solution)/shard_map/ppermute | solution.py:480
  76.8 2.7 %collective-permute-done.22 = f32[2,48,128]{2,1,0:T(8,128)S(1)} collective-permute-done((f32[2,48,128]{2,1,0:T(8,128)S(1)}, f32[2,48,128]{2,1,0:T(8,128)S(1)}, u32[]{:S(2)}, u32[]{:S(2)}) %collective-permute-start.22) | collective-permute-done | bytes 49184 | tf_op jit(solution)/shard_map/ppermute | solution.py:480
  79.7 1.9 %collective-permute-start.24 = (f32[8,4,256]{2,1,0:T(4,128)S(1)}, f32[8,4,256]{2,1,0:T(4,128)S(1)}, u32[]{:S(2)}, u32[]{:S(2)}) collective-permute-start(f32[8,4,256]{2,1,0:T(4,128)S(1)} %get-tuple-element.37), channel_id=1, source_target_pairs={{0,1},{1,0},{2,3},{3,2},{4,5},{5,4},{6,7},{7,6},{8,9},{9,8},{10,11... | collective-permute-start | bytes 98312 | tf_op jit(solution)/shard_map/ppermute | solution.py:480
  81.6 2.5 %collective-permute-start.26 = (f32[8,4,256]{2,1,0:T(4,128)S(1)}, f32[8,4,256]{2,1,0:T(4,128)S(1)}, u32[]{:S(2)}, u32[]{:S(2)}) collective-permute-start(f32[8,4,256]{2,1,0:T(4,128)S(1)} %get-tuple-element.39), channel_id=1, source_target_pairs={{0,3},{1,2},{2,1},{3,0},{4,7},{5,6},{6,5},{7,4},{8,11},{9,10},{10,... | collective-permute-start | bytes 98312 | tf_op jit(solution)/shard_map/ppermute | solution.py:480
  84.1 1.2 %lookup.1 = (bf16[8,512,512]{2,1,0:T(8,128)(2,1)S(1)}, f32[4,2,128,128]{3,2,1,0:T(8,128)S(1)}, f32[32,512]{1,0:T(8,128)S(1)}) custom-call(f32[8,56,128]{2,1,0:T(8,128)S(1)} %bitcast.29), custom_call_target="tpu_custom_call" | custom-call | tf_op jit(solution)/shard_map/lookup/pallas_call | solution.py:513
  85.4 2.8 %first_sweep.1 = (f32[1,8,512]{2,1,0:T(8,128)S(1)}, f32[1,32,16,128]{3,2,1,0:T(8,128)S(1)}, f32[1,2,16,128]{3,2,1,0:T(8,128)S(1)}) custom-call(s32[32]{0:T(128)S(1)} %copy-done.6, s32[32]{0:T(128)S(1)} %copy-done.7, s32[32]{0:T(128)S(1)} %copy-done.8, bf16[8,512,512]{2,1,0:T(8,128)(2,1)S(1)} %get-tuple-element.22.refs_0_, ...), custom_call_target="tpu_custom_call" | custom-call | tf_op jit(solution)/shard_map/first_sweep/pallas_call | solution.py:513
  88.2 11.4 %other_sweeps.1 = (f32[32,8,64]{2,1,0:T(8,128)}, f32[8,4,256]{2,1,0:T(4,128)}) custom-call(s32[32]{0:T(128)S(1)} %copy-done.6, s32[32]{0:T(128)S(1)} %copy-done.7, s32[32]{0:T(128)S(1)} %copy-done.8, bf16[8,512,512]{2,1,0:T(8,128)(2,1)S(1)} %get-tuple-element.22.refs_0_, f32[4,2,128,128]{3,2,1,0:T(8,128)S(1)} %get-tuple-element.23.refs_1_, ...), custom_call_target="tpu_custom_call" | custom-call | tf_op jit(solution)/shard_map/other_sweeps/pallas_call | solution.py:513
  (66 shorter events, 11.0 us)
Async XLA Ops:
  3.9 42.2 %copy-start.1 = (bf16[8,8,16,256]{3,2,1,0:T(8,128)(2,1)S(1)}, bf16[8,8,16,256]{3,2,1,0:T(8,128)(2,1)}, u32[]{:S(2)}) copy-start(bf16[8,8,16,256]{3,2,1,0:T(8,128)(2,1)} %coher_ref.1) | copy-start | bytes 1572868
  3.9 42.3 %copy-start.4 = (f32[8,4,256]{2,1,0:T(4,128)S(1)}, f32[8,4,256]{2,1,0:T(4,128)}, u32[]{:S(2)}) copy-start(f32[8,4,256]{2,1,0:T(4,128)} %vis_ref.1) | copy-start | bytes 98308
  3.9 43.3 %copy-start.6 = (s32[32]{0:T(128)S(1)}, s32[32]{0:T(128)}, u32[]{:S(2)}) copy-start(s32[32]{0:T(128)} %order_ref.9) | copy-start | bytes 388
  4.6 8.0 %collective-permute-start.4 = (bf16[3,8,16,256]{3,2,1,0:T(8,128)(2,1)S(1)}, bf16[3,8,16,256]{3,2,1,0:T(8,128)(2,1)S(1)}, u32[]{:S(2)}, u32[]{:S(2)}) collective-permute-start(bf16[3,8,16,256]{3,2,1,0:T(8,128)(2,1)S(1)} %get-tuple-element.26), channel_id=1, source_target_pairs={{0,1},{1,0},{2,3},{3,2},{4,5},{5,4},{6,7},{7,6},{8,9},{9,8},{10,11... | collective-permute-start | bytes 589832 | tf_op jit(solution)/shard_map/ppermute | solution.py:480
  12.6 13.4 %collective-permute-start.5 = (bf16[3,8,16,256]{3,2,1,0:T(8,128)(2,1)S(1)}, bf16[3,8,16,256]{3,2,1,0:T(8,128)(2,1)S(1)}, u32[]{:S(2)}, u32[]{:S(2)}) collective-permute-start(bf16[3,8,16,256]{3,2,1,0:T(8,128)(2,1)S(1)} %add.24), channel_id=1, source_target_pairs={{0,2},{1,3},{2,0},{3,1},{4,6},{5,7},{6,4},{7,5},{8,10},{9,11},{10,... | collective-permute-start | bytes 589832 | tf_op jit(solution)/shard_map/ppermute | solution.py:480
  15.4 4.7 %collective-permute-start.12 = (bf16[1,8,16,256]{3,2,1,0:T(8,128)(2,1)S(1)}, bf16[1,8,16,256]{3,2,1,0:T(8,128)(2,1)S(1)}, u32[]{:S(2)}, u32[]{:S(2)}) collective-permute-start(bf16[1,8,16,256]{3,2,1,0:T(8,128)(2,1)S(1)} %get-tuple-element.28), channel_id=1, source_target_pairs={{0,1},{1,0},{2,3},{3,2},{4,5},{5,4},{6,7},{7,6},{8,9},{9,8},{10,11... | collective-permute-start | bytes 196616 | tf_op jit(solution)/shard_map/ppermute | solution.py:480
  20.2 65.2 %copy-start.7 = (s32[32]{0:T(128)S(1)}, s32[32]{0:T(128)}, u32[]{:S(2)}) copy-start(s32[32]{0:T(128)} %counts_ref.3) | copy-start | bytes 388
  20.2 65.2 %copy-start.8 = (s32[32]{0:T(128)S(1)}, s32[32]{0:T(128)}, u32[]{:S(2)}) copy-start(s32[32]{0:T(128)} %damping_ref.3) | copy-start | bytes 388
  20.2 5.8 %collective-permute-start.13 = (bf16[1,8,16,256]{3,2,1,0:T(8,128)(2,1)S(1)}, bf16[1,8,16,256]{3,2,1,0:T(8,128)(2,1)S(1)}, u32[]{:S(2)}, u32[]{:S(2)}) collective-permute-start(bf16[1,8,16,256]{3,2,1,0:T(8,128)(2,1)S(1)} %add.28), channel_id=1, source_target_pairs={{0,2},{1,3},{2,0},{3,1},{4,6},{5,7},{6,4},{7,5},{8,10},{9,11},{10,... | collective-permute-start | bytes 196616 | tf_op jit(solution)/shard_map/ppermute | solution.py:480
  27.0 17.8 %collective-permute-start.14 = (f32[2,240,128]{2,1,0:T(8,128)S(1)}, f32[2,240,128]{2,1,0:T(8,128)S(1)}, u32[]{:S(2)}, u32[]{:S(2)}) collective-permute-start(f32[2,240,128]{2,1,0:T(8,128)S(1)} %get-tuple-element.29), channel_id=1, source_target_pairs={{0,8},{4,12},{8,0},{12,4},{16,24},{20,28},{24,16},{28,20},{1,9},{5... | collective-permute-start | bytes 737288 | tf_op jit(solution)/shard_map/ppermute | solution.py:480
  28.4 16.4 %collective-permute-start.15 = (f32[2,240,128]{2,1,0:T(8,128)S(1)}, f32[2,240,128]{2,1,0:T(8,128)S(1)}, u32[]{:S(2)}, u32[]{:S(2)}) collective-permute-start(f32[2,240,128]{2,1,0:T(8,128)S(1)} %get-tuple-element.29), channel_id=1, source_target_pairs={{0,16},{4,20},{8,24},{12,28},{16,0},{20,4},{24,8},{28,12},{1,17},{... | collective-permute-start | bytes 737288 | tf_op jit(solution)/shard_map/ppermute | solution.py:480
  29.9 14.9 %collective-permute-start.16 = (f32[2,240,128]{2,1,0:T(8,128)S(1)}, f32[2,240,128]{2,1,0:T(8,128)S(1)}, u32[]{:S(2)}, u32[]{:S(2)}) collective-permute-start(f32[2,240,128]{2,1,0:T(8,128)S(1)} %get-tuple-element.29), channel_id=1, source_target_pairs={{0,24},{4,28},{8,16},{12,20},{16,8},{20,12},{24,0},{28,4},{1,25},{... | collective-permute-start | bytes 737288 | tf_op jit(solution)/shard_map/ppermute | solution.py:480
  30.6 9.4 %collective-permute-start = (f32[56,128]{1,0:T(8,128)S(1)}, f32[56,128]{1,0:T(8,128)S(1)}, u32[]{:S(2)}, u32[]{:S(2)}) collective-permute-start(f32[56,128]{1,0:T(8,128)S(1)} %get-tuple-element.21), channel_id=1, source_target_pairs={{0,8},{4,12},{8,0},{12,4},{16,24},{20,28},{24,16},{28,20},{1,9},{5... | collective-permute-start | bytes 86024 | tf_op jit(solution)/shard_map/ppermute | solution.py:480
  31.9 10.2 %collective-permute-start.1 = (f32[56,128]{1,0:T(8,128)S(1)}, f32[56,128]{1,0:T(8,128)S(1)}, u32[]{:S(2)}, u32[]{:S(2)}) collective-permute-start(f32[56,128]{1,0:T(8,128)S(1)} %get-tuple-element.21), channel_id=1, source_target_pairs={{0,16},{4,20},{8,24},{12,28},{16,0},{20,4},{24,8},{28,12},{1,17},{... | collective-permute-start | bytes 86024 | tf_op jit(solution)/shard_map/ppermute | solution.py:480
  39.9 4.8 %collective-permute-start.2 = (f32[56,128]{1,0:T(8,128)S(1)}, f32[56,128]{1,0:T(8,128)S(1)}, u32[]{:S(2)}, u32[]{:S(2)}) collective-permute-start(f32[56,128]{1,0:T(8,128)S(1)} %get-tuple-element.21), channel_id=1, source_target_pairs={{0,24},{4,28},{8,16},{12,20},{16,8},{20,12},{24,0},{28,4},{1,25},{... | collective-permute-start | bytes 86024 | tf_op jit(solution)/shard_map/ppermute | solution.py:480
  44.7 1.4 %collective-permute-start.3 = (f32[4,56,128]{2,1,0:T(8,128)S(1)}, f32[4,56,128]{2,1,0:T(8,128)S(1)}, u32[]{:S(2)}, u32[]{:S(2)}) collective-permute-start(f32[4,56,128]{2,1,0:T(8,128)S(1)} %get-tuple-element.41), channel_id=1, source_target_pairs={{0,4},{4,0},{8,12},{12,8},{16,20},{20,16},{24,28},{28,24},{1,5},{5... | collective-permute-start | bytes 344072 | tf_op jit(solution)/shard_map/ppermute | solution.py:480
  44.9 43.3 %collective-permute-start.17 = (f32[4,2,240,128]{3,2,1,0:T(8,128)S(1)}, f32[4,2,240,128]{3,2,1,0:T(8,128)S(1)}, u32[]{:S(2)}, u32[]{:S(2)}) collective-permute-start(f32[4,2,240,128]{3,2,1,0:T(8,128)S(1)} %pad_maximum_fusion), channel_id=1, source_target_pairs={{0,4},{4,0},{8,12},{12,8},{16,20},{20,16},{24,28},{28,24},{1,5},{5... | collective-permute-start | bytes 2949128 | tf_op jit(solution)/shard_map/ppermute | solution.py:480
  48.4 5.3 %collective-permute-start.6 = (f32[2,96,128]{2,1,0:T(8,128)S(1)}, f32[2,96,128]{2,1,0:T(8,128)S(1)}, u32[]{:S(2)}, u32[]{:S(2)}) collective-permute-start(f32[2,96,128]{2,1,0:T(8,128)S(1)} %other_targets.1), channel_id=1, source_target_pairs={{0,1},{1,0},{2,3},{3,2},{4,5},{5,4},{6,7},{7,6},{8,9},{9,8},{10,11... | collective-permute-start | bytes 294920 | tf_op jit(solution)/shard_map/ppermute | solution.py:480
  53.7 13.3 %collective-permute-start.7 = (f32[2,96,128]{2,1,0:T(8,128)S(1)}, f32[2,96,128]{2,1,0:T(8,128)S(1)}, u32[]{:S(2)}, u32[]{:S(2)}) collective-permute-start(f32[2,96,128]{2,1,0:T(8,128)S(1)} %add.26), channel_id=1, source_target_pairs={{0,2},{1,3},{2,0},{3,1},{4,6},{5,7},{6,4},{7,5},{8,10},{9,11},{10,... | collective-permute-start | bytes 294920 | tf_op jit(solution)/shard_map/ppermute | solution.py:480
  57.9 4.3 %collective-permute-start.18 = (f32[2,32,128]{2,1,0:T(8,128)S(1)}, f32[2,32,128]{2,1,0:T(8,128)S(1)}, u32[]{:S(2)}, u32[]{:S(2)}) collective-permute-start(f32[2,32,128]{2,1,0:T(8,128)S(1)} %first_target.1), channel_id=1, source_target_pairs={{0,1},{1,0},{2,3},{3,2},{4,5},{5,4},{6,7},{7,6},{8,9},{9,8},{10,11... | collective-permute-start | bytes 98312 | tf_op jit(solution)/shard_map/ppermute | solution.py:480
  62.2 4.8 %collective-permute-start.19 = (f32[2,32,128]{2,1,0:T(8,128)S(1)}, f32[2,32,128]{2,1,0:T(8,128)S(1)}, u32[]{:S(2)}, u32[]{:S(2)}) collective-permute-start(f32[2,32,128]{2,1,0:T(8,128)S(1)} %add.30), channel_id=1, source_target_pairs={{0,2},{1,3},{2,0},{3,1},{4,6},{5,7},{6,4},{7,5},{8,10},{9,11},{10,... | collective-permute-start | bytes 98312 | tf_op jit(solution)/shard_map/ppermute | solution.py:480
  67.1 5.7 %collective-permute-start.10 = (f32[2,96,128]{2,1,0:T(8,128)S(1)}, f32[2,96,128]{2,1,0:T(8,128)S(1)}, u32[]{:S(2)}, u32[]{:S(2)}) collective-permute-start(f32[2,96,128]{2,1,0:T(8,128)S(1)} %add.27), channel_id=1, source_target_pairs={{0,24},{4,28},{8,16},{12,20},{16,8},{20,12},{24,0},{28,4},{1,25},{... | collective-permute-start | bytes 294920 | tf_op jit(solution)/shard_map/ppermute | solution.py:480
  69.5 5.1 %collective-permute-start.8 = (f32[2,96,128]{2,1,0:T(8,128)S(1)}, f32[2,96,128]{2,1,0:T(8,128)S(1)}, u32[]{:S(2)}, u32[]{:S(2)}) collective-permute-start(f32[2,96,128]{2,1,0:T(8,128)S(1)} %add.27), channel_id=1, source_target_pairs={{0,8},{4,12},{8,0},{12,4},{16,24},{20,28},{24,16},{28,20},{1,9},{5... | collective-permute-start | bytes 294920 | tf_op jit(solution)/shard_map/ppermute | solution.py:480
  70.1 5.6 %collective-permute-start.9 = (f32[2,96,128]{2,1,0:T(8,128)S(1)}, f32[2,96,128]{2,1,0:T(8,128)S(1)}, u32[]{:S(2)}, u32[]{:S(2)}) collective-permute-start(f32[2,96,128]{2,1,0:T(8,128)S(1)} %add.27), channel_id=1, source_target_pairs={{0,16},{4,20},{8,24},{12,28},{16,0},{20,4},{24,8},{28,12},{1,17},{... | collective-permute-start | bytes 294920 | tf_op jit(solution)/shard_map/ppermute | solution.py:480
  70.6 5.2 %collective-permute-start.20 = (f32[2,48,128]{2,1,0:T(8,128)S(1)}, f32[2,48,128]{2,1,0:T(8,128)S(1)}, u32[]{:S(2)}, u32[]{:S(2)}) collective-permute-start(f32[2,48,128]{2,1,0:T(8,128)S(1)} %get-tuple-element.43), channel_id=1, source_target_pairs={{0,8},{4,12},{8,0},{12,4},{16,24},{20,28},{24,16},{28,20},{1,9},{5... | collective-permute-start | bytes 147464 | tf_op jit(solution)/shard_map/ppermute | solution.py:480
  72.8 4.1 %collective-permute-start.21 = (f32[2,48,128]{2,1,0:T(8,128)S(1)}, f32[2,48,128]{2,1,0:T(8,128)S(1)}, u32[]{:S(2)}, u32[]{:S(2)}) collective-permute-start(f32[2,48,128]{2,1,0:T(8,128)S(1)} %get-tuple-element.43), channel_id=1, source_target_pairs={{0,16},{4,20},{8,24},{12,28},{16,0},{20,4},{24,8},{28,12},{1,17},{... | collective-permute-start | bytes 147464 | tf_op jit(solution)/shard_map/ppermute | solution.py:480
  74.6 5.0 %collective-permute-start.22 = (f32[2,48,128]{2,1,0:T(8,128)S(1)}, f32[2,48,128]{2,1,0:T(8,128)S(1)}, u32[]{:S(2)}, u32[]{:S(2)}) collective-permute-start(f32[2,48,128]{2,1,0:T(8,128)S(1)} %get-tuple-element.43), channel_id=1, source_target_pairs={{0,24},{4,28},{8,16},{12,20},{16,8},{20,12},{24,0},{28,4},{1,25},{... | collective-permute-start | bytes 147464 | tf_op jit(solution)/shard_map/ppermute | solution.py:480
  75.7 12.5 %collective-permute-start.11 = (f32[4,2,96,128]{3,2,1,0:T(8,128)S(1)}, f32[4,2,96,128]{3,2,1,0:T(8,128)S(1)}, u32[]{:S(2)}, u32[]{:S(2)}) collective-permute-start(f32[4,2,96,128]{3,2,1,0:T(8,128)S(1)} %pad_maximum_fusion.1), channel_id=1, source_target_pairs={{0,4},{4,0},{8,12},{12,8},{16,20},{20,16},{24,28},{28,24},{1,5},{5... | collective-permute-start | bytes 1179656 | tf_op jit(solution)/shard_map/ppermute | solution.py:480
  79.6 2.0 %collective-permute-start.23 = (f32[4,2,48,128]{3,2,1,0:T(8,128)S(1)}, f32[4,2,48,128]{3,2,1,0:T(8,128)S(1)}, u32[]{:S(2)}, u32[]{:S(2)}) collective-permute-start(f32[4,2,48,128]{3,2,1,0:T(8,128)S(1)} %pad_maximum_fusion.3), channel_id=1, source_target_pairs={{0,4},{4,0},{8,12},{12,8},{16,20},{20,16},{24,28},{28,24},{1,5},{5... | collective-permute-start | bytes 589832 | tf_op jit(solution)/shard_map/ppermute | solution.py:480
  79.7 8.5 %collective-permute-start.24 = (f32[8,4,256]{2,1,0:T(4,128)S(1)}, f32[8,4,256]{2,1,0:T(4,128)S(1)}, u32[]{:S(2)}, u32[]{:S(2)}) collective-permute-start(f32[8,4,256]{2,1,0:T(4,128)S(1)} %get-tuple-element.37), channel_id=1, source_target_pairs={{0,1},{1,0},{2,3},{3,2},{4,5},{5,4},{6,7},{7,6},{8,9},{9,8},{10,11... | collective-permute-start | bytes 98312 | tf_op jit(solution)/shard_map/ppermute | solution.py:480
  81.5 6.6 %collective-permute-start.25 = (f32[8,4,256]{2,1,0:T(4,128)S(1)}, f32[8,4,256]{2,1,0:T(4,128)S(1)}, u32[]{:S(2)}, u32[]{:S(2)}) collective-permute-start(f32[8,4,256]{2,1,0:T(4,128)S(1)} %get-tuple-element.38), channel_id=1, source_target_pairs={{0,2},{1,3},{2,0},{3,1},{4,6},{5,7},{6,4},{7,5},{8,10},{9,11},{10,... | collective-permute-start | bytes 98312 | tf_op jit(solution)/shard_map/ppermute | solution.py:480
  81.6 6.5 %collective-permute-start.26 = (f32[8,4,256]{2,1,0:T(4,128)S(1)}, f32[8,4,256]{2,1,0:T(4,128)S(1)}, u32[]{:S(2)}, u32[]{:S(2)}) collective-permute-start(f32[8,4,256]{2,1,0:T(4,128)S(1)} %get-tuple-element.39), channel_id=1, source_target_pairs={{0,3},{1,2},{2,1},{3,0},{4,7},{5,6},{6,5},{7,4},{8,11},{9,10},{10,... | collective-permute-start | bytes 98312 | tf_op jit(solution)/shard_map/ppermute | solution.py:480
  (5 other events, 43.2 us)
where the time goes:
time: 101 us; the launch traced here: 99.7 us
  starting transfers between devices  39.1 us (39%)
  waiting for transfers between devices  36 us (36%)
  Pallas kernels  20 us (20%)
  local copies, waits for them, and re-layouts  3.32 us (3%)
    ppermute x27, starting transfers between devices, exchange(): lax.ppermute(block, axis, [(i, i ^ mask) for i in range(lax.axis_size(axi...  39.1 us
    ppermute x27, waiting for transfers between devices, exchange(): lax.ppermute(block, axis, [(i, i ^ mask) for i in range(lax.axis_size(axi...  36 us
    pallas_call x8, Pallas kernels, call(): pl.pallas_call(functools.partial(kernel, **static), out_shape=[jax.ShapeD...  19.3 us
    unnamed x20, local copies, waits for them, and re-layouts  3.31 us
  transfers between devices with their start and end apart: 27, of which 12 were waited for; matrix products, arithmetic and copies ran while one was open for 0% of the time, Pallas kernels for 7%

commit v1 on v0

--- a/solution.py
+++ b/solution.py
@@ -12,10 +12,12 @@
 F32 = jnp.float32
 BF16 = jnp.bfloat16
 VMEM_BYTES = 24 * 1024 * 1024
+MOST_VMEM_BYTES = 60 * 1024 * 1024
 GRAM = [(u, v) for u in range(4) for v in range(u, 4)]
 M_ROWS = 32
 K_ROWS = 16
-FIRST = 1
+GROUPS = [(0, 2), (2, 4)]
+TARGETS = [(0, 4)]
 
 
 def mul(x, y):
@@ -81,7 +83,7 @@
 
 
 def prep_kernel(order_ref, stations_ref, offs_ref, *refs, owned, per):
-    *coher_refs, out_ref, first_ref, rest_ref = refs
+    coher_refs, out_ref, chosen_refs = refs[:SOLVED], refs[SOLVED], refs[SOLVED + 1 :]
     lane = lax.axis_index("dir")
     width = offs_ref.shape[2]
     station_rows = 2 * stations_ref.shape[1] // 128
@@ -101,11 +103,8 @@
         out_ref[part_rows + row : part_rows + row + 1] = stations_ref[end : end + 1, tile * 128 : tile * 128 + 128].astype(F32)
     for i in range(SOLVED):
         mine = order_ref[i] // owned == lane
-        value = jnp.where(mine, coher_refs[i][0], jnp.zeros_like(coher_refs[i][0]))
-        if i < FIRST:
-            first_ref[i] = value
-        else:
-            rest_ref[i - FIRST] = value
+        [(low, ref)] = [(low, ref) for (low, high), ref in zip(GROUPS, chosen_refs) if low <= i < high]
+        ref[i - low] = jnp.where(mine, coher_refs[i][0], jnp.zeros_like(coher_refs[i][0]))
 
 
 def fill_table(blocks_ref, table, width):
@@ -153,8 +152,7 @@
                     ends_ref[i, end, chunk : chunk + 8, :] = out[i * 8 : i * 8 + 8, column : column + 128]
 
 
-def model_kernel(blocks_ref, coher_ref, vis_ref, part_ref, begin_ref, *refs, width):
-    *piece_refs, table, ends = refs
+def model_kernel(blocks_ref, coher_ref, vis_ref, part_ref, begin_ref, table, ends, *, width):
     owned = coher_ref.shape[0]
     baselines = coher_ref.shape[3]
     channels = vis_ref.shape[1]
@@ -182,13 +180,8 @@
         acc = lax.fori_loop(0, owned, add_model, [(zeros, zeros)] * 4)
         for c in range(8):
             total_part = acc[c // 2][c % 2]
-            lanes = [total_part[x * channels : (x + 1) * channels] for x in range(len(piece_refs))]
+            lanes = [total_part[x : x + channels] for x in range(0, total_part.shape[0], channels)]
             vis = vis_ref[c, :, at]
-            for k, piece_ref in enumerate(piece_refs):
-                value = lanes[0]
-                for x in range(1, len(lanes)):
-                    value = jnp.where(lane ^ k == x, lanes[x], value)
-                piece_ref[c, :, at] = value + vis if k == 0 else value
             part_ref[c, :, at] = jnp.concatenate([jnp.where(lane == x, y + vis, y) for x, y in enumerate(lanes)], axis=0)
 
 
@@ -196,101 +189,100 @@
     return jnp.sum(values, axis=0, keepdims=True)
 
 
-def target_kernel(order_ref, part_ref, solved_ref, begin_ref, m_ref, *, owned, low):
-    baselines = part_ref.shape[2]
-    lane = lax.axis_index("dir")
+def pair_list(low, high):
+    return [(m, i) for i in range(low, high) for m in range(i)]
+
+
+def load_coher(refs, i, at):
+    [(low, ref)] = [(low, ref) for (low, high), ref in zip(GROUPS, refs) if low <= i < high]
+    return as_matrix([ref[i - low, c, :, at].astype(F32) for c in range(8)])
+
+
+def target_kernel(first_ref, begin_ref, *refs, low, high):
+    *solved_refs, out_ref = refs
+    baselines = first_ref.shape[2]
     for half in range(baselines // 128):
         at = pl.ds(half * 128, 128)
-        for i in range(solved_ref.shape[0]):
-            coher = as_matrix([solved_ref[i, c, :, at].astype(F32) for c in range(8)])
-            row = (low + i) * 8
+        out = 0
+        for i in range(low, high):
+            coher = load_coher(solved_refs, i, at)
             gain_p, gain_q = [
-                as_matrix([begin_ref[row + c : row + c + 1, pl.ds(end * baselines + half * 128, 128)] for c in range(8)])
+                as_matrix([begin_ref[i * 8 + c : i * 8 + c + 1, pl.ds(end * baselines + half * 128, 128)] for c in range(8)])
                 for end in (0, 1)
             ]
             model = apply_gains(gain_p, coher, gain_q)
-            flag = (order_ref[low + i] // owned == lane).astype(F32)
-            target = [
-                (part_ref[2 * e, :, at] + flag * model[e][0], part_ref[2 * e + 1, :, at] + flag * model[e][1])
-                for e in range(4)
-            ]
-            out = i * M_ROWS
+            target = [(first_ref[2 * e, :, at] + model[e][0], first_ref[2 * e + 1, :, at] + model[e][1]) for e in range(4)]
             for u in range(4):
                 for v in range(4):
                     value = mul_conj(target[u], coher[v])
-                    m_ref[half, out : out + 1, :] = summed(value[0])
-                    m_ref[half, out + 1 : out + 2, :] = summed(value[1])
+                    out_ref[half, out : out + 1, :] = summed(value[0])
+                    out_ref[half, out + 1 : out + 2, :] = summed(value[1])
                     out += 2
 
 
-def pair_list(low):
-    return [(m, i) for i in range(low, SOLVED) for m in range(i)]
-
-
-def product_kernel(*refs, low):
-    *solved_refs, kx_ref, own_ref = refs
-    where = [(ref, i) for ref in solved_refs for i in range(ref.shape[0])]
-    baselines = solved_refs[0].shape[3]
-    channels = own_ref.shape[2]
-    lane = lax.axis_index("dir")
-    for half in range(baselines // 128):
+def product_kernel(*refs, low, high):
+    *solved_refs, out_ref = refs
+    for half in range(out_ref.shape[0]):
         at = pl.ds(half * 128, 128)
-
-        def load(i):
-            ref, place = where[i]
-            return [ref[place, c, :, at].astype(F32) for c in range(8)]
-
         out = 0
-        for i in range(low, len(where)):
-            parts = load(i)
-            for c in range(8):
-                mine = parts[c][:channels]
-                for x in range(1, parts[c].shape[0] // channels):
-                    mine = jnp.where(lane == x, parts[c][x * channels : (x + 1) * channels], mine)
-                own_ref[i - low, c, :, at] = mine
-            coher = as_matrix(parts)
+        for i in range(low, high):
+            coher = load_coher(solved_refs, i, at)
             for u, v in GRAM:
                 value = mul_conj(coher[u], coher[v])
-                kx_ref[half, out : out + 1, :] = summed(value[0])
+                out_ref[half, out : out + 1, :] = summed(value[0])
                 out += 1
                 if u != v:
-                    kx_ref[half, out : out + 1, :] = summed(value[1])
+                    out_ref[half, out : out + 1, :] = summed(value[1])
                     out += 1
-        if low == 0:
-            continue
-        for m, i in pair_list(low):
-            coher, other = as_matrix(load(i)), as_matrix(load(m))
+        for m, i in pair_list(low, high):
+            coher, other = load_coher(solved_refs, i, at), load_coher(solved_refs, m, at)
             for u in range(4):
                 for v in range(4):
                     value = mul_conj(other[u], coher[v])
-                    kx_ref[half, out : out + 1, :] = summed(value[0])
-                    kx_ref[half, out + 1 : out + 2, :] = summed(value[1])
+                    out_ref[half, out : out + 1, :] = summed(value[0])
+                    out_ref[half, out + 1 : out + 2, :] = summed(value[1])
                     out += 2
 
 
-def sweep_kernel(order_ref, counts_ref, damping_ref, *refs, low, high, tiles, factor, last):
-    hots, begin, start_ref = refs[:3]
-    near_m, far_m, near_kx, far_kx = refs[3:7]
-    refs = refs[7:]
+def own_kernel(first_ref, *refs):
+    *solved_refs, res_ref, own_ref = refs
+    channels = res_ref.shape[1]
+    lane = lax.axis_index("dir")
+
+    def select(value):
+        mine = value[:channels]
+        for x in range(1, value.shape[0] // channels):
+            mine = jnp.where(lane == x, value[x * channels : (x + 1) * channels], mine)
+        return mine
+
+    for c in range(8):
+        res_ref[c] = select(first_ref[c])
+        for (low, high), solved_ref in zip(GROUPS, solved_refs):
+            for i in range(low, high):
+                own_ref[i, c] = select(solved_ref[i - low, c].astype(F32))
+
+
+def sweep_kernel(order_ref, counts_ref, damping_ref, *refs, low, high, tiles, factor):
+    last = high == SOLVED
+    hots, begin, start_ref, res_ref, own_ref = refs[:5]
+    targets, refs = refs[5:7], refs[7:]
+    products = [refs[2 * g : 2 * g + 2] for g in range(len(GROUPS))]
+    ends, values, state, m_now, k_now = refs[-5:]
+    refs = refs[2 * len(GROUPS) : -5]
+    stages = [stage for stage in TARGETS if stage[1] <= low]
+    earlier_moved = {m: (refs[s], m - stage[0]) for s, stage in enumerate(stages) for m in range(*stage)}
+    refs = refs[len(stages) :]
     if last:
-        earlier, earlier_gains, earlier_after, offs_ref, own_a, own_b = refs[:6]
-        pieces = refs[6:-8]
-        gains_ref, out_ref = refs[-8:-6]
+        earlier_gains = {m: (refs[s], m - stage[0]) for s, stage in enumerate(stages) for m in range(*stage)}
+        offs_ref, gains_ref, out_ref, moved = refs[len(stages) :]
     else:
-        solved_ref, moved_ref, after_ref = refs[:3]
-    ends, values, state, m_now, k_now, moved = refs[-6:]
+        solved_ref, moved, out_ref = refs
     groups, count = hots.shape[:2]
     chunks = groups * tiles
-    kx_stride = near_kx.shape[0] // (chunks // 2)
-    m_stride = near_m.shape[0] // (chunks // 2)
-    x_start = kx_stride - M_ROWS * len(pair_list(low)) if low else 0
-    k_start = 0 if low else high * M_ROWS
-
-    def m_at(row):
-        return jnp.concatenate([ref[pl.ds(row, chunks // 2, stride=m_stride), :] for ref in (near_m, far_m)], axis=0)
-
-    def kx_at(row):
-        return jnp.concatenate([ref[pl.ds(row, chunks // 2, stride=kx_stride), :] for ref in (near_kx, far_kx)], axis=0)
+
+    def rows_at(pair, row):
+        stride = pair[0].shape[0] // (chunks // 2)
+        return jnp.concatenate([ref[pl.ds(row, chunks // 2, stride=stride), :] for ref in pair], axis=0)
 
     def fetch(gain_now, only=None):
         split = split_rows(gain_now)
@@ -322,21 +314,26 @@
         return gram
 
     def prepare(i):
+        [(pair, first, end)] = [(pair, *group) for pair, group in zip(products, GROUPS) if group[0] <= i < group[1]]
         for row in range(K_ROWS):
-            k_now[row] = kx_at(k_start + (i - low) * K_ROWS + row)
-        for out in range(4):
-            for w in range(4):
-                row = (out * 4 + w) * 2
-                value = (m_at((i - low) * M_ROWS + row), m_at((i - low) * M_ROWS + row + 1))
-                for m in range(i):
-                    base = x_start + pair_list(low).index((m, i)) * M_ROWS
-                    source = moved.at[m - low] if m >= low else earlier.at[m]
-                    for uv in range(4):
-                        delta = (source[(out * 4 + uv) * 2], source[(out * 4 + uv) * 2 + 1])
-                        at = base + (uv * 4 + w) * 2
-                        value = add(value, mul(delta, (kx_at(at), kx_at(at + 1))))
-                m_now[row] = value[0]
-                m_now[row + 1] = value[1]
+            k_now[row] = rows_at(pair, (i - first) * K_ROWS + row)
+        for w in range(4):
+            value = []
+            for out in range(4):
+                row = (i - low) * M_ROWS + (out * 4 + w) * 2
+                value.append((rows_at(targets, row), rows_at(targets, row + 1)))
+            for m in range(i):
+                base = (end - first) * K_ROWS + pair_list(first, end).index((m, i)) * M_ROWS
+                ref, place = (moved, m - low) if m >= low else earlier_moved[m]
+                for uv in range(4):
+                    at = base + (uv * 4 + w) * 2
+                    cross = (rows_at(pair, at), rows_at(pair, at + 1))
+                    for out in range(4):
+                        row = (out * 4 + uv) * 2
+                        value[out] = add(value[out], mul((ref[place, row], ref[place, row + 1]), cross))
+            for out in range(4):
+                m_now[(out * 4 + w) * 2] = value[out][0]
+                m_now[(out * 4 + w) * 2 + 1] = value[out][1]
 
     def hermitian(gain):
         a = gain[0][0] ** 2 + gain[0][1] ** 2 + gain[2][0] ** 2 + gain[2][1] ** 2
@@ -413,27 +410,27 @@
             rows += [y[0] * diag_a - high[0], y[1] * diag_a - high[1]]
         return jnp.concatenate([value * scale for value in rows], axis=0)
 
-    def add_change(i, coher_ref, after):
+    def add_change(i):
         for tile in range(tiles):
             at = pl.ds(tile * 128, 128)
-            coher = as_matrix([coher_ref[c, :, at] for c in range(8)])
+            coher = as_matrix([own_ref[i, c, :, at] for c in range(8)])
             rows = [tile * 8 + c for c in range(8)]
             one = [as_matrix([begin[i, end, row : row + 1, :] for row in rows]) for end in (0, 1)]
-            two = [as_matrix([after[end, row : row + 1, :] for row in rows]) for end in (0, 1)]
+            two = [as_matrix([ends[end, row : row + 1, :] for row in rows]) for end in (0, 1)]
             before, now = apply_gains(one[0], coher, one[1]), apply_gains(two[0], coher, two[1])
             for e in range(4):
                 change = sub(before[e], now[e])
                 out_ref[2 * e, :, at] += change[0]
                 out_ref[2 * e + 1, :, at] += change[1]
 
-    width = offs_ref.shape[2] if last else None
+    out_ref[...] = res_ref[...]
     if last:
+        width = offs_ref.shape[2]
         comp = lax.broadcasted_iota(jnp.int32, (8, width), 0)
         gains_ref[...] = offs_ref[...] + jnp.where((comp == 0) | (comp == 6), 1.0, 0.0)[None]
-        out_ref[...] = functools.reduce(lambda x, y: x + y, [piece[...] for piece in pieces])
         for i in range(low):
-            gains_ref[order_ref[i]] = earlier_gains[i, :, :width]
-            add_change(i, own_a.at[i], earlier_after.at[i])
+            ref, place = earlier_gains[i]
+            gains_ref[order_ref[i]] = ref[place, :, :width]
     values[...] = jnp.zeros(values.shape, F32)
     for i in range(low, high):
         which = order_ref[i]
@@ -453,27 +450,24 @@
 
         lax.fori_loop(0, jnp.minimum(counts_ref[which], LM_ITERS) - 1, more, jnp.int32(0))
         one_round()
+        fetch(state[...], 1 if i + 1 == SOLVED else None)
         if last:
             gains_ref[which] = state[:, :width]
-            fetch(state[...], 1 if i + 1 == high else None)
-            add_change(i, own_b.at[i - low], ends)
         else:
             solved_ref[i - low] = state[...]
-            fetch(state[...])
-            after_ref[i - low] = ends[:, : tiles * 8, :]
+        add_change(i)
         if i + 1 == SOLVED:
             break
         p0, q0 = gain_at(begin.at[i])
         p1, q1 = gain_at(ends)
-        store = moved if last else moved_ref
         for a in (0, 1):
             for b in (0, 1):
                 for u in (0, 1):
                     for v in (0, 1):
                         delta = sub(mul_conj(p0[2 * a + u], q0[2 * b + v]), mul_conj(p1[2 * a + u], q1[2 * b + v]))
                         row = ((2 * a + b) * 4 + 2 * u + v) * 2
-                        store[i - low, row] = delta[0]
-                        store[i - low, row + 1] = delta[1]
+                        moved[i - low, row] = delta[0]
+                        moved[i - low, row + 1] = delta[1]
 
 
 def exchange(block, axis, mask):
@@ -505,9 +499,7 @@
     width = gain_offsets.shape[2]
     count = groups * width
     tiles = baselines // 128
-    lanes = lax.axis_size("dir")
     params = pltpu.CompilerParams(vmem_limit_bytes=VMEM_BYTES)
-    rest = SOLVED - FIRST
 
     def call(kernel, name, shapes, scalars, arrays, scratch=(), **static):
         return pl.pallas_call(
@@ -526,99 +518,105 @@
     block = coherencies.shape[1:]
     whole = lambda shape: pl.BlockSpec(shape, lambda g, order: (0,) * len(shape))
     picked = lambda i: pl.BlockSpec((1,) + block, lambda g, order: (order[i] % owned, 0, 0, 0))
-    shapes = [(part_rows + 8, 128), (FIRST,) + block, (rest,) + block]
-    packed, chosen_first, chosen_rest = pl.pallas_call(
+    shapes = [(part_rows + 8, 128)] + [(high - low,) + block for low, high in GROUPS]
+    packed, *chosen = pl.pallas_call(
         functools.partial(prep_kernel, owned=owned, per=per),
-        out_shape=[jax.ShapeDtypeStruct(shape, dtype) for shape, dtype in zip(shapes, (F32, BF16, BF16))],
+        out_shape=[jax.ShapeDtypeStruct(shape, dtype) for shape, dtype in zip(shapes, [F32] + [BF16] * len(GROUPS))],
         grid_spec=pltpu.PrefetchScalarGridSpec(
             num_scalar_prefetch=1,
             grid=(1,),
             in_specs=[whole(stations.shape), whole(gain_offsets.shape)] + [picked(i) for i in range(SOLVED)],
             out_specs=[whole(shape) for shape in shapes],
         ),
-        compiler_params=params,
+        compiler_params=pltpu.CompilerParams(vmem_limit_bytes=MOST_VMEM_BYTES),
         name="prepare",
     )(solve_order, stations, gain_offsets, *[coherencies] * SOLVED)
 
     near = chip_blocks(packed, "bl")
     blocks = jnp.stack([near, exchange(near, "bl", 1)], axis=1).reshape(groups, part_rows + 8, 128)
-    shared_first = butterfly_sum(chosen_first, "dir")
-    shared_rest = butterfly_sum(chosen_rest, "dir")
+    shared = [butterfly_sum(value, "dir") for value in chosen]
 
     table = ((part_rows * per, count), F32)
-    part, begin, *pieces = call(
+    part, begin = call(
         model_kernel,
         "first_model",
-        [((8, channel_count, baselines), F32), ((SOLVED * 8, 2 * baselines), F32)] + [(visibilities.shape, F32)] * lanes,
+        [((8, channel_count, baselines), F32), ((SOLVED * 8, 2 * baselines), F32)],
         [],
         [blocks, coherencies, visibilities],
         [table, ((part_rows * per, 2 * baselines), F32)],
         width=width,
     )
-    [m_first] = call(
-        target_kernel, "first_target", [((tiles, FIRST * M_ROWS, 128), F32)], [solve_order],
-        [part, shared_first, begin], owned=owned, low=0,
+    chunks = groups * tiles
+    hots, ends, start = call(
+        lookup_kernel,
+        "lookup",
+        [((groups, count, 2 * baselines), BF16), ((SOLVED, 2, chunks * 8, 128), F32), ((SOLVED * 8, count), F32)],
+        [],
+        [blocks],
+        [table],
+        width=width,
+        owned=owned,
     )
-    k_first, own_first = call(
-        product_kernel, "first_products",
-        [((tiles, FIRST * K_ROWS, 128), F32), ((FIRST, 8, channels, baselines), F32)], [], [shared_first], low=0,
+    first = butterfly_sum(part, "dir")
+    res, own = call(
+        own_kernel,
+        "own_channels",
+        [(visibilities.shape, F32), ((SOLVED, 8, channels, baselines), F32)],
+        [],
+        [first, *shared],
     )
-    hots, ends, start = call(
-        lookup_kernel, "lookup",
-        [
-            ((groups, count, 2 * baselines), BF16),
-            ((SOLVED, 2, groups * tiles * 8, 128), F32),
-            ((SOLVED * 8, count), F32),
-        ],
-        [], [blocks], [table], width=width, owned=owned,
-    )
-    [m_rest] = call(
-        target_kernel, "other_targets", [((tiles, rest * M_ROWS, 128), F32)], [solve_order],
-        [part, shared_rest, begin], owned=owned, low=FIRST,
-    )
-    kx_rows = rest * K_ROWS + len(pair_list(FIRST)) * M_ROWS
-    kx_rest, own_rest = call(
-        product_kernel, "other_products",
-        [((tiles, kx_rows, 128), F32), ((rest, 8, channels, baselines), F32)], [], [shared_first, shared_rest], low=FIRST,
-    )
-
-    first_near = chip_blocks(jnp.concatenate([butterfly_sum(m_first, "dir"), k_first], axis=1), "bl")
-    first_far = exchange(first_near, "bl", 1)
-    pieces = [pieces[0]] + [exchange(piece, "dir", k) for k, piece in enumerate(pieces) if k]
-    kx_near = chip_blocks(kx_rest, "bl")
-    kx_far = exchange(kx_near, "bl", 1)
-    m_near = chip_blocks(butterfly_sum(m_rest, "dir"), "bl")
-    m_far = exchange(m_near, "bl", 1)
-
-    chunks = groups * tiles
-    static = dict(tiles=tiles, factor=baselines * groups * channel_count / count)
-    scratch = [
-        ((2, chunks * 8, 128), F32),
-        ((2, chunks * 16, 128), F32),
-        ((8, count), F32),
-        ((M_ROWS, chunks, 128), F32),
-        ((K_ROWS, chunks, 128), F32),
-    ]
-    flat = lambda *arrays: [array.reshape(-1, 128) for array in arrays]
-    scalars = [solve_order, counts, damping]
-    solved_first, moved_first, after_first = call(
-        sweep_kernel, "first_sweep",
-        [((FIRST, 8, count), F32), ((FIRST, M_ROWS, chunks, 128), F32), ((FIRST, 2, tiles * 8, 128), F32)],
-        scalars,
-        [hots, ends, start] + flat(first_near, first_far, first_near, first_far),
-        scratch + [((1, 8, 128), F32)],
-        low=0, high=FIRST, last=False, **static,
-    )
-    gains, residual = call(
-        sweep_kernel, "other_sweeps",
-        [(gain_offsets.shape, F32), (visibilities.shape, F32)],
-        scalars,
-        [hots, ends, start] + flat(m_near, m_far, kx_near, kx_far)
-        + [moved_first, solved_first, after_first, gain_offsets, own_first, own_rest] + pieces,
-        scratch + [((rest, M_ROWS, chunks, 128), F32)],
-        low=FIRST, high=SOLVED, last=True, **static,
-    )
-    return gains, residual
+    moved, solved = [], []
+    flat = lambda near: [near.reshape(-1, 128), exchange(near, "bl", 1).reshape(-1, 128)]
+    products = []
+    for g, (low, high) in enumerate(GROUPS):
+        rows = (high - low) * K_ROWS + len(pair_list(low, high)) * M_ROWS
+        [value] = call(
+            product_kernel, "products", [((tiles, rows, 128), F32)], [], shared[: g + 1], low=low, high=high
+        )
+        products += flat(chip_blocks(value, "bl"))
+    for low, high in TARGETS:
+        [value] = call(
+            target_kernel,
+            "targets",
+            [((tiles, (high - low) * M_ROWS, 128), F32)],
+            [],
+            [first, begin] + shared,
+            low=low,
+            high=high,
+        )
+        targets = flat(chip_blocks(value, "bl"))
+        last = high == SOLVED
+        moved_shape = ((high - low, M_ROWS, chunks, 128), F32)
+        outs = call(
+            sweep_kernel,
+            "sweep",
+            [(gain_offsets.shape, F32), (visibilities.shape, F32)]
+            if last
+            else [((high - low, 8, count), F32), moved_shape, (visibilities.shape, F32)],
+            [solve_order, counts, damping],
+            [hots, ends, start, res, own]
+            + targets
+            + products
+            + moved
+            + (solved + [gain_offsets] if last else []),
+            ([moved_shape] if last else [])
+            + [
+                ((2, chunks * 8, 128), F32),
+                ((2, chunks * 16, 128), F32),
+                ((8, count), F32),
+                ((M_ROWS, chunks, 128), F32),
+                ((K_ROWS, chunks, 128), F32),
+            ],
+            low=low,
+            high=high,
+            tiles=tiles,
+            factor=baselines * groups * channel_count / count,
+        )
+        if not last:
+            solved.append(outs[0])
+            moved.append(outs[1])
+            res = outs[2]
+    return outs[0], outs[1]
 
 
 def solution(mesh):

time: 101 us -> 76 us (0.75); the launches traced: 99.7 us -> 75.7 us
  starting transfers between devices: 39.1 us -> 24.2 us
  waiting for transfers between devices: 36 us -> 26.1 us
  local copies, waits for them, and re-layouts: 3.32 us -> 0.05 us
  other arithmetic: 0.36 us -> 2.88 us
  Pallas kernels: 20 us -> 21.6 us
    ppermute x27 -> x22, starting transfers between devices: 39.1 us -> 24.2 us  [exchange(): lax.ppermute(block, axis, [(i, i ^ mask) for i in range(lax.axis_size(axi...]
    ppermute x27 -> x22, waiting for transfers between devices: 36 us -> 26.1 us  [exchange(): lax.ppermute(block, axis, [(i, i ^ mask) for i in range(lax.axis_size(axi...]
    unnamed x20 -> x12, local copies, waits for them, and re-layouts: 3.31 us -> 0.03 us
    pallas_call x1, Pallas kernels: 0.66 us -> 2.54 us  [on_device(): pl.pallas_call(functools.partial(prep_kernel, owned=owned, per=per), out_...]
    add x8 -> x6, other arithmetic: 0.19 us -> 1.99 us  [butterfly_sum(): value = value + exchange(value, axis, mask)]
    pallas_call x8 -> x7, Pallas kernels: 19.3 us -> 19.1 us  [call(): pl.pallas_call(functools.partial(kernel, **static), out_shape=[jax.ShapeD...]
  transfers between devices with their start and end apart: 27 -> 22, of which waited for: 12 -> 12; matrix products, arithmetic and copies ran while one was open for 0% -> 4% of each run, Pallas kernels for 7% -> 5%
where the time goes in v1:
time: 76 us; the launch traced here: 75.7 us
  waiting for transfers between devices  26.1 us (34%)
  starting transfers between devices  24.2 us (32%)
  Pallas kernels  21.6 us (28%)
  other arithmetic  2.88 us (4%)
  between operations  0.86 us (1%)
    ppermute x22, waiting for transfers between devices, exchange(): lax.ppermute(block, axis, [(i, i ^ mask) for i in range(lax.axis_size(axi...  26.1 us
    ppermute x22, starting transfers between devices, exchange(): lax.ppermute(block, axis, [(i, i ^ mask) for i in range(lax.axis_size(axi...  24.2 us
    pallas_call x7, Pallas kernels, call(): pl.pallas_call(functools.partial(kernel, **static), out_shape=[jax.ShapeD...  19.1 us
    pallas_call x1, Pallas kernels, on_device(): pl.pallas_call(functools.partial(prep_kernel, owned=owned, per=per), out_...  2.54 us
    add x6, other arithmetic, butterfly_sum(): value = value + exchange(value, axis, mask)  1.99 us
  transfers between devices with their start and end apart: 22, of which 12 were waited for; matrix products, arithmetic and copies ran while one was open for 4% of the time, Pallas kernels for 5%

profile of v1, /device:TPU:0, one launch (start us, length us, event | category | flops | bytes accessed | tf_op | source)
XLA Modules:
  0.0 75.7 jit_solution(16140928056773957631)
XLA Ops:
  0.6 2.5 %prepare.1 = (f32[56,128]{1,0:T(8,128)}, bf16[2,8,16,256]{3,2,1,0:T(8,128)(2,1)}, bf16[2,8,16,256]{3,2,1,0:T(8,128)(2,1)}) custom-call(s32[32]{0:T(128)} %order_ref.3, s32[2,256]{1,0:T(2,128)} %stations_ref.1, f32[32,8,64]{2,1,0:T(8,128)} %refs_11_.1, bf16[8,8,16,256]{3,2,1,0:T(8,128)(2,1)} %coher_ref.1, bf16[8,8,16,256]{3,2,1,0:T(8,128)(2,1)} %coher_ref.1, ...), custom_call_target="tpu_custom_call" | custom-call | tf_op jit(solution)/shard_map/prepare/pallas_call | solution.py:522
  3.2 3.0 %collective-permute-start.6 = (bf16[2,8,16,256]{3,2,1,0:T(8,128)(2,1)}, bf16[2,8,16,256]{3,2,1,0:T(8,128)(2,1)S(1)}, u32[]{:S(2)}, u32[]{:S(2)}) collective-permute-start(bf16[2,8,16,256]{3,2,1,0:T(8,128)(2,1)} %get-tuple-element.17), channel_id=1, source_target_pairs={{0,1},{1,0},{2,3},{3,2},{4,5},{5,4},{6,7},{7,6},{8,9},{9,8},{10,11... | collective-permute-start | bytes 393224 | tf_op jit(solution)/shard_map/ppermute | solution.py:474
  6.2 2.9 %collective-permute-start.2 = (f32[56,128]{1,0:T(8,128)}, f32[56,128]{1,0:T(8,128)S(1)}, u32[]{:S(2)}, u32[]{:S(2)}) collective-permute-start(f32[56,128]{1,0:T(8,128)} %get-tuple-element.12), channel_id=1, source_target_pairs={{0,24},{4,28},{8,16},{12,20},{16,8},{20,12},{24,0},{28,4},{1,25},{... | collective-permute-start | bytes 86024 | tf_op jit(solution)/shard_map/ppermute | solution.py:474
  9.7 1.0 %collective-permute-done.6 = bf16[2,8,16,256]{3,2,1,0:T(8,128)(2,1)S(1)} collective-permute-done((bf16[2,8,16,256]{3,2,1,0:T(8,128)(2,1)}, bf16[2,8,16,256]{3,2,1,0:T(8,128)(2,1)S(1)}, u32[]{:S(2)}, u32[]{:S(2)}) %collective-permute-start.6) | collective-permute-done | bytes 131104 | tf_op jit(solution)/shard_map/ppermute | solution.py:474
  10.7 0.9 %add.20 = bf16[2,8,16,256]{3,2,1,0:T(8,128)(2,1)S(1)} add(bf16[2,8,16,256]{3,2,1,0:T(8,128)(2,1)} %get-tuple-element.17, bf16[2,8,16,256]{3,2,1,0:T(8,128)(2,1)S(1)} %collective-permute-done.6) | non-fusion elementwise | flops 65536 | bytes 393216 | tf_op jit(solution)/shard_map/add | solution.py:480
  11.7 3.1 %collective-permute-start.7 = (bf16[2,8,16,256]{3,2,1,0:T(8,128)(2,1)S(1)}, bf16[2,8,16,256]{3,2,1,0:T(8,128)(2,1)S(1)}, u32[]{:S(2)}, u32[]{:S(2)}) collective-permute-start(bf16[2,8,16,256]{3,2,1,0:T(8,128)(2,1)S(1)} %add.20), channel_id=1, source_target_pairs={{0,2},{1,3},{2,0},{3,1},{4,6},{5,7},{6,4},{7,5},{8,10},{9,11},{10,... | collective-permute-start | bytes 393224 | tf_op jit(solution)/shard_map/ppermute | solution.py:474
  14.8 0.9 %add.22 = bf16[2,8,16,256]{3,2,1,0:T(8,128)(2,1)S(1)} add(bf16[2,8,16,256]{3,2,1,0:T(8,128)(2,1)} %get-tuple-element.18, bf16[2,8,16,256]{3,2,1,0:T(8,128)(2,1)S(1)} %collective-permute-done.8) | non-fusion elementwise | flops 65536 | bytes 393216 | tf_op jit(solution)/shard_map/add | solution.py:480
  15.8 1.0 %collective-permute-start.9 = (bf16[2,8,16,256]{3,2,1,0:T(8,128)(2,1)S(1)}, bf16[2,8,16,256]{3,2,1,0:T(8,128)(2,1)S(1)}, u32[]{:S(2)}, u32[]{:S(2)}) collective-permute-start(bf16[2,8,16,256]{3,2,1,0:T(8,128)(2,1)S(1)} %add.22), channel_id=1, source_target_pairs={{0,2},{1,3},{2,0},{3,1},{4,6},{5,7},{6,4},{7,5},{8,10},{9,11},{10,... | collective-permute-start | bytes 393224 | tf_op jit(solution)/shard_map/ppermute | solution.py:474
  16.8 0.8 %fusion = (f32[4,1,56,128]{3,2,0,1:T(8,128)S(1)}, f32[4,56,128]{2,1,0:T(8,128)S(1)}) fusion(f32[1,56,128]{2,1,0:T(8,128)S(1)} %bitcast.48, f32[1,56,128]{2,1,0:T(8,128)S(1)} %bitcast.49, f32[1,56,128]{2,1,0:T(8,128)S(1)} %bitcast.50, f32[1,56,128]{2,1,0:T(8,128)} %bitcast.47), kind=kLoop, calls=%fused_computation.5 | loop fusion | flops 86016 | bytes 344064 | tf_op jit(solution)/shard_map/stack | solution.py:536
  17.7 5.5 %collective-permute-done.7 = bf16[2,8,16,256]{3,2,1,0:T(8,128)(2,1)S(1)} collective-permute-done((bf16[2,8,16,256]{3,2,1,0:T(8,128)(2,1)S(1)}, bf16[2,8,16,256]{3,2,1,0:T(8,128)(2,1)S(1)}, u32[]{:S(2)}, u32[]{:S(2)}) %collective-permute-start.7) | collective-permute-done | bytes 131104 | tf_op jit(solution)/shard_map/ppermute | solution.py:474
  23.3 1.7 %collective-permute-done.9 = bf16[2,8,16,256]{3,2,1,0:T(8,128)(2,1)S(1)} collective-permute-done((bf16[2,8,16,256]{3,2,1,0:T(8,128)(2,1)S(1)}, bf16[2,8,16,256]{3,2,1,0:T(8,128)(2,1)S(1)}, u32[]{:S(2)}, u32[]{:S(2)}) %collective-permute-start.9) | collective-permute-done | bytes 131104 | tf_op jit(solution)/shard_map/ppermute | solution.py:474
  25.0 0.7 products.3
  25.7 2.7 %collective-permute-start.20 = (f32[2,192,128]{2,1,0:T(8,128)S(1)}, f32[2,192,128]{2,1,0:T(8,128)S(1)}, u32[]{:S(2)}, u32[]{:S(2)}) collective-permute-start(f32[2,192,128]{2,1,0:T(8,128)S(1)} %products.3), channel_id=1, source_target_pairs={{0,24},{4,28},{8,16},{12,20},{16,8},{20,12},{24,0},{28,4},{1,25},{... | collective-permute-start | bytes 589832 | tf_op jit(solution)/shard_map/ppermute | solution.py:474
  28.4 0.5 collective-permute-start.19
  29.3 1.0 %first_model.1 = (f32[8,16,256]{2,1,0:T(8,128)S(1)}, f32[32,512]{1,0:T(8,128)S(1)}) custom-call(f32[8,56,128]{2,1,0:T(8,128)S(1)} %bitcast.28, bf16[8,8,16,256]{3,2,1,0:T(8,128)(2,1)S(1)} %copy-done, f32[8,4,256]{2,1,0:T(4,128)S(1)} %copy-done.2), custom_call_target="tpu_custom_call" | custom-call | tf_op jit(solution)/shard_map/first_model/pallas_call | solution.py:505
  30.3 0.6 collective-permute-start.4
  30.9 4.4 %collective-permute-done.4 = f32[8,16,256]{2,1,0:T(8,128)S(1)} collective-permute-done((f32[8,16,256]{2,1,0:T(8,128)S(1)}, f32[8,16,256]{2,1,0:T(8,128)S(1)}, u32[]{:S(2)}, u32[]{:S(2)}) %collective-permute-start.4) | collective-permute-done | bytes 131104 | tf_op jit(solution)/shard_map/ppermute | solution.py:474
  35.4 2.0 %collective-permute-start.5 = (f32[8,16,256]{2,1,0:T(8,128)S(1)}, f32[8,16,256]{2,1,0:T(8,128)S(1)}, u32[]{:S(2)}, u32[]{:S(2)}) collective-permute-start(f32[8,16,256]{2,1,0:T(8,128)S(1)} %add.18), channel_id=1, source_target_pairs={{0,2},{1,3},{2,0},{3,1},{4,6},{5,7},{6,4},{7,5},{8,10},{9,11},{10,... | collective-permute-start | bytes 393224 | tf_op jit(solution)/shard_map/ppermute | solution.py:474
  37.5 5.2 %collective-permute-done.5 = f32[8,16,256]{2,1,0:T(8,128)S(1)} collective-permute-done((f32[8,16,256]{2,1,0:T(8,128)S(1)}, f32[8,16,256]{2,1,0:T(8,128)S(1)}, u32[]{:S(2)}, u32[]{:S(2)}) %collective-permute-start.5) | collective-permute-done | bytes 131104 | tf_op jit(solution)/shard_map/ppermute | solution.py:474
  42.7 0.7 targets.1
  43.5 2.7 %collective-permute-start.12 = (f32[2,128,128]{2,1,0:T(8,128)S(1)}, f32[2,128,128]{2,1,0:T(8,128)S(1)}, u32[]{:S(2)}, u32[]{:S(2)}) collective-permute-start(f32[2,128,128]{2,1,0:T(8,128)S(1)} %targets.1), channel_id=1, source_target_pairs={{0,24},{4,28},{8,16},{12,20},{16,8},{20,12},{24,0},{28,4},{1,25},{... | collective-permute-start | bytes 393224 | tf_op jit(solution)/shard_map/ppermute | solution.py:474
  46.2 0.5 collective-permute-start.11
  47.0 2.4 %collective-permute-done.12 = f32[2,128,128]{2,1,0:T(8,128)S(1)} collective-permute-done((f32[2,128,128]{2,1,0:T(8,128)S(1)}, f32[2,128,128]{2,1,0:T(8,128)S(1)}, u32[]{:S(2)}, u32[]{:S(2)}) %collective-permute-start.12) | collective-permute-done | bytes 131104 | tf_op jit(solution)/shard_map/ppermute | solution.py:474
  49.4 1.7 %collective-permute-done.11 = f32[2,128,128]{2,1,0:T(8,128)S(1)} collective-permute-done((f32[2,128,128]{2,1,0:T(8,128)S(1)}, f32[2,128,128]{2,1,0:T(8,128)S(1)}, u32[]{:S(2)}, u32[]{:S(2)}) %collective-permute-start.11) | collective-permute-done | bytes 131104 | tf_op jit(solution)/shard_map/ppermute | solution.py:474
  51.1 0.5 collective-permute-done.10
  52.0 1.6 %collective-permute-start.16 = (f32[2,64,128]{2,1,0:T(8,128)S(1)}, f32[2,64,128]{2,1,0:T(8,128)S(1)}, u32[]{:S(2)}, u32[]{:S(2)}) collective-permute-start(f32[2,64,128]{2,1,0:T(8,128)S(1)} %products.2), channel_id=1, source_target_pairs={{0,24},{4,28},{8,16},{12,20},{16,8},{20,12},{24,0},{28,4},{1,25},{... | collective-permute-start | bytes 196616 | tf_op jit(solution)/shard_map/ppermute | solution.py:474
  53.6 0.9 %collective-permute-start.15 = (f32[2,64,128]{2,1,0:T(8,128)S(1)}, f32[2,64,128]{2,1,0:T(8,128)S(1)}, u32[]{:S(2)}, u32[]{:S(2)}) collective-permute-start(f32[2,64,128]{2,1,0:T(8,128)S(1)} %products.2), channel_id=1, source_target_pairs={{0,16},{4,20},{8,24},{12,28},{16,0},{20,4},{24,8},{28,12},{1,17},{... | collective-permute-start | bytes 196616 | tf_op jit(solution)/shard_map/ppermute | solution.py:474
  54.5 1.1 %collective-permute-start.14 = (f32[2,64,128]{2,1,0:T(8,128)S(1)}, f32[2,64,128]{2,1,0:T(8,128)S(1)}, u32[]{:S(2)}, u32[]{:S(2)}) collective-permute-start(f32[2,64,128]{2,1,0:T(8,128)S(1)} %products.2), channel_id=1, source_target_pairs={{0,8},{4,12},{8,0},{12,4},{16,24},{20,28},{24,16},{28,20},{1,9},{5... | collective-permute-start | bytes 196616 | tf_op jit(solution)/shard_map/ppermute | solution.py:474
  55.6 2.0 %collective-permute-done.16 = f32[2,64,128]{2,1,0:T(8,128)S(1)} collective-permute-done((f32[2,64,128]{2,1,0:T(8,128)S(1)}, f32[2,64,128]{2,1,0:T(8,128)S(1)}, u32[]{:S(2)}, u32[]{:S(2)}) %collective-permute-start.16) | collective-permute-done | bytes 65568 | tf_op jit(solution)/shard_map/ppermute | solution.py:474
  57.6 1.3 %collective-permute-done.15 = f32[2,64,128]{2,1,0:T(8,128)S(1)} collective-permute-done((f32[2,64,128]{2,1,0:T(8,128)S(1)}, f32[2,64,128]{2,1,0:T(8,128)S(1)}, u32[]{:S(2)}, u32[]{:S(2)}) %collective-permute-start.15) | collective-permute-done | bytes 65568 | tf_op jit(solution)/shard_map/ppermute | solution.py:474
  59.1 1.2 %lookup.1 = (bf16[8,512,512]{2,1,0:T(8,128)(2,1)S(1)}, f32[4,2,128,128]{3,2,1,0:T(8,128)S(1)}, f32[32,512]{1,0:T(8,128)S(1)}) custom-call(f32[8,56,128]{2,1,0:T(8,128)S(1)} %bitcast.29), custom_call_target="tpu_custom_call" | custom-call | tf_op jit(solution)/shard_map/lookup/pallas_call | solution.py:505
  60.6 15.1 %sweep.1 = (f32[32,8,64]{2,1,0:T(8,128)}, f32[8,4,256]{2,1,0:T(4,128)}) custom-call(s32[32]{0:T(128)S(1)} %copy-done.3, s32[32]{0:T(128)S(1)} %copy-done.4, s32[32]{0:T(128)S(1)} %copy-done.5, bf16[8,512,512]{2,1,0:T(8,128)(2,1)S(1)} %get-tuple-element.13.refs_0_, f32[4,2,128,128]{3,2,1,0:T(8,128)S(1)} %get-tuple-element.14.refs_1_, ...), custom_call_target="tpu_custom_call" | custom-call | tf_op jit(solution)/shard_map/sweep/pallas_call | solution.py:505
  (44 shorter events, 2.6 us)
Async XLA Ops:
  0.6 28.7 %copy-start = (bf16[8,8,16,256]{3,2,1,0:T(8,128)(2,1)S(1)}, bf16[8,8,16,256]{3,2,1,0:T(8,128)(2,1)}, u32[]{:S(2)}) copy-start(bf16[8,8,16,256]{3,2,1,0:T(8,128)(2,1)} %coher_ref.1) | copy-start | bytes 1572868
  0.6 28.7 %copy-start.2 = (f32[8,4,256]{2,1,0:T(4,128)S(1)}, f32[8,4,256]{2,1,0:T(4,128)}, u32[]{:S(2)}) copy-start(f32[8,4,256]{2,1,0:T(4,128)} %vis_ref.1) | copy-start | bytes 98308
  3.2 7.6 %collective-permute-start.6 = (bf16[2,8,16,256]{3,2,1,0:T(8,128)(2,1)}, bf16[2,8,16,256]{3,2,1,0:T(8,128)(2,1)S(1)}, u32[]{:S(2)}, u32[]{:S(2)}) collective-permute-start(bf16[2,8,16,256]{3,2,1,0:T(8,128)(2,1)} %get-tuple-element.17), channel_id=1, source_target_pairs={{0,1},{1,0},{2,3},{3,2},{4,5},{5,4},{6,7},{7,6},{8,9},{9,8},{10,11... | collective-permute-start | bytes 393224 | tf_op jit(solution)/shard_map/ppermute | solution.py:474
  6.2 8.6 %collective-permute-start.8 = (bf16[2,8,16,256]{3,2,1,0:T(8,128)(2,1)}, bf16[2,8,16,256]{3,2,1,0:T(8,128)(2,1)S(1)}, u32[]{:S(2)}, u32[]{:S(2)}) collective-permute-start(bf16[2,8,16,256]{3,2,1,0:T(8,128)(2,1)} %get-tuple-element.18), channel_id=1, source_target_pairs={{0,1},{1,0},{2,3},{3,2},{4,5},{5,4},{6,7},{7,6},{8,9},{9,8},{10,11... | collective-permute-start | bytes 393224 | tf_op jit(solution)/shard_map/ppermute | solution.py:474
  6.2 10.5 %collective-permute-start.2 = (f32[56,128]{1,0:T(8,128)}, f32[56,128]{1,0:T(8,128)S(1)}, u32[]{:S(2)}, u32[]{:S(2)}) collective-permute-start(f32[56,128]{1,0:T(8,128)} %get-tuple-element.12), channel_id=1, source_target_pairs={{0,24},{4,28},{8,16},{12,20},{16,8},{20,12},{24,0},{28,4},{1,25},{... | collective-permute-start | bytes 86024 | tf_op jit(solution)/shard_map/ppermute | solution.py:474
  9.1 7.7 %collective-permute-start.1 = (f32[56,128]{1,0:T(8,128)}, f32[56,128]{1,0:T(8,128)S(1)}, u32[]{:S(2)}, u32[]{:S(2)}) collective-permute-start(f32[56,128]{1,0:T(8,128)} %get-tuple-element.12), channel_id=1, source_target_pairs={{0,16},{4,20},{8,24},{12,28},{16,0},{20,4},{24,8},{28,12},{1,17},{... | collective-permute-start | bytes 86024 | tf_op jit(solution)/shard_map/ppermute | solution.py:474
  9.6 7.2 %collective-permute-start = (f32[56,128]{1,0:T(8,128)}, f32[56,128]{1,0:T(8,128)S(1)}, u32[]{:S(2)}, u32[]{:S(2)}) collective-permute-start(f32[56,128]{1,0:T(8,128)} %get-tuple-element.12), channel_id=1, source_target_pairs={{0,8},{4,12},{8,0},{12,4},{16,24},{20,28},{24,16},{28,20},{1,9},{5... | collective-permute-start | bytes 86024 | tf_op jit(solution)/shard_map/ppermute | solution.py:474
  11.7 11.6 %collective-permute-start.7 = (bf16[2,8,16,256]{3,2,1,0:T(8,128)(2,1)S(1)}, bf16[2,8,16,256]{3,2,1,0:T(8,128)(2,1)S(1)}, u32[]{:S(2)}, u32[]{:S(2)}) collective-permute-start(bf16[2,8,16,256]{3,2,1,0:T(8,128)(2,1)S(1)} %add.20), channel_id=1, source_target_pairs={{0,2},{1,3},{2,0},{3,1},{4,6},{5,7},{6,4},{7,5},{8,10},{9,11},{10,... | collective-permute-start | bytes 393224 | tf_op jit(solution)/shard_map/ppermute | solution.py:474
  15.8 9.2 %collective-permute-start.9 = (bf16[2,8,16,256]{3,2,1,0:T(8,128)(2,1)S(1)}, bf16[2,8,16,256]{3,2,1,0:T(8,128)(2,1)S(1)}, u32[]{:S(2)}, u32[]{:S(2)}) collective-permute-start(bf16[2,8,16,256]{3,2,1,0:T(8,128)(2,1)S(1)} %add.22), channel_id=1, source_target_pairs={{0,2},{1,3},{2,0},{3,1},{4,6},{5,7},{6,4},{7,5},{8,10},{9,11},{10,... | collective-permute-start | bytes 393224 | tf_op jit(solution)/shard_map/ppermute | solution.py:474
  17.6 43.0 %copy-start.1 = (f32[32,8,64]{2,1,0:T(8,128)S(1)}, f32[32,8,64]{2,1,0:T(8,128)}, u32[]{:S(2)}) copy-start(f32[32,8,64]{2,1,0:T(8,128)} %refs_11_.1) | copy-start | bytes 196612
  17.6 43.0 %copy-start.3 = (s32[32]{0:T(128)S(1)}, s32[32]{0:T(128)}, u32[]{:S(2)}) copy-start(s32[32]{0:T(128)} %order_ref.3) | copy-start | bytes 388
  17.6 43.0 %copy-start.4 = (s32[32]{0:T(128)S(1)}, s32[32]{0:T(128)}, u32[]{:S(2)}) copy-start(s32[32]{0:T(128)} %counts_ref.1) | copy-start | bytes 388
  17.6 43.0 %copy-start.5 = (s32[32]{0:T(128)S(1)}, s32[32]{0:T(128)}, u32[]{:S(2)}) copy-start(s32[32]{0:T(128)} %damping_ref.1) | copy-start | bytes 388
  17.6 11.6 %collective-permute-start.3 = (f32[4,56,128]{2,1,0:T(8,128)S(1)}, f32[4,56,128]{2,1,0:T(8,128)S(1)}, u32[]{:S(2)}, u32[]{:S(2)}) collective-permute-start(f32[4,56,128]{2,1,0:T(8,128)S(1)} %get-tuple-element.23), channel_id=1, source_target_pairs={{0,4},{4,0},{8,12},{12,8},{16,20},{20,16},{24,28},{28,24},{1,5},{5... | collective-permute-start | bytes 344072 | tf_op jit(solution)/shard_map/ppermute | solution.py:474
  25.7 11.6 %collective-permute-start.20 = (f32[2,192,128]{2,1,0:T(8,128)S(1)}, f32[2,192,128]{2,1,0:T(8,128)S(1)}, u32[]{:S(2)}, u32[]{:S(2)}) collective-permute-start(f32[2,192,128]{2,1,0:T(8,128)S(1)} %products.3), channel_id=1, source_target_pairs={{0,24},{4,28},{8,16},{12,20},{16,8},{20,12},{24,0},{28,4},{1,25},{... | collective-permute-start | bytes 589832 | tf_op jit(solution)/shard_map/ppermute | solution.py:474
  28.4 8.9 %collective-permute-start.19 = (f32[2,192,128]{2,1,0:T(8,128)S(1)}, f32[2,192,128]{2,1,0:T(8,128)S(1)}, u32[]{:S(2)}, u32[]{:S(2)}) collective-permute-start(f32[2,192,128]{2,1,0:T(8,128)S(1)} %products.3), channel_id=1, source_target_pairs={{0,16},{4,20},{8,24},{12,28},{16,0},{20,4},{24,8},{28,12},{1,17},{... | collective-permute-start | bytes 589832 | tf_op jit(solution)/shard_map/ppermute | solution.py:474
  28.9 8.4 %collective-permute-start.18 = (f32[2,192,128]{2,1,0:T(8,128)S(1)}, f32[2,192,128]{2,1,0:T(8,128)S(1)}, u32[]{:S(2)}, u32[]{:S(2)}) collective-permute-start(f32[2,192,128]{2,1,0:T(8,128)S(1)} %products.3), channel_id=1, source_target_pairs={{0,8},{4,12},{8,0},{12,4},{16,24},{20,28},{24,16},{28,20},{1,9},{5... | collective-permute-start | bytes 589832 | tf_op jit(solution)/shard_map/ppermute | solution.py:474
  30.3 5.0 %collective-permute-start.4 = (f32[8,16,256]{2,1,0:T(8,128)S(1)}, f32[8,16,256]{2,1,0:T(8,128)S(1)}, u32[]{:S(2)}, u32[]{:S(2)}) collective-permute-start(f32[8,16,256]{2,1,0:T(8,128)S(1)} %get-tuple-element.16), channel_id=1, source_target_pairs={{0,1},{1,0},{2,3},{3,2},{4,5},{5,4},{6,7},{7,6},{8,9},{9,8},{10,11... | collective-permute-start | bytes 393224 | tf_op jit(solution)/shard_map/ppermute | solution.py:474
  35.4 7.3 %collective-permute-start.5 = (f32[8,16,256]{2,1,0:T(8,128)S(1)}, f32[8,16,256]{2,1,0:T(8,128)S(1)}, u32[]{:S(2)}, u32[]{:S(2)}) collective-permute-start(f32[8,16,256]{2,1,0:T(8,128)S(1)} %add.18), channel_id=1, source_target_pairs={{0,2},{1,3},{2,0},{3,1},{4,6},{5,7},{6,4},{7,5},{8,10},{9,11},{10,... | collective-permute-start | bytes 393224 | tf_op jit(solution)/shard_map/ppermute | solution.py:474
  37.4 23.2 %collective-permute-start.21 = (f32[4,2,192,128]{3,2,1,0:T(8,128)S(1)}, f32[4,2,192,128]{3,2,1,0:T(8,128)S(1)}, u32[]{:S(2)}, u32[]{:S(2)}) collective-permute-start(f32[4,2,192,128]{3,2,1,0:T(8,128)S(1)} %pad_maximum_fusion), channel_id=1, source_target_pairs={{0,4},{4,0},{8,12},{12,8},{16,20},{20,16},{24,28},{28,24},{1,5},{5... | collective-permute-start | bytes 2359304 | tf_op jit(solution)/shard_map/ppermute | solution.py:474
  43.5 5.9 %collective-permute-start.12 = (f32[2,128,128]{2,1,0:T(8,128)S(1)}, f32[2,128,128]{2,1,0:T(8,128)S(1)}, u32[]{:S(2)}, u32[]{:S(2)}) collective-permute-start(f32[2,128,128]{2,1,0:T(8,128)S(1)} %targets.1), channel_id=1, source_target_pairs={{0,24},{4,28},{8,16},{12,20},{16,8},{20,12},{24,0},{28,4},{1,25},{... | collective-permute-start | bytes 393224 | tf_op jit(solution)/shard_map/ppermute | solution.py:474
  46.2 5.0 %collective-permute-start.11 = (f32[2,128,128]{2,1,0:T(8,128)S(1)}, f32[2,128,128]{2,1,0:T(8,128)S(1)}, u32[]{:S(2)}, u32[]{:S(2)}) collective-permute-start(f32[2,128,128]{2,1,0:T(8,128)S(1)} %targets.1), channel_id=1, source_target_pairs={{0,16},{4,20},{8,24},{12,28},{16,0},{20,4},{24,8},{28,12},{1,17},{... | collective-permute-start | bytes 393224 | tf_op jit(solution)/shard_map/ppermute | solution.py:474
  46.7 5.0 %collective-permute-start.10 = (f32[2,128,128]{2,1,0:T(8,128)S(1)}, f32[2,128,128]{2,1,0:T(8,128)S(1)}, u32[]{:S(2)}, u32[]{:S(2)}) collective-permute-start(f32[2,128,128]{2,1,0:T(8,128)S(1)} %targets.1), channel_id=1, source_target_pairs={{0,8},{4,12},{8,0},{12,4},{16,24},{20,28},{24,16},{28,20},{1,9},{5... | collective-permute-start | bytes 393224 | tf_op jit(solution)/shard_map/ppermute | solution.py:474
  51.7 8.9 %collective-permute-start.13 = (f32[4,2,128,128]{3,2,1,0:T(8,128)S(1)}, f32[4,2,128,128]{3,2,1,0:T(8,128)S(1)}, u32[]{:S(2)}, u32[]{:S(2)}) collective-permute-start(f32[4,2,128,128]{3,2,1,0:T(8,128)S(1)} %pad_maximum_fusion.1), channel_id=1, source_target_pairs={{0,4},{4,0},{8,12},{12,8},{16,20},{20,16},{24,28},{28,24},{1,5},{5... | collective-permute-start | bytes 1572872 | tf_op jit(solution)/shard_map/ppermute | solution.py:474
  52.0 5.6 %collective-permute-start.16 = (f32[2,64,128]{2,1,0:T(8,128)S(1)}, f32[2,64,128]{2,1,0:T(8,128)S(1)}, u32[]{:S(2)}, u32[]{:S(2)}) collective-permute-start(f32[2,64,128]{2,1,0:T(8,128)S(1)} %products.2), channel_id=1, source_target_pairs={{0,24},{4,28},{8,16},{12,20},{16,8},{20,12},{24,0},{28,4},{1,25},{... | collective-permute-start | bytes 196616 | tf_op jit(solution)/shard_map/ppermute | solution.py:474
  53.6 5.3 %collective-permute-start.15 = (f32[2,64,128]{2,1,0:T(8,128)S(1)}, f32[2,64,128]{2,1,0:T(8,128)S(1)}, u32[]{:S(2)}, u32[]{:S(2)}) collective-permute-start(f32[2,64,128]{2,1,0:T(8,128)S(1)} %products.2), channel_id=1, source_target_pairs={{0,16},{4,20},{8,24},{12,28},{16,0},{20,4},{24,8},{28,12},{1,17},{... | collective-permute-start | bytes 196616 | tf_op jit(solution)/shard_map/ppermute | solution.py:474
  54.5 4.5 %collective-permute-start.14 = (f32[2,64,128]{2,1,0:T(8,128)S(1)}, f32[2,64,128]{2,1,0:T(8,128)S(1)}, u32[]{:S(2)}, u32[]{:S(2)}) collective-permute-start(f32[2,64,128]{2,1,0:T(8,128)S(1)} %products.2), channel_id=1, source_target_pairs={{0,8},{4,12},{8,0},{12,4},{16,24},{20,28},{24,16},{28,20},{1,9},{5... | collective-permute-start | bytes 196616 | tf_op jit(solution)/shard_map/ppermute | solution.py:474
  59.0 1.6 %collective-permute-start.17 = (f32[4,2,64,128]{3,2,1,0:T(8,128)S(1)}, f32[4,2,64,128]{3,2,1,0:T(8,128)S(1)}, u32[]{:S(2)}, u32[]{:S(2)}) collective-permute-start(f32[4,2,64,128]{3,2,1,0:T(8,128)S(1)} %pad_maximum_fusion.2), channel_id=1, source_target_pairs={{0,4},{4,0},{8,12},{12,8},{16,20},{20,16},{24,28},{28,24},{1,5},{5... | collective-permute-start | bytes 786440 | tf_op jit(solution)/shard_map/ppermute | solution.py:474

commit v2 on v1

--- a/solution.py
+++ b/solution.py
@@ -107,8 +107,13 @@
         ref[i - low] = jnp.where(mine, coher_refs[i][0], jnp.zeros_like(coher_refs[i][0]))
 
 
-def fill_table(blocks_ref, table, width):
-    groups, rows, lanes = blocks_ref.shape
+def keep_kernel(one_ref, out_ref):
+    out_ref[...] = one_ref[...]
+
+
+def fill_table(blocks, table, width):
+    rows, lanes = blocks[0].shape[1:]
+    groups = 2 * blocks[0].shape[0]
     part_rows = rows - 8
     per = lanes // width
     lane_of = lax.broadcasted_iota(jnp.int32, (part_rows, lanes), 1) // width
@@ -116,7 +121,8 @@
         for q in range(per):
             tile_rows = jnp.zeros((part_rows, lanes), F32)
             for u in range(per):
-                block = blocks_ref[per * tile + u, :part_rows]
+                j = per * tile + u
+                block = blocks[j % 2][j // 2, :part_rows]
                 shift = ((u - q) * width) % lanes
                 if shift:
                     block = pltpu.roll(block, shift, 1)
@@ -124,24 +130,24 @@
             table[q * part_rows : (q + 1) * part_rows, tile * lanes : (tile + 1) * lanes] = tile_rows
 
 
-def block_stations(blocks_ref, g, tiles, base):
-    part_rows = blocks_ref.shape[1] - 8
-    rows = blocks_ref[g, part_rows:, :].astype(jnp.int32) ^ base
+def block_stations(block, tiles, base):
+    part_rows = block.shape[0] - 8
+    rows = block[part_rows:, :].astype(jnp.int32) ^ base
     return [jnp.concatenate([rows[end * tiles + t : end * tiles + t + 1] for t in range(tiles)], axis=1) for end in (0, 1)]
 
 
-def lookup_kernel(blocks_ref, hots_ref, ends_ref, start_ref, table, *, width, owned):
-    groups = blocks_ref.shape[0]
+def lookup_kernel(near_ref, far_ref, hots_ref, ends_ref, start_ref, table, *, width, owned):
+    groups = hots_ref.shape[0]
     baselines = hots_ref.shape[2] // 2
     tiles = baselines // 128
     base = lax.axis_index("bl").astype(jnp.int32) * width
-    fill_table(blocks_ref, table, width)
+    fill_table([near_ref, far_ref], table, width)
     start = table[owned * 8 : (owned + SOLVED) * 8, :]
     start_ref[...] = start
     split = split_rows(start)
     for g in range(groups):
         half = groups // 2
-        rows_p, rows_q = block_stations(blocks_ref, 2 * (g % half) + g // half, tiles, base)
+        rows_p, rows_q = block_stations((near_ref, far_ref)[g // half].at[g % half], tiles, base)
         hots_ref[g] = one_hot(rows_p, rows_q, groups * width)
         out = jnp.dot(split, hots_ref[g], preferred_element_type=F32)
         out = out[: SOLVED * 8] + out[SOLVED * 8 :]
@@ -152,14 +158,14 @@
                     ends_ref[i, end, chunk : chunk + 8, :] = out[i * 8 : i * 8 + 8, column : column + 128]
 
 
-def model_kernel(blocks_ref, coher_ref, vis_ref, part_ref, begin_ref, table, ends, *, width):
+def model_kernel(near_ref, far_ref, coher_ref, vis_ref, part_ref, begin_ref, table, ends, *, width):
     owned = coher_ref.shape[0]
     baselines = coher_ref.shape[3]
     channels = vis_ref.shape[1]
     lane = lax.axis_index("dir")
     base = lax.axis_index("bl").astype(jnp.int32) * width
-    fill_table(blocks_ref, table, width)
-    rows_p, rows_q = block_stations(blocks_ref, 0, baselines // 128, base)
+    fill_table([near_ref, far_ref], table, width)
+    rows_p, rows_q = block_stations(near_ref.at[0], baselines // 128, base)
     ends[...] = pick(one_hot(rows_p, rows_q, table.shape[1]), table[...])
     begin_ref[...] = ends[owned * 8 : (owned + SOLVED) * 8, :]
 
@@ -266,9 +272,9 @@
     last = high == SOLVED
     hots, begin, start_ref, res_ref, own_ref = refs[:5]
     targets, refs = refs[5:7], refs[7:]
-    products = [refs[2 * g : 2 * g + 2] for g in range(len(GROUPS))]
+    pair, refs = refs[:2], refs[2:]
     ends, values, state, m_now, k_now = refs[-5:]
-    refs = refs[2 * len(GROUPS) : -5]
+    refs = refs[:-5]
     stages = [stage for stage in TARGETS if stage[1] <= low]
     earlier_moved = {m: (refs[s], m - stage[0]) for s, stage in enumerate(stages) for m in range(*stage)}
     refs = refs[len(stages) :]
@@ -314,16 +320,15 @@
         return gram
 
     def prepare(i):
-        [(pair, first, end)] = [(pair, *group) for pair, group in zip(products, GROUPS) if group[0] <= i < group[1]]
         for row in range(K_ROWS):
-            k_now[row] = rows_at(pair, (i - first) * K_ROWS + row)
+            k_now[row] = rows_at(pair, i * K_ROWS + row)
         for w in range(4):
             value = []
             for out in range(4):
                 row = (i - low) * M_ROWS + (out * 4 + w) * 2
                 value.append((rows_at(targets, row), rows_at(targets, row + 1)))
             for m in range(i):
-                base = (end - first) * K_ROWS + pair_list(first, end).index((m, i)) * M_ROWS
+                base = SOLVED * K_ROWS + pair_list(0, SOLVED).index((m, i)) * M_ROWS
                 ref, place = (moved, m - low) if m >= low else earlier_moved[m]
                 for uv in range(4):
                     at = base + (uv * 4 + w) * 2
@@ -474,12 +479,11 @@
     return lax.ppermute(block, axis, [(i, i ^ mask) for i in range(lax.axis_size(axis))])
 
 
-def butterfly_sum(value, axis):
-    mask = 1
-    while mask < lax.axis_size(axis):
-        value = value + exchange(value, axis, mask)
-        mask *= 2
-    return value
+def butterfly_sums(value, axis):
+    sums = [value]
+    while 1 << (len(sums) - 1) < lax.axis_size(axis):
+        sums.append(sums[-1] + exchange(sums[-1], axis, 1 << (len(sums) - 1)))
+    return sums
 
 
 def chip_blocks(block, axis):
@@ -501,17 +505,23 @@
     tiles = baselines // 128
     params = pltpu.CompilerParams(vmem_limit_bytes=VMEM_BYTES)
 
-    def call(kernel, name, shapes, scalars, arrays, scratch=(), **static):
+    def call(kernel, name, shapes, scalars, arrays, scratch=(), after=(), **static):
+        first, skip = len(scalars) + len(arrays), len(after)
+
+        def body(*refs):
+            kernel(*refs[:first], *refs[first + skip :], **static)
+
         return pl.pallas_call(
-            functools.partial(kernel, **static),
+            body,
             out_shape=[jax.ShapeDtypeStruct(*shape) for shape in shapes],
             in_specs=[pl.BlockSpec(memory_space=pltpu.SMEM)] * len(scalars)
-            + [pl.BlockSpec(memory_space=pltpu.VMEM)] * len(arrays),
+            + [pl.BlockSpec(memory_space=pltpu.VMEM)] * len(arrays)
+            + [pl.BlockSpec(memory_space=pl.ANY)] * skip,
             out_specs=[pl.BlockSpec(memory_space=pltpu.VMEM)] * len(shapes),
             scratch_shapes=[pltpu.VMEM(*shape) for shape in scratch],
             compiler_params=params,
             name=name,
-        )(*scalars, *arrays)
+        )(*scalars, *arrays, *after)
 
     per = 128 // width
     part_rows = -(-(owned + SOLVED) // per) * 8
@@ -533,8 +543,8 @@
     )(solve_order, stations, gain_offsets, *[coherencies] * SOLVED)
 
     near = chip_blocks(packed, "bl")
-    blocks = jnp.stack([near, exchange(near, "bl", 1)], axis=1).reshape(groups, part_rows + 8, 128)
-    shared = [butterfly_sum(value, "dir") for value in chosen]
+    blocks = [near, exchange(near, "bl", 1)]
+    shared = [butterfly_sums(value, "dir")[-1] for value in chosen]
 
     table = ((part_rows * per, count), F32)
     part, begin = call(
@@ -542,7 +552,7 @@
         "first_model",
         [((8, channel_count, baselines), F32), ((SOLVED * 8, 2 * baselines), F32)],
         [],
-        [blocks, coherencies, visibilities],
+        blocks + [coherencies, visibilities],
         [table, ((part_rows * per, 2 * baselines), F32)],
         width=width,
     )
@@ -552,12 +562,14 @@
         "lookup",
         [((groups, count, 2 * baselines), BF16), ((SOLVED, 2, chunks * 8, 128), F32), ((SOLVED * 8, count), F32)],
         [],
-        [blocks],
+        blocks,
         [table],
         width=width,
         owned=owned,
+        after=[part],
     )
-    first = butterfly_sum(part, "dir")
+    partials = butterfly_sums(part, "dir")
+    first = partials[-1]
     res, own = call(
         own_kernel,
         "own_channels",
@@ -567,13 +579,11 @@
     )
     moved, solved = [], []
     flat = lambda near: [near.reshape(-1, 128), exchange(near, "bl", 1).reshape(-1, 128)]
-    products = []
-    for g, (low, high) in enumerate(GROUPS):
-        rows = (high - low) * K_ROWS + len(pair_list(low, high)) * M_ROWS
-        [value] = call(
-            product_kernel, "products", [((tiles, rows, 128), F32)], [], shared[: g + 1], low=low, high=high
-        )
-        products += flat(chip_blocks(value, "bl"))
+    rows = SOLVED * K_ROWS + len(pair_list(0, SOLVED)) * M_ROWS
+    [value] = call(
+        product_kernel, "products", [((tiles, rows, 128), F32)], [], shared, after=[part], low=0, high=SOLVED
+    )
+    kx_near = chip_blocks(value, "bl")
     for low, high in TARGETS:
         [value] = call(
             target_kernel,
@@ -583,7 +593,10 @@
             [first, begin] + shared,
             low=low,
             high=high,
+            after=[value],
         )
+        [kx_near] = call(keep_kernel, "keep", [(kx_near.shape, F32)], [], [kx_near], after=[value])
+        products = flat(kx_near)
         targets = flat(chip_blocks(value, "bl"))
         last = high == SOLVED
         moved_shape = ((high - low, M_ROWS, chunks, 128), F32)

time: 76 us -> 68.3 us (0.90); the launches traced: 75.7 us -> 68.9 us
  waiting for transfers between devices: 26.1 us -> 19.8 us
  starting transfers between devices: 24.2 us -> 19.9 us
  Pallas kernels: 21.6 us -> 23.7 us
  local copies, waits for them, and re-layouts: 0.05 us -> 1.82 us
    ppermute x22 -> x18, waiting for transfers between devices: 26.1 us -> 19.8 us  [exchange(): lax.ppermute(block, axis, [(i, i ^ mask) for i in range(lax.axis_size(axi...]
    ppermute x22 -> x18, starting transfers between devices: 24.2 us -> 19.9 us  [exchange(): lax.ppermute(block, axis, [(i, i ^ mask) for i in range(lax.axis_size(axi...]
    pallas_call x7, Pallas kernels: 19.1 us -> 21.3 us  [call(): pl.pallas_call(body, out_shape=[jax.ShapeDtypeStruct(*shape) for shape in...]
    unnamed x12, local copies, waits for them, and re-layouts: 0.03 us -> 1.82 us
    another operation x2 -> x0, other arithmetic: 0.78 us -> none  [on_device(): jnp.stack([near, exchange(near, 'bl', 1)], axis=1)]
    another operation x3, other arithmetic: 0.11 us -> 0.87 us  [chip_blocks(): jnp.stack([block] + [exchange(block, axis, 2 * j) for j in range(1, chips)])]
  transfers between devices with their start and end apart: 22 -> 18, of which waited for: 12 -> 10; matrix products, arithmetic and copies ran while one was open for 4% -> 4% of each run, Pallas kernels for 5% -> 6%
where the time goes in v2:
time: 68.3 us; the launch traced here: 68.9 us
  Pallas kernels  23.7 us (35%)
  starting transfers between devices  19.9 us (29%)
  waiting for transfers between devices  19.8 us (29%)
  other arithmetic  2.86 us (4%)
  local copies, waits for them, and re-layouts  1.82 us (3%)
  between operations  0.79 us (1%)
    pallas_call x7, Pallas kernels, call(): pl.pallas_call(body, out_shape=[jax.ShapeDtypeStruct(*shape) for shape in...  21.3 us
    ppermute x18, starting transfers between devices, exchange(): lax.ppermute(block, axis, [(i, i ^ mask) for i in range(lax.axis_size(axi...  19.9 us
    ppermute x18, waiting for transfers between devices, exchange(): lax.ppermute(block, axis, [(i, i ^ mask) for i in range(lax.axis_size(axi...  19.8 us
    pallas_call x1, Pallas kernels, on_device(): pl.pallas_call(functools.partial(prep_kernel, owned=owned, per=per), out_...  2.41 us
    add x6, other arithmetic, butterfly_sums(): sums.append(sums[-1] + exchange(sums[-1], axis, 1 << len(sums) - 1))  1.99 us
    unnamed x12, local copies, waits for them, and re-layouts  1.82 us
  transfers between devices with their start and end apart: 18, of which 10 were waited for; matrix products, arithmetic and copies ran while one was open for 4% of the time, Pallas kernels for 6%

profile of v2, /device:TPU:0, one launch (start us, length us, event | category | flops | bytes accessed | tf_op | source)
XLA Modules:
  0.0 68.9 jit_solution(9591776604675926006)
XLA Ops:
  0.6 2.4 %prepare.1 = (f32[56,128]{1,0:T(8,128)}, bf16[2,8,16,256]{3,2,1,0:T(8,128)(2,1)}, bf16[2,8,16,256]{3,2,1,0:T(8,128)(2,1)}) custom-call(s32[32]{0:T(128)} %refs_0_.3, s32[2,256]{1,0:T(2,128)} %stations_ref.1, f32[32,8,64]{2,1,0:T(8,128)} %refs_12_.1, bf16[8,8,16,256]{3,2,1,0:T(8,128)(2,1)} %refs_2_.4, bf16[8,8,16,256]{3,2,1,0:T(8,128)(2,1)} %refs_2_.4, ...), custom_call_target="tpu_custom_call" | custom-call | tf_op jit(solution)/shard_map/prepare/pallas_call | solution.py:532
  3.0 3.0 %collective-permute-start.6 = (bf16[2,8,16,256]{3,2,1,0:T(8,128)(2,1)}, bf16[2,8,16,256]{3,2,1,0:T(8,128)(2,1)S(1)}, u32[]{:S(2)}, u32[]{:S(2)}) collective-permute-start(bf16[2,8,16,256]{3,2,1,0:T(8,128)(2,1)} %get-tuple-element.17), channel_id=1, source_target_pairs={{0,1},{1,0},{2,3},{3,2},{4,5},{5,4},{6,7},{7,6},{8,9},{9,8},{10,11... | collective-permute-start | bytes 393224 | tf_op jit(solution)/shard_map/ppermute | solution.py:479
  6.1 2.9 %collective-permute-start.2 = (f32[56,128]{1,0:T(8,128)}, f32[56,128]{1,0:T(8,128)S(1)}, u32[]{:S(2)}, u32[]{:S(2)}) collective-permute-start(f32[56,128]{1,0:T(8,128)} %get-tuple-element.12), channel_id=1, source_target_pairs={{0,24},{4,28},{8,16},{12,20},{16,8},{20,12},{24,0},{28,4},{1,25},{... | collective-permute-start | bytes 86024 | tf_op jit(solution)/shard_map/ppermute | solution.py:479
  9.0 0.5 collective-permute-start.1
  9.6 1.0 %collective-permute-done.6 = bf16[2,8,16,256]{3,2,1,0:T(8,128)(2,1)S(1)} collective-permute-done((bf16[2,8,16,256]{3,2,1,0:T(8,128)(2,1)}, bf16[2,8,16,256]{3,2,1,0:T(8,128)(2,1)S(1)}, u32[]{:S(2)}, u32[]{:S(2)}) %collective-permute-start.6) | collective-permute-done | bytes 131104 | tf_op jit(solution)/shard_map/ppermute | solution.py:479
  10.6 0.9 %add.20 = bf16[2,8,16,256]{3,2,1,0:T(8,128)(2,1)S(1)} add(bf16[2,8,16,256]{3,2,1,0:T(8,128)(2,1)} %get-tuple-element.17, bf16[2,8,16,256]{3,2,1,0:T(8,128)(2,1)S(1)} %collective-permute-done.6) | non-fusion elementwise | flops 65536 | bytes 393216 | tf_op jit(solution)/shard_map/add | solution.py:485
  11.5 3.1 %collective-permute-start.7 = (bf16[2,8,16,256]{3,2,1,0:T(8,128)(2,1)S(1)}, bf16[2,8,16,256]{3,2,1,0:T(8,128)(2,1)S(1)}, u32[]{:S(2)}, u32[]{:S(2)}) collective-permute-start(bf16[2,8,16,256]{3,2,1,0:T(8,128)(2,1)S(1)} %add.20), channel_id=1, source_target_pairs={{0,2},{1,3},{2,0},{3,1},{4,6},{5,7},{6,4},{7,5},{8,10},{9,11},{10,... | collective-permute-start | bytes 393224 | tf_op jit(solution)/shard_map/ppermute | solution.py:479
  14.7 0.9 %add.22 = bf16[2,8,16,256]{3,2,1,0:T(8,128)(2,1)S(1)} add(bf16[2,8,16,256]{3,2,1,0:T(8,128)(2,1)} %get-tuple-element.18, bf16[2,8,16,256]{3,2,1,0:T(8,128)(2,1)S(1)} %collective-permute-done.8) | non-fusion elementwise | flops 65536 | bytes 393216 | tf_op jit(solution)/shard_map/add | solution.py:485
  15.6 1.0 %collective-permute-start.9 = (bf16[2,8,16,256]{3,2,1,0:T(8,128)(2,1)S(1)}, bf16[2,8,16,256]{3,2,1,0:T(8,128)(2,1)S(1)}, u32[]{:S(2)}, u32[]{:S(2)}) collective-permute-start(bf16[2,8,16,256]{3,2,1,0:T(8,128)(2,1)S(1)} %add.22), channel_id=1, source_target_pairs={{0,2},{1,3},{2,0},{3,1},{4,6},{5,7},{6,4},{7,5},{8,10},{9,11},{10,... | collective-permute-start | bytes 393224 | tf_op jit(solution)/shard_map/ppermute | solution.py:479
  16.6 0.8 %pad_maximum_fusion.2.refs_0_ = f32[4,56,128]{2,1,0:T(8,128)S(1)} fusion(f32[1,56,128]{2,1,0:T(8,128)S(1)} %bitcast.29, f32[1,56,128]{2,1,0:T(8,128)S(1)} %bitcast.30, f32[1,56,128]{2,1,0:T(8,128)S(1)} %bitcast.31, f32[1,56,128]{2,1,0:T(8,128)} %bitcast.28), kind=kLoop, calls=%fused_computation.2 | loop fusion | flops 86016 | bytes 229376 | tf_op jit(solution)/shard_map/stack | solution.py:492
  17.5 1.3 %collective-permute-done.3.refs_1_ = f32[4,56,128]{2,1,0:T(8,128)S(1)} collective-permute-done((f32[4,56,128]{2,1,0:T(8,128)S(1)}, f32[4,56,128]{2,1,0:T(8,128)S(1)}, u32[]{:S(2)}, u32[]{:S(2)}) %collective-permute-start.3) | collective-permute-done | bytes 114720 | tf_op jit(solution)/shard_map/ppermute | solution.py:479
  18.8 1.0 %copy-done = bf16[8,8,16,256]{3,2,1,0:T(8,128)(2,1)S(1)} copy-done((bf16[8,8,16,256]{3,2,1,0:T(8,128)(2,1)S(1)}, bf16[8,8,16,256]{3,2,1,0:T(8,128)(2,1)}, u32[]{:S(2)}) %copy-start) | copy-done | bytes 524312
  19.8 0.8 %copy-done.2 = f32[8,4,256]{2,1,0:T(4,128)S(1)} copy-done((f32[8,4,256]{2,1,0:T(4,128)S(1)}, f32[8,4,256]{2,1,0:T(4,128)}, u32[]{:S(2)}) %copy-start.2) | copy-done | bytes 32792
  20.6 1.0 %first_model.1 = (f32[8,16,256]{2,1,0:T(8,128)S(1)}, f32[32,512]{1,0:T(8,128)S(1)}) custom-call(f32[4,56,128]{2,1,0:T(8,128)S(1)} %pad_maximum_fusion.2.refs_0_, f32[4,56,128]{2,1,0:T(8,128)S(1)} %collective-permute-done.3.refs_1_, bf16[8,8,16,256]{3,2,1,0:T(8,128)(2,1)S(1)} %copy-done, f32[8,4,256]{2,1,0:T(4,128)S(1)} %copy-done.2), custom_call_target="tpu_custom_call" | custom-call | tf_op jit(solution)/shard_map/first_model/pallas_call | solution.py:514
  21.6 1.3 %collective-permute-start.4 = (f32[8,16,256]{2,1,0:T(8,128)S(1)}, f32[8,16,256]{2,1,0:T(8,128)S(1)}, u32[]{:S(2)}, u32[]{:S(2)}) collective-permute-start(f32[8,16,256]{2,1,0:T(8,128)S(1)} %get-tuple-element.13.refs_2_), channel_id=1, source_target_pairs={{0,1},{1,0},{2,3},{3,2},{4,5},{5,4},{6,7},{7,6},{8,9},{9,8},{10,11... | collective-permute-start | bytes 393224 | tf_op jit(solution)/shard_map/ppermute | solution.py:479
  23.1 1.7 %collective-permute-done.9 = bf16[2,8,16,256]{3,2,1,0:T(8,128)(2,1)S(1)} collective-permute-done((bf16[2,8,16,256]{3,2,1,0:T(8,128)(2,1)S(1)}, bf16[2,8,16,256]{3,2,1,0:T(8,128)(2,1)S(1)}, u32[]{:S(2)}, u32[]{:S(2)}) %collective-permute-start.9) | collective-permute-done | bytes 131104 | tf_op jit(solution)/shard_map/ppermute | solution.py:479
  24.9 0.9 %products.1.refs_4_ = f32[2,256,128]{2,1,0:T(8,128)S(1)} custom-call(bf16[2,8,16,256]{3,2,1,0:T(8,128)(2,1)S(1)} %add.21.refs_1_.refs_0_.refs_2_, bf16[2,8,16,256]{3,2,1,0:T(8,128)(2,1)S(1)} %add.23.refs_2_.refs_1_.refs_3_, f32[8,16,256]{2,1,0:T(8,128)S(1)} %get-tuple-element.13.refs_2_), custom_call_target="tpu_custom_call" | custom-call | tf_op jit(solution)/shard_map/products/pallas_call | solution.py:514
  25.9 2.7 %collective-permute-start.16 = (f32[2,256,128]{2,1,0:T(8,128)S(1)}, f32[2,256,128]{2,1,0:T(8,128)S(1)}, u32[]{:S(2)}, u32[]{:S(2)}) collective-permute-start(f32[2,256,128]{2,1,0:T(8,128)S(1)} %products.1.refs_4_), channel_id=1, source_target_pairs={{0,24},{4,28},{8,16},{12,20},{16,8},{20,12},{24,0},{28,4},{1,25},{... | collective-permute-start | bytes 786440 | tf_op jit(solution)/shard_map/ppermute | solution.py:479
  28.6 0.5 collective-permute-start.15
  29.1 0.3 collective-permute-start.14
  29.4 0.5 collective-permute-start.5
  29.9 6.8 %collective-permute-done.5 = f32[8,16,256]{2,1,0:T(8,128)S(1)} collective-permute-done((f32[8,16,256]{2,1,0:T(8,128)S(1)}, f32[8,16,256]{2,1,0:T(8,128)S(1)}, u32[]{:S(2)}, u32[]{:S(2)}) %collective-permute-start.5) | collective-permute-done | bytes 131104 | tf_op jit(solution)/shard_map/ppermute | solution.py:479
  36.8 0.7 %targets.1.refs_1_ = f32[2,128,128]{2,1,0:T(8,128)S(1)} custom-call(f32[8,16,256]{2,1,0:T(8,128)S(1)} %add.19.refs_0_, f32[32,512]{1,0:T(8,128)S(1)} %get-tuple-element.21.refs_1_, bf16[2,8,16,256]{3,2,1,0:T(8,128)(2,1)S(1)} %add.21.refs_1_.refs_0_.refs_2_, bf16[2,8,16,256]{3,2,1,0:T(8,128)(2,1)S(1)} %add.23.refs_2_.refs_1_.refs_3_, ...), custom_call_target="tpu_custom_call" | custom-call | tf_op jit(solution)/shard_map/targets/pallas_call | solution.py:514
  37.5 2.1 %collective-permute-done.15 = f32[2,256,128]{2,1,0:T(8,128)S(1)} collective-permute-done((f32[2,256,128]{2,1,0:T(8,128)S(1)}, f32[2,256,128]{2,1,0:T(8,128)S(1)}, u32[]{:S(2)}, u32[]{:S(2)}) %collective-permute-start.15) | collective-permute-done | bytes 262176 | tf_op jit(solution)/shard_map/ppermute | solution.py:479
  40.0 1.6 %collective-permute-start.12 = (f32[2,128,128]{2,1,0:T(8,128)S(1)}, f32[2,128,128]{2,1,0:T(8,128)S(1)}, u32[]{:S(2)}, u32[]{:S(2)}) collective-permute-start(f32[2,128,128]{2,1,0:T(8,128)S(1)} %targets.1.refs_1_), channel_id=1, source_target_pairs={{0,24},{4,28},{8,16},{12,20},{16,8},{20,12},{24,0},{28,4},{1,25},{... | collective-permute-start | bytes 393224 | tf_op jit(solution)/shard_map/ppermute | solution.py:479
  41.7 1.4 %collective-permute-start.11 = (f32[2,128,128]{2,1,0:T(8,128)S(1)}, f32[2,128,128]{2,1,0:T(8,128)S(1)}, u32[]{:S(2)}, u32[]{:S(2)}) collective-permute-start(f32[2,128,128]{2,1,0:T(8,128)S(1)} %targets.1.refs_1_), channel_id=1, source_target_pairs={{0,16},{4,20},{8,24},{12,28},{16,0},{20,4},{24,8},{28,12},{1,17},{... | collective-permute-start | bytes 393224 | tf_op jit(solution)/shard_map/ppermute | solution.py:479
  43.0 0.5 collective-permute-start.10
  43.6 3.8 %collective-permute-done.12 = f32[2,128,128]{2,1,0:T(8,128)S(1)} collective-permute-done((f32[2,128,128]{2,1,0:T(8,128)S(1)}, f32[2,128,128]{2,1,0:T(8,128)S(1)}, u32[]{:S(2)}, u32[]{:S(2)}) %collective-permute-start.12) | collective-permute-done | bytes 131104 | tf_op jit(solution)/shard_map/ppermute | solution.py:479
  47.3 2.3 %collective-permute-done.11 = f32[2,128,128]{2,1,0:T(8,128)S(1)} collective-permute-done((f32[2,128,128]{2,1,0:T(8,128)S(1)}, f32[2,128,128]{2,1,0:T(8,128)S(1)}, u32[]{:S(2)}, u32[]{:S(2)}) %collective-permute-start.11) | collective-permute-done | bytes 131104 | tf_op jit(solution)/shard_map/ppermute | solution.py:479
  49.8 1.3 %lookup.1 = (bf16[8,512,512]{2,1,0:T(8,128)(2,1)S(1)}, f32[4,2,128,128]{3,2,1,0:T(8,128)S(1)}, f32[32,512]{1,0:T(8,128)S(1)}) custom-call(f32[4,56,128]{2,1,0:T(8,128)S(1)} %pad_maximum_fusion.2.refs_0_, f32[4,56,128]{2,1,0:T(8,128)S(1)} %collective-permute-done.3.refs_1_, f32[8,16,256]{2,1,0:T(8,128)S(1)} %get-tuple-element.13.refs_2_), custom_call_target="tpu_custom_call" | custom-call | tf_op jit(solution)/shard_map/lookup/pallas_call | solution.py:514
  51.2 0.5 collective-permute-done.13
  51.7 17.2 %sweep.1 = (f32[32,8,64]{2,1,0:T(8,128)}, f32[8,4,256]{2,1,0:T(4,128)}) custom-call(s32[32]{0:T(128)S(1)} %copy-done.3, s32[32]{0:T(128)S(1)} %copy-done.4, s32[32]{0:T(128)S(1)} %copy-done.5, bf16[8,512,512]{2,1,0:T(8,128)(2,1)S(1)} %get-tuple-element.14.refs_3_, f32[4,2,128,128]{3,2,1,0:T(8,128)S(1)} %get-tuple-element.15.refs_4_, ...), custom_call_target="tpu_custom_call" | custom-call | tf_op jit(solution)/shard_map/sweep/pallas_call | solution.py:514
  (33 shorter events, 1.2 us)
Async XLA Ops:
  3.0 7.6 %collective-permute-start.6 = (bf16[2,8,16,256]{3,2,1,0:T(8,128)(2,1)}, bf16[2,8,16,256]{3,2,1,0:T(8,128)(2,1)S(1)}, u32[]{:S(2)}, u32[]{:S(2)}) collective-permute-start(bf16[2,8,16,256]{3,2,1,0:T(8,128)(2,1)} %get-tuple-element.17), channel_id=1, source_target_pairs={{0,1},{1,0},{2,3},{3,2},{4,5},{5,4},{6,7},{7,6},{8,9},{9,8},{10,11... | collective-permute-start | bytes 393224 | tf_op jit(solution)/shard_map/ppermute | solution.py:479
  6.1 8.6 %collective-permute-start.8 = (bf16[2,8,16,256]{3,2,1,0:T(8,128)(2,1)}, bf16[2,8,16,256]{3,2,1,0:T(8,128)(2,1)S(1)}, u32[]{:S(2)}, u32[]{:S(2)}) collective-permute-start(bf16[2,8,16,256]{3,2,1,0:T(8,128)(2,1)} %get-tuple-element.18), channel_id=1, source_target_pairs={{0,1},{1,0},{2,3},{3,2},{4,5},{5,4},{6,7},{7,6},{8,9},{9,8},{10,11... | collective-permute-start | bytes 393224 | tf_op jit(solution)/shard_map/ppermute | solution.py:479
  6.1 10.5 %collective-permute-start.2 = (f32[56,128]{1,0:T(8,128)}, f32[56,128]{1,0:T(8,128)S(1)}, u32[]{:S(2)}, u32[]{:S(2)}) collective-permute-start(f32[56,128]{1,0:T(8,128)} %get-tuple-element.12), channel_id=1, source_target_pairs={{0,24},{4,28},{8,16},{12,20},{16,8},{20,12},{24,0},{28,4},{1,25},{... | collective-permute-start | bytes 86024 | tf_op jit(solution)/shard_map/ppermute | solution.py:479
  9.0 7.7 %collective-permute-start.1 = (f32[56,128]{1,0:T(8,128)}, f32[56,128]{1,0:T(8,128)S(1)}, u32[]{:S(2)}, u32[]{:S(2)}) collective-permute-start(f32[56,128]{1,0:T(8,128)} %get-tuple-element.12), channel_id=1, source_target_pairs={{0,16},{4,20},{8,24},{12,28},{16,0},{20,4},{24,8},{28,12},{1,17},{... | collective-permute-start | bytes 86024 | tf_op jit(solution)/shard_map/ppermute | solution.py:479
  9.5 7.2 %collective-permute-start = (f32[56,128]{1,0:T(8,128)}, f32[56,128]{1,0:T(8,128)S(1)}, u32[]{:S(2)}, u32[]{:S(2)}) collective-permute-start(f32[56,128]{1,0:T(8,128)} %get-tuple-element.12), channel_id=1, source_target_pairs={{0,8},{4,12},{8,0},{12,4},{16,24},{20,28},{24,16},{28,20},{1,9},{5... | collective-permute-start | bytes 86024 | tf_op jit(solution)/shard_map/ppermute | solution.py:479
  11.5 11.6 %collective-permute-start.7 = (bf16[2,8,16,256]{3,2,1,0:T(8,128)(2,1)S(1)}, bf16[2,8,16,256]{3,2,1,0:T(8,128)(2,1)S(1)}, u32[]{:S(2)}, u32[]{:S(2)}) collective-permute-start(bf16[2,8,16,256]{3,2,1,0:T(8,128)(2,1)S(1)} %add.20), channel_id=1, source_target_pairs={{0,2},{1,3},{2,0},{3,1},{4,6},{5,7},{6,4},{7,5},{8,10},{9,11},{10,... | collective-permute-start | bytes 393224 | tf_op jit(solution)/shard_map/ppermute | solution.py:479
  15.6 9.2 %collective-permute-start.9 = (bf16[2,8,16,256]{3,2,1,0:T(8,128)(2,1)S(1)}, bf16[2,8,16,256]{3,2,1,0:T(8,128)(2,1)S(1)}, u32[]{:S(2)}, u32[]{:S(2)}) collective-permute-start(bf16[2,8,16,256]{3,2,1,0:T(8,128)(2,1)S(1)} %add.22), channel_id=1, source_target_pairs={{0,2},{1,3},{2,0},{3,1},{4,6},{5,7},{6,4},{7,5},{8,10},{9,11},{10,... | collective-permute-start | bytes 393224 | tf_op jit(solution)/shard_map/ppermute | solution.py:479
  17.4 1.4 %collective-permute-start.3 = (f32[4,56,128]{2,1,0:T(8,128)S(1)}, f32[4,56,128]{2,1,0:T(8,128)S(1)}, u32[]{:S(2)}, u32[]{:S(2)}) collective-permute-start(f32[4,56,128]{2,1,0:T(8,128)S(1)} %pad_maximum_fusion.2.refs_0_), channel_id=1, source_target_pairs={{0,4},{4,0},{8,12},{12,8},{16,20},{20,16},{24,28},{28,24},{1,5},{5... | collective-permute-start | bytes 344072 | tf_op jit(solution)/shard_map/ppermute | solution.py:479
  18.8 1.0 %copy-start = (bf16[8,8,16,256]{3,2,1,0:T(8,128)(2,1)S(1)}, bf16[8,8,16,256]{3,2,1,0:T(8,128)(2,1)}, u32[]{:S(2)}) copy-start(bf16[8,8,16,256]{3,2,1,0:T(8,128)(2,1)} %refs_2_.4) | copy-start | bytes 1572868
  19.8 0.8 %copy-start.2 = (f32[8,4,256]{2,1,0:T(4,128)S(1)}, f32[8,4,256]{2,1,0:T(4,128)}, u32[]{:S(2)}) copy-start(f32[8,4,256]{2,1,0:T(4,128)} %refs_3_.3) | copy-start | bytes 98308
  21.6 7.8 %collective-permute-start.4 = (f32[8,16,256]{2,1,0:T(8,128)S(1)}, f32[8,16,256]{2,1,0:T(8,128)S(1)}, u32[]{:S(2)}, u32[]{:S(2)}) collective-permute-start(f32[8,16,256]{2,1,0:T(8,128)S(1)} %get-tuple-element.13.refs_2_), channel_id=1, source_target_pairs={{0,1},{1,0},{2,3},{3,2},{4,5},{5,4},{6,7},{7,6},{8,9},{9,8},{10,11... | collective-permute-start | bytes 393224 | tf_op jit(solution)/shard_map/ppermute | solution.py:479
  24.9 26.8 %copy-start.1 = (f32[32,8,64]{2,1,0:T(8,128)S(1)}, f32[32,8,64]{2,1,0:T(8,128)}, u32[]{:S(2)}) copy-start(f32[32,8,64]{2,1,0:T(8,128)} %refs_12_.1) | copy-start | bytes 196612
  24.9 26.8 %copy-start.3 = (s32[32]{0:T(128)S(1)}, s32[32]{0:T(128)}, u32[]{:S(2)}) copy-start(s32[32]{0:T(128)} %refs_0_.3) | copy-start | bytes 388
  24.9 26.8 %copy-start.4 = (s32[32]{0:T(128)S(1)}, s32[32]{0:T(128)}, u32[]{:S(2)}) copy-start(s32[32]{0:T(128)} %refs_1_.3) | copy-start | bytes 388
  24.9 26.8 %copy-start.5 = (s32[32]{0:T(128)S(1)}, s32[32]{0:T(128)}, u32[]{:S(2)}) copy-start(s32[32]{0:T(128)} %refs_2_.5) | copy-start | bytes 388
  25.9 11.7 %collective-permute-start.16 = (f32[2,256,128]{2,1,0:T(8,128)S(1)}, f32[2,256,128]{2,1,0:T(8,128)S(1)}, u32[]{:S(2)}, u32[]{:S(2)}) collective-permute-start(f32[2,256,128]{2,1,0:T(8,128)S(1)} %products.1.refs_4_), channel_id=1, source_target_pairs={{0,24},{4,28},{8,16},{12,20},{16,8},{20,12},{24,0},{28,4},{1,25},{... | collective-permute-start | bytes 786440 | tf_op jit(solution)/shard_map/ppermute | solution.py:479
  28.6 11.0 %collective-permute-start.15 = (f32[2,256,128]{2,1,0:T(8,128)S(1)}, f32[2,256,128]{2,1,0:T(8,128)S(1)}, u32[]{:S(2)}, u32[]{:S(2)}) collective-permute-start(f32[2,256,128]{2,1,0:T(8,128)S(1)} %products.1.refs_4_), channel_id=1, source_target_pairs={{0,16},{4,20},{8,24},{12,28},{16,0},{20,4},{24,8},{28,12},{1,17},{... | collective-permute-start | bytes 786440 | tf_op jit(solution)/shard_map/ppermute | solution.py:479
  29.1 10.7 %collective-permute-start.14 = (f32[2,256,128]{2,1,0:T(8,128)S(1)}, f32[2,256,128]{2,1,0:T(8,128)S(1)}, u32[]{:S(2)}, u32[]{:S(2)}) collective-permute-start(f32[2,256,128]{2,1,0:T(8,128)S(1)} %products.1.refs_4_), channel_id=1, source_target_pairs={{0,8},{4,12},{8,0},{12,4},{16,24},{20,28},{24,16},{28,20},{1,9},{5... | collective-permute-start | bytes 786440 | tf_op jit(solution)/shard_map/ppermute | solution.py:479
  29.4 7.3 %collective-permute-start.5 = (f32[8,16,256]{2,1,0:T(8,128)S(1)}, f32[8,16,256]{2,1,0:T(8,128)S(1)}, u32[]{:S(2)}, u32[]{:S(2)}) collective-permute-start(f32[8,16,256]{2,1,0:T(8,128)S(1)} %add.18), channel_id=1, source_target_pairs={{0,2},{1,3},{2,0},{3,1},{4,6},{5,7},{6,4},{7,5},{8,10},{9,11},{10,... | collective-permute-start | bytes 393224 | tf_op jit(solution)/shard_map/ppermute | solution.py:479
  39.9 11.7 %collective-permute-start.17 = (f32[4,2,256,128]{3,2,1,0:T(8,128)S(1)}, f32[4,2,256,128]{3,2,1,0:T(8,128)S(1)}, u32[]{:S(2)}, u32[]{:S(2)}) collective-permute-start(f32[4,2,256,128]{3,2,1,0:T(8,128)S(1)} %keep.1), channel_id=1, source_target_pairs={{0,4},{4,0},{8,12},{12,8},{16,20},{20,16},{24,28},{28,24},{1,5},{5... | collective-permute-start | bytes 3145736 | tf_op jit(solution)/shard_map/ppermute | solution.py:479
  40.0 7.3 %collective-permute-start.12 = (f32[2,128,128]{2,1,0:T(8,128)S(1)}, f32[2,128,128]{2,1,0:T(8,128)S(1)}, u32[]{:S(2)}, u32[]{:S(2)}) collective-permute-start(f32[2,128,128]{2,1,0:T(8,128)S(1)} %targets.1.refs_1_), channel_id=1, source_target_pairs={{0,24},{4,28},{8,16},{12,20},{16,8},{20,12},{24,0},{28,4},{1,25},{... | collective-permute-start | bytes 393224 | tf_op jit(solution)/shard_map/ppermute | solution.py:479
  41.7 8.0 %collective-permute-start.11 = (f32[2,128,128]{2,1,0:T(8,128)S(1)}, f32[2,128,128]{2,1,0:T(8,128)S(1)}, u32[]{:S(2)}, u32[]{:S(2)}) collective-permute-start(f32[2,128,128]{2,1,0:T(8,128)S(1)} %targets.1.refs_1_), channel_id=1, source_target_pairs={{0,16},{4,20},{8,24},{12,28},{16,0},{20,4},{24,8},{28,12},{1,17},{... | collective-permute-start | bytes 393224 | tf_op jit(solution)/shard_map/ppermute | solution.py:479
  43.0 6.6 %collective-permute-start.10 = (f32[2,128,128]{2,1,0:T(8,128)S(1)}, f32[2,128,128]{2,1,0:T(8,128)S(1)}, u32[]{:S(2)}, u32[]{:S(2)}) collective-permute-start(f32[2,128,128]{2,1,0:T(8,128)S(1)} %targets.1.refs_1_), channel_id=1, source_target_pairs={{0,8},{4,12},{8,0},{12,4},{16,24},{20,28},{24,16},{28,20},{1,9},{5... | collective-permute-start | bytes 393224 | tf_op jit(solution)/shard_map/ppermute | solution.py:479
  49.7 2.0 %collective-permute-start.13 = (f32[4,2,128,128]{3,2,1,0:T(8,128)S(1)}, f32[4,2,128,128]{3,2,1,0:T(8,128)S(1)}, u32[]{:S(2)}, u32[]{:S(2)}) collective-permute-start(f32[4,2,128,128]{3,2,1,0:T(8,128)S(1)} %pad_maximum_fusion.1), channel_id=1, source_target_pairs={{0,4},{4,0},{8,12},{12,8},{16,20},{20,16},{24,28},{28,24},{1,5},{5... | collective-permute-start | bytes 1572872 | tf_op jit(solution)/shard_map/ppermute | solution.py:479

commit v3 on v2

--- a/solution.py
+++ b/solution.py
@@ -136,26 +136,42 @@
     return [jnp.concatenate([rows[end * tiles + t : end * tiles + t + 1] for t in range(tiles)], axis=1) for end in (0, 1)]
 
 
-def lookup_kernel(near_ref, far_ref, hots_ref, ends_ref, start_ref, table, *, width, owned):
-    groups = hots_ref.shape[0]
-    baselines = hots_ref.shape[2] // 2
-    tiles = baselines // 128
+def fetch_columns(rows, hots, part, at):
+    count = rows.shape[0]
+    parts = rows.shape[1] // 128
+    wide = jnp.concatenate([rows[:, w * 128 : w * 128 + 128] for w in range(parts)], axis=0)
+    out = jnp.dot(split_rows(wide), hots[:, at], preferred_element_type=F32)
+    out = out[: parts * count] + out[parts * count :]
+    which = jnp.concatenate([part[:, at]] * (count // 8), axis=0)
+    value = out[:count]
+    for w in range(1, parts):
+        value = jnp.where(which == w, out[w * count : w * count + count], value)
+    return value
+
+
+def lookup_kernel(near_ref, far_ref, hots_ref, turned_ref, part_ref, ends_ref, start_ref, table, *, width, owned, tiles):
+    half = near_ref.shape[0]
+    chunks = 2 * half * tiles
     base = lax.axis_index("bl").astype(jnp.int32) * width
     fill_table([near_ref, far_ref], table, width)
     start = table[owned * 8 : (owned + SOLVED) * 8, :]
     start_ref[...] = start
-    split = split_rows(start)
-    for g in range(groups):
-        half = groups // 2
-        rows_p, rows_q = block_stations((near_ref, far_ref)[g // half].at[g % half], tiles, base)
-        hots_ref[g] = one_hot(rows_p, rows_q, groups * width)
-        out = jnp.dot(split, hots_ref[g], preferred_element_type=F32)
-        out = out[: SOLVED * 8] + out[SOLVED * 8 :]
-        for i in range(SOLVED):
-            for end in (0, 1):
-                for t in range(tiles):
-                    chunk, column = (g * tiles + t) * 8, (end * tiles + t) * 128
-                    ends_ref[i, end, chunk : chunk + 8, :] = out[i * 8 : i * 8 + 8, column : column + 128]
+    pairs = [block_stations(ref.at[j], tiles, base) for ref in (near_ref, far_ref) for j in range(half)]
+    step = min(8, chunks)
+    for end in (0, 1):
+        rows = jnp.concatenate([pair[end] for pair in pairs], axis=1)
+        for first in range(0, chunks, step):
+            at = pl.ds((end * chunks + first) * 128, step * 128)
+            here = rows[:, first * 128 : (first + step) * 128]
+            index = lax.broadcasted_iota(jnp.int32, (128, step * 128), 0)
+            hot = jnp.where(index == (here & 127), 1.0, 0.0)
+            hots_ref[:, at] = hot.astype(BF16)
+            turned_ref[at, :] = jnp.transpose(hot).astype(BF16)
+            part_ref[:, at] = jnp.broadcast_to(here >> 7, (8, step * 128))
+            out = fetch_columns(start, hots_ref, part_ref, at)
+            for i in range(SOLVED):
+                for t in range(step):
+                    ends_ref[i, end, (first + t) * 8 : (first + t) * 8 + 8, :] = out[i * 8 : i * 8 + 8, t * 128 : t * 128 + 128]
 
 
 def model_kernel(near_ref, far_ref, coher_ref, vis_ref, part_ref, begin_ref, table, ends, *, width):
@@ -250,9 +266,11 @@
                     out += 2
 
 
-def own_kernel(first_ref, *refs):
-    *solved_refs, res_ref, own_ref = refs
+def own_kernel(offs_ref, first_ref, *refs):
+    *solved_refs, res_ref, own_ref, gains_ref = refs
     channels = res_ref.shape[1]
+    comp = lax.broadcasted_iota(jnp.int32, offs_ref.shape[1:], 0)
+    gains_ref[...] = offs_ref[...] + jnp.where((comp == 0) | (comp == 6), 1.0, 0.0)[None]
     lane = lax.axis_index("dir")
 
     def select(value):
@@ -270,8 +288,8 @@
 
 def sweep_kernel(order_ref, counts_ref, damping_ref, *refs, low, high, tiles, factor):
     last = high == SOLVED
-    hots, begin, start_ref, res_ref, own_ref = refs[:5]
-    targets, refs = refs[5:7], refs[7:]
+    hots, turned, part, begin, start_ref, res_ref, own_ref = refs[:7]
+    targets, refs = refs[7:9], refs[9:]
     pair, refs = refs[:2], refs[2:]
     ends, values, state, m_now, k_now = refs[-5:]
     refs = refs[:-5]
@@ -280,25 +298,24 @@
     refs = refs[len(stages) :]
     if last:
         earlier_gains = {m: (refs[s], m - stage[0]) for s, stage in enumerate(stages) for m in range(*stage)}
-        offs_ref, gains_ref, out_ref, moved = refs[len(stages) :]
+        start_own, gains_ref, out_ref, moved = refs[len(stages) :]
     else:
         solved_ref, moved, out_ref = refs
-    groups, count = hots.shape[:2]
-    chunks = groups * tiles
+    chunks = hots.shape[1] // 256
+    parts = start_ref.shape[1] // 128
 
     def rows_at(pair, row):
         stride = pair[0].shape[0] // (chunks // 2)
         return jnp.concatenate([ref[pl.ds(row, chunks // 2, stride=stride), :] for ref in pair], axis=0)
 
     def fetch(gain_now, only=None):
-        split = split_rows(gain_now)
-        for g in range(groups if only is None else only):
-            out = jnp.dot(split, hots[g], preferred_element_type=F32)
-            out = out[:8] + out[8:]
-            for end in (0, 1):
-                for t in range(tiles):
-                    chunk, column = (g * tiles + t) * 8, (end * tiles + t) * 128
-                    ends[end, chunk : chunk + 8, :] = out[:, column : column + 128]
+        step = min(8, chunks) if only is None else only
+        for end in (0, 1):
+            for first in range(0, chunks if only is None else only, step):
+                at = pl.ds((end * chunks + first) * 128, step * 128)
+                out = fetch_columns(gain_now, hots, part, at)
+                for t in range(step):
+                    ends[end, (first + t) * 8 : (first + t) * 8 + 8, :] = out[:, t * 128 : t * 128 + 128]
 
     def gain_at(ref):
         return [as_matrix([ref[end, pl.ds(c, chunks, stride=8), :] for c in range(8)]) for end in (0, 1)]
@@ -391,12 +408,11 @@
                     row += 1
 
     def station_sums():
-        acc = jnp.zeros((32, count), F32)
-        for g in range(groups):
-            starts = [(end, (g * tiles + t) * 16) for end in (0, 1) for t in range(tiles)]
-            split = split_rows(jnp.concatenate([values[end, at : at + 16, :] for end, at in starts], axis=1))
-            acc += lax.dot_general(split, hots[g], (((1,), (1,)), ((), ())), preferred_element_type=F32)
-        return acc[:16] + acc[16:]
+        rows = jnp.concatenate([values[end, at * 16 : at * 16 + 16, :] for end in (0, 1) for at in range(chunks)], axis=1)
+        which = jnp.concatenate([part[...]] * 2, axis=0)
+        wide = [split_rows(jnp.where(which == w, rows, jnp.zeros_like(rows))) for w in range(parts)]
+        acc = jnp.dot(jnp.concatenate(wide, axis=0), turned[...], preferred_element_type=F32)
+        return jnp.concatenate([acc[w * 32 : w * 32 + 16] + acc[w * 32 + 16 : w * 32 + 32] for w in range(parts)], axis=1)
 
     def solve(sums, gain_now, damp):
         numer = sums[:8] + damp * gain_now
@@ -430,9 +446,8 @@
 
     out_ref[...] = res_ref[...]
     if last:
-        width = offs_ref.shape[2]
-        comp = lax.broadcasted_iota(jnp.int32, (8, width), 0)
-        gains_ref[...] = offs_ref[...] + jnp.where((comp == 0) | (comp == 6), 1.0, 0.0)[None]
+        width = start_own.shape[2]
+        gains_ref[...] = start_own[...]
         for i in range(low):
             ref, place = earlier_gains[i]
             gains_ref[order_ref[i]] = ref[place, :, :width]
@@ -455,7 +470,7 @@
 
         lax.fori_loop(0, jnp.minimum(counts_ref[which], LM_ITERS) - 1, more, jnp.int32(0))
         one_round()
-        fetch(state[...], 1 if i + 1 == SOLVED else None)
+        fetch(state[...], tiles if i + 1 == SOLVED else None)
         if last:
             gains_ref[which] = state[:, :width]
         else:
@@ -557,25 +572,32 @@
         width=width,
     )
     chunks = groups * tiles
-    hots, ends, start = call(
+    hots, turned, hot_part, ends, start = call(
         lookup_kernel,
         "lookup",
-        [((groups, count, 2 * baselines), BF16), ((SOLVED, 2, chunks * 8, 128), F32), ((SOLVED * 8, count), F32)],
+        [
+            ((128, 256 * chunks), BF16),
+            ((256 * chunks, 128), BF16),
+            ((8, 256 * chunks), jnp.int32),
+            ((SOLVED, 2, chunks * 8, 128), F32),
+            ((SOLVED * 8, count), F32),
+        ],
         [],
         blocks,
         [table],
         width=width,
         owned=owned,
+        tiles=tiles,
         after=[part],
     )
     partials = butterfly_sums(part, "dir")
     first = partials[-1]
-    res, own = call(
+    res, own, start_own = call(
         own_kernel,
         "own_channels",
-        [(visibilities.shape, F32), ((SOLVED, 8, channels, baselines), F32)],
+        [(visibilities.shape, F32), ((SOLVED, 8, channels, baselines), F32), (gain_offsets.shape, F32)],
         [],
-        [first, *shared],
+        [gain_offsets, first, *shared],
     )
     moved, solved = [], []
     flat = lambda near: [near.reshape(-1, 128), exchange(near, "bl", 1).reshape(-1, 128)]
@@ -593,7 +615,7 @@
             [first, begin] + shared,
             low=low,
             high=high,
-            after=[value],
+            after=[value, hots],
         )
         [kx_near] = call(keep_kernel, "keep", [(kx_near.shape, F32)], [], [kx_near], after=[value])
         products = flat(kx_near)
@@ -607,11 +629,11 @@
             if last
             else [((high - low, 8, count), F32), moved_shape, (visibilities.shape, F32)],
             [solve_order, counts, damping],
-            [hots, ends, start, res, own]
+            [hots, turned, hot_part, ends, start, res, own]
             + targets
             + products
             + moved
-            + (solved + [gain_offsets] if last else []),
+            + (solved + [start_own] if last else []),
             ([moved_shape] if last else [])
             + [
                 ((2, chunks * 8, 128), F32),

time: 68.3 us -> 62.4 us (0.914); the launches traced: 68.9 us -> 62.2 us
  Pallas kernels: 23.7 us -> 15.9 us
  waiting for transfers between devices: 19.8 us -> 22.5 us
  other arithmetic: 2.86 us -> 2.12 us
    pallas_call x7, Pallas kernels: 21.3 us -> 13.5 us  [call(): pl.pallas_call(body, out_shape=[jax.ShapeDtypeStruct(*shape) for shape in...]
    ppermute x18, waiting for transfers between devices: 19.8 us -> 22.5 us  [exchange(): lax.ppermute(block, axis, [(i, i ^ mask) for i in range(lax.axis_size(axi...]
    another operation x3, other arithmetic: 0.87 us -> 0.13 us  [chip_blocks(): jnp.stack([block] + [exchange(block, axis, 2 * j) for j in range(1, chips)])]
    unnamed x12 -> x14, local copies, waits for them, and re-layouts: 1.82 us -> 1.45 us
  transfers between devices with their start and end apart: 18 -> 18, of which waited for: 10 -> 10; matrix products, arithmetic and copies ran while one was open for 4% -> 3% of each run, Pallas kernels for 6% -> 6%
where the time goes in v3:
time: 62.4 us; the launch traced here: 62.2 us
  waiting for transfers between devices  22.5 us (36%)
  starting transfers between devices  19.5 us (31%)
  Pallas kernels  15.9 us (25%)
  other arithmetic  2.12 us (3%)
  local copies, waits for them, and re-layouts  1.45 us (2%)
  between operations  0.78 us (1%)
    ppermute x18, waiting for transfers between devices, exchange(): lax.ppermute(block, axis, [(i, i ^ mask) for i in range(lax.axis_size(axi...  22.5 us
    ppermute x18, starting transfers between devices, exchange(): lax.ppermute(block, axis, [(i, i ^ mask) for i in range(lax.axis_size(axi...  19.5 us
    pallas_call x7, Pallas kernels, call(): pl.pallas_call(body, out_shape=[jax.ShapeDtypeStruct(*shape) for shape in...  13.5 us
    pallas_call x1, Pallas kernels, on_device(): pl.pallas_call(functools.partial(prep_kernel, owned=owned, per=per), out_...  2.42 us
    add x6, other arithmetic, butterfly_sums(): sums.append(sums[-1] + exchange(sums[-1], axis, 1 << len(sums) - 1))  1.99 us
    unnamed x14, local copies, waits for them, and re-layouts  1.45 us
  transfers between devices with their start and end apart: 18, of which 10 were waited for; matrix products, arithmetic and copies ran while one was open for 3% of the time, Pallas kernels for 6%

profile of v3, /device:TPU:0, one launch (start us, length us, event | category | flops | bytes accessed | tf_op | source)
XLA Modules:
  0.0 62.2 jit_solution(2047557689673156560)
XLA Ops:
  0.6 2.4 %prepare.1 = (f32[56,128]{1,0:T(8,128)}, bf16[2,8,16,256]{3,2,1,0:T(8,128)(2,1)}, bf16[2,8,16,256]{3,2,1,0:T(8,128)(2,1)}) custom-call(s32[32]{0:T(128)} %refs_0_.5, s32[2,256]{1,0:T(2,128)} %stations_ref.1, f32[32,8,64]{2,1,0:T(8,128)} %refs_0_.4, bf16[8,8,16,256]{3,2,1,0:T(8,128)(2,1)} %refs_2_.4, bf16[8,8,16,256]{3,2,1,0:T(8,128)(2,1)} %refs_2_.4, ...), custom_call_target="tpu_custom_call" | custom-call | tf_op jit(solution)/shard_map/prepare/pallas_call | solution.py:547
  3.1 3.0 %collective-permute-start.6 = (bf16[2,8,16,256]{3,2,1,0:T(8,128)(2,1)}, bf16[2,8,16,256]{3,2,1,0:T(8,128)(2,1)S(1)}, u32[]{:S(2)}, u32[]{:S(2)}) collective-permute-start(bf16[2,8,16,256]{3,2,1,0:T(8,128)(2,1)} %get-tuple-element.22), channel_id=1, source_target_pairs={{0,1},{1,0},{2,3},{3,2},{4,5},{5,4},{6,7},{7,6},{8,9},{9,8},{10,11... | collective-permute-start | bytes 393224 | tf_op jit(solution)/shard_map/ppermute | solution.py:494
  6.1 2.8 %collective-permute-start.2 = (f32[56,128]{1,0:T(8,128)}, f32[56,128]{1,0:T(8,128)S(1)}, u32[]{:S(2)}, u32[]{:S(2)}) collective-permute-start(f32[56,128]{1,0:T(8,128)} %get-tuple-element.15), channel_id=1, source_target_pairs={{0,24},{4,28},{8,16},{12,20},{16,8},{20,12},{24,0},{28,4},{1,25},{... | collective-permute-start | bytes 86024 | tf_op jit(solution)/shard_map/ppermute | solution.py:494
  9.0 0.5 collective-permute-start.1
  9.6 1.0 %collective-permute-done.6 = bf16[2,8,16,256]{3,2,1,0:T(8,128)(2,1)S(1)} collective-permute-done((bf16[2,8,16,256]{3,2,1,0:T(8,128)(2,1)}, bf16[2,8,16,256]{3,2,1,0:T(8,128)(2,1)S(1)}, u32[]{:S(2)}, u32[]{:S(2)}) %collective-permute-start.6) | collective-permute-done | bytes 131104 | tf_op jit(solution)/shard_map/ppermute | solution.py:494
  10.6 0.9 %add.20 = bf16[2,8,16,256]{3,2,1,0:T(8,128)(2,1)S(1)} add(bf16[2,8,16,256]{3,2,1,0:T(8,128)(2,1)} %get-tuple-element.22, bf16[2,8,16,256]{3,2,1,0:T(8,128)(2,1)S(1)} %collective-permute-done.6) | non-fusion elementwise | flops 65536 | bytes 393216 | tf_op jit(solution)/shard_map/add | solution.py:500
  11.6 3.1 %collective-permute-start.7 = (bf16[2,8,16,256]{3,2,1,0:T(8,128)(2,1)S(1)}, bf16[2,8,16,256]{3,2,1,0:T(8,128)(2,1)S(1)}, u32[]{:S(2)}, u32[]{:S(2)}) collective-permute-start(bf16[2,8,16,256]{3,2,1,0:T(8,128)(2,1)S(1)} %add.20), channel_id=1, source_target_pairs={{0,2},{1,3},{2,0},{3,1},{4,6},{5,7},{6,4},{7,5},{8,10},{9,11},{10,... | collective-permute-start | bytes 393224 | tf_op jit(solution)/shard_map/ppermute | solution.py:494
  14.7 0.9 %add.22 = bf16[2,8,16,256]{3,2,1,0:T(8,128)(2,1)S(1)} add(bf16[2,8,16,256]{3,2,1,0:T(8,128)(2,1)} %get-tuple-element.23, bf16[2,8,16,256]{3,2,1,0:T(8,128)(2,1)S(1)} %collective-permute-done.8) | non-fusion elementwise | flops 65536 | bytes 393216 | tf_op jit(solution)/shard_map/add | solution.py:500
  15.6 1.0 %collective-permute-start.9 = (bf16[2,8,16,256]{3,2,1,0:T(8,128)(2,1)S(1)}, bf16[2,8,16,256]{3,2,1,0:T(8,128)(2,1)S(1)}, u32[]{:S(2)}, u32[]{:S(2)}) collective-permute-start(bf16[2,8,16,256]{3,2,1,0:T(8,128)(2,1)S(1)} %add.22), channel_id=1, source_target_pairs={{0,2},{1,3},{2,0},{3,1},{4,6},{5,7},{6,4},{7,5},{8,10},{9,11},{10,... | collective-permute-start | bytes 393224 | tf_op jit(solution)/shard_map/ppermute | solution.py:494
  16.8 1.3 %collective-permute-done.3.refs_1_ = f32[4,56,128]{2,1,0:T(8,128)S(1)} collective-permute-done((f32[4,56,128]{2,1,0:T(8,128)S(1)}, f32[4,56,128]{2,1,0:T(8,128)S(1)}, u32[]{:S(2)}, u32[]{:S(2)}) %collective-permute-start.3) | collective-permute-done | bytes 114720 | tf_op jit(solution)/shard_map/ppermute | solution.py:494
  18.1 1.0 %first_model.1 = (f32[8,16,256]{2,1,0:T(8,128)S(1)}, f32[32,512]{1,0:T(8,128)S(1)}) custom-call(f32[4,56,128]{2,1,0:T(8,128)S(1)} %pad_maximum_fusion.2.refs_0_, f32[4,56,128]{2,1,0:T(8,128)S(1)} %collective-permute-done.3.refs_1_, bf16[8,8,16,256]{3,2,1,0:T(8,128)(2,1)S(1)} %copy-done, f32[8,4,256]{2,1,0:T(4,128)S(1)} %copy-done.2), custom_call_target="tpu_custom_call" | custom-call | tf_op jit(solution)/shard_map/first_model/pallas_call | solution.py:529
  19.1 1.4 %collective-permute-start.4 = (f32[8,16,256]{2,1,0:T(8,128)S(1)}, f32[8,16,256]{2,1,0:T(8,128)S(1)}, u32[]{:S(2)}, u32[]{:S(2)}) collective-permute-start(f32[8,16,256]{2,1,0:T(8,128)S(1)} %get-tuple-element.16.refs_2_), channel_id=1, source_target_pairs={{0,1},{1,0},{2,3},{3,2},{4,5},{5,4},{6,7},{7,6},{8,9},{9,8},{10,11... | collective-permute-start | bytes 393224 | tf_op jit(solution)/shard_map/ppermute | solution.py:494
  20.4 2.8 %collective-permute-done.7 = bf16[2,8,16,256]{3,2,1,0:T(8,128)(2,1)S(1)} collective-permute-done((bf16[2,8,16,256]{3,2,1,0:T(8,128)(2,1)S(1)}, bf16[2,8,16,256]{3,2,1,0:T(8,128)(2,1)S(1)}, u32[]{:S(2)}, u32[]{:S(2)}) %collective-permute-start.7) | collective-permute-done | bytes 131104 | tf_op jit(solution)/shard_map/ppermute | solution.py:494
  23.3 1.7 %collective-permute-done.9 = bf16[2,8,16,256]{3,2,1,0:T(8,128)(2,1)S(1)} collective-permute-done((bf16[2,8,16,256]{3,2,1,0:T(8,128)(2,1)S(1)}, bf16[2,8,16,256]{3,2,1,0:T(8,128)(2,1)S(1)}, u32[]{:S(2)}, u32[]{:S(2)}) %collective-permute-start.9) | collective-permute-done | bytes 131104 | tf_op jit(solution)/shard_map/ppermute | solution.py:494
  25.0 0.9 %products.1.refs_4_ = f32[2,256,128]{2,1,0:T(8,128)S(1)} custom-call(bf16[2,8,16,256]{3,2,1,0:T(8,128)(2,1)S(1)} %add.21.refs_2_.refs_0_, bf16[2,8,16,256]{3,2,1,0:T(8,128)(2,1)S(1)} %add.23.refs_3_.refs_1_, f32[8,16,256]{2,1,0:T(8,128)S(1)} %get-tuple-element.16.refs_2_), custom_call_target="tpu_custom_call" | custom-call | tf_op jit(solution)/shard_map/products/pallas_call | solution.py:529
  25.9 2.7 %collective-permute-start.16 = (f32[2,256,128]{2,1,0:T(8,128)S(1)}, f32[2,256,128]{2,1,0:T(8,128)S(1)}, u32[]{:S(2)}, u32[]{:S(2)}) collective-permute-start(f32[2,256,128]{2,1,0:T(8,128)S(1)} %products.1.refs_4_), channel_id=1, source_target_pairs={{0,24},{4,28},{8,16},{12,20},{16,8},{20,12},{24,0},{28,4},{1,25},{... | collective-permute-start | bytes 786440 | tf_op jit(solution)/shard_map/ppermute | solution.py:494
  28.6 0.5 collective-permute-start.15
  29.1 0.3 collective-permute-start.14
  29.6 0.8 %lookup.1 = (bf16[128,4096]{1,0:T(8,128)(2,1)S(1)}, bf16[4096,128]{1,0:T(8,128)(2,1)S(1)}, s32[8,4096]{1,0:T(8,128)S(1)}, f32[4,2,128,128]{3,2,1,0:T(8,128)S(1)}, f32[32,512]{1,0:T(8,128)S(1)}) custom-call(f32[4,56,128]{2,1,0:T(8,128)S(1)} %pad_maximum_fusion.2.refs_0_, f32[4,56,128]{2,1,0:T(8,128)S(1)} %collective-permute-done.3.refs_1_, ...), custom_call_target="tpu_custom_call" | custom-call | tf_op jit(solution)/shard_map/lookup/pallas_call | solution.py:529
  30.4 6.4 %collective-permute-done.5 = f32[8,16,256]{2,1,0:T(8,128)S(1)} collective-permute-done((f32[8,16,256]{2,1,0:T(8,128)S(1)}, f32[8,16,256]{2,1,0:T(8,128)S(1)}, u32[]{:S(2)}, u32[]{:S(2)}) %collective-permute-start.5) | collective-permute-done | bytes 131104 | tf_op jit(solution)/shard_map/ppermute | solution.py:494
  36.8 0.7 %targets.1.refs_1_ = f32[2,128,128]{2,1,0:T(8,128)S(1)} custom-call(f32[8,16,256]{2,1,0:T(8,128)S(1)} %add.19.refs_1_.refs_0_, f32[32,512]{1,0:T(8,128)S(1)} %get-tuple-element.26.refs_1_, bf16[2,8,16,256]{3,2,1,0:T(8,128)(2,1)S(1)} %add.21.refs_2_.refs_0_, bf16[2,8,16,256]{3,2,1,0:T(8,128)(2,1)S(1)} %add.23.refs_3_.refs_1_, ...), custom_call_target="tpu_custom_call" | custom-call | tf_op jit(solution)/shard_map/targets/pallas_call | solution.py:529
  37.6 2.0 %collective-permute-done.15 = f32[2,256,128]{2,1,0:T(8,128)S(1)} collective-permute-done((f32[2,256,128]{2,1,0:T(8,128)S(1)}, f32[2,256,128]{2,1,0:T(8,128)S(1)}, u32[]{:S(2)}, u32[]{:S(2)}) %collective-permute-start.15) | collective-permute-done | bytes 262176 | tf_op jit(solution)/shard_map/ppermute | solution.py:494
  39.6 0.2 collective-permute-done.14
  40.0 1.6 %collective-permute-start.12 = (f32[2,128,128]{2,1,0:T(8,128)S(1)}, f32[2,128,128]{2,1,0:T(8,128)S(1)}, u32[]{:S(2)}, u32[]{:S(2)}) collective-permute-start(f32[2,128,128]{2,1,0:T(8,128)S(1)} %targets.1.refs_1_), channel_id=1, source_target_pairs={{0,24},{4,28},{8,16},{12,20},{16,8},{20,12},{24,0},{28,4},{1,25},{... | collective-permute-start | bytes 393224 | tf_op jit(solution)/shard_map/ppermute | solution.py:494
  41.7 1.4 %collective-permute-start.11 = (f32[2,128,128]{2,1,0:T(8,128)S(1)}, f32[2,128,128]{2,1,0:T(8,128)S(1)}, u32[]{:S(2)}, u32[]{:S(2)}) collective-permute-start(f32[2,128,128]{2,1,0:T(8,128)S(1)} %targets.1.refs_1_), channel_id=1, source_target_pairs={{0,16},{4,20},{8,24},{12,28},{16,0},{20,4},{24,8},{28,12},{1,17},{... | collective-permute-start | bytes 393224 | tf_op jit(solution)/shard_map/ppermute | solution.py:494
  43.1 0.5 collective-permute-start.10
  43.6 3.8 %collective-permute-done.12 = f32[2,128,128]{2,1,0:T(8,128)S(1)} collective-permute-done((f32[2,128,128]{2,1,0:T(8,128)S(1)}, f32[2,128,128]{2,1,0:T(8,128)S(1)}, u32[]{:S(2)}, u32[]{:S(2)}) %collective-permute-start.12) | collective-permute-done | bytes 131104 | tf_op jit(solution)/shard_map/ppermute | solution.py:494
  47.3 2.3 %collective-permute-done.11 = f32[2,128,128]{2,1,0:T(8,128)S(1)} collective-permute-done((f32[2,128,128]{2,1,0:T(8,128)S(1)}, f32[2,128,128]{2,1,0:T(8,128)S(1)}, u32[]{:S(2)}, u32[]{:S(2)}) %collective-permute-start.11) | collective-permute-done | bytes 131104 | tf_op jit(solution)/shard_map/ppermute | solution.py:494
  49.8 0.8 %copy-done.1 = f32[32,8,64]{2,1,0:T(8,128)S(1)} copy-done((f32[32,8,64]{2,1,0:T(8,128)S(1)}, f32[32,8,64]{2,1,0:T(8,128)}, u32[]{:S(2)}) %copy-start.1) | copy-done | bytes 65560
  50.7 1.0 %collective-permute-done.13 = f32[4,2,128,128]{3,2,1,0:T(8,128)S(1)} collective-permute-done((f32[4,2,128,128]{3,2,1,0:T(8,128)S(1)}, f32[4,2,128,128]{3,2,1,0:T(8,128)S(1)}, u32[]{:S(2)}, u32[]{:S(2)}) %collective-permute-start.13) | collective-permute-done | bytes 524320 | tf_op jit(solution)/shard_map/ppermute | solution.py:494
  51.7 0.6 %copy-done.3 = s32[32]{0:T(128)S(1)} copy-done((s32[32]{0:T(128)S(1)}, s32[32]{0:T(128)}, u32[]{:S(2)}) %copy-start.3) | copy-done | bytes 152
  52.4 9.8 %sweep.1 = (f32[32,8,64]{2,1,0:T(8,128)}, f32[8,4,256]{2,1,0:T(4,128)}) custom-call(s32[32]{0:T(128)S(1)} %copy-done.3, s32[32]{0:T(128)S(1)} %copy-done.4, s32[32]{0:T(128)S(1)} %copy-done.5, bf16[128,4096]{1,0:T(8,128)(2,1)S(1)} %get-tuple-element.17.refs_5_.refs_3_, bf16[4096,128]{1,0:T(8,128)(2,1)S(1)} %get-tuple-element.18.refs_4_, ...), custom_call_target="tpu_custom_call" | custom-call | tf_op jit(solution)/shard_map/sweep/pallas_call | solution.py:529
  (35 shorter events, 1.0 us)
Async XLA Ops:
  3.1 15.0 %copy-start = (bf16[8,8,16,256]{3,2,1,0:T(8,128)(2,1)S(1)}, bf16[8,8,16,256]{3,2,1,0:T(8,128)(2,1)}, u32[]{:S(2)}) copy-start(bf16[8,8,16,256]{3,2,1,0:T(8,128)(2,1)} %refs_2_.4) | copy-start | bytes 1572868
  3.1 7.6 %collective-permute-start.6 = (bf16[2,8,16,256]{3,2,1,0:T(8,128)(2,1)}, bf16[2,8,16,256]{3,2,1,0:T(8,128)(2,1)S(1)}, u32[]{:S(2)}, u32[]{:S(2)}) collective-permute-start(bf16[2,8,16,256]{3,2,1,0:T(8,128)(2,1)} %get-tuple-element.22), channel_id=1, source_target_pairs={{0,1},{1,0},{2,3},{3,2},{4,5},{5,4},{6,7},{7,6},{8,9},{9,8},{10,11... | collective-permute-start | bytes 393224 | tf_op jit(solution)/shard_map/ppermute | solution.py:494
  6.1 8.6 %collective-permute-start.8 = (bf16[2,8,16,256]{3,2,1,0:T(8,128)(2,1)}, bf16[2,8,16,256]{3,2,1,0:T(8,128)(2,1)S(1)}, u32[]{:S(2)}, u32[]{:S(2)}) collective-permute-start(bf16[2,8,16,256]{3,2,1,0:T(8,128)(2,1)} %get-tuple-element.23), channel_id=1, source_target_pairs={{0,1},{1,0},{2,3},{3,2},{4,5},{5,4},{6,7},{7,6},{8,9},{9,8},{10,11... | collective-permute-start | bytes 393224 | tf_op jit(solution)/shard_map/ppermute | solution.py:494
  6.1 10.5 %collective-permute-start.2 = (f32[56,128]{1,0:T(8,128)}, f32[56,128]{1,0:T(8,128)S(1)}, u32[]{:S(2)}, u32[]{:S(2)}) collective-permute-start(f32[56,128]{1,0:T(8,128)} %get-tuple-element.15), channel_id=1, source_target_pairs={{0,24},{4,28},{8,16},{12,20},{16,8},{20,12},{24,0},{28,4},{1,25},{... | collective-permute-start | bytes 86024 | tf_op jit(solution)/shard_map/ppermute | solution.py:494
  9.0 7.7 %collective-permute-start.1 = (f32[56,128]{1,0:T(8,128)}, f32[56,128]{1,0:T(8,128)S(1)}, u32[]{:S(2)}, u32[]{:S(2)}) collective-permute-start(f32[56,128]{1,0:T(8,128)} %get-tuple-element.15), channel_id=1, source_target_pairs={{0,16},{4,20},{8,24},{12,28},{16,0},{20,4},{24,8},{28,12},{1,17},{... | collective-permute-start | bytes 86024 | tf_op jit(solution)/shard_map/ppermute | solution.py:494
  9.5 7.2 %collective-permute-start = (f32[56,128]{1,0:T(8,128)}, f32[56,128]{1,0:T(8,128)S(1)}, u32[]{:S(2)}, u32[]{:S(2)}) collective-permute-start(f32[56,128]{1,0:T(8,128)} %get-tuple-element.15), channel_id=1, source_target_pairs={{0,8},{4,12},{8,0},{12,4},{16,24},{20,28},{24,16},{28,20},{1,9},{5... | collective-permute-start | bytes 86024 | tf_op jit(solution)/shard_map/ppermute | solution.py:494
  11.6 5.1 %copy-start.6 = (f32[56,128]{1,0:T(8,128)S(1)}, f32[56,128]{1,0:T(8,128)}, u32[]{:S(2)}) copy-start(f32[56,128]{1,0:T(8,128)} %get-tuple-element.15) | copy-start | bytes 86020
  11.6 11.7 %collective-permute-start.7 = (bf16[2,8,16,256]{3,2,1,0:T(8,128)(2,1)S(1)}, bf16[2,8,16,256]{3,2,1,0:T(8,128)(2,1)S(1)}, u32[]{:S(2)}, u32[]{:S(2)}) collective-permute-start(bf16[2,8,16,256]{3,2,1,0:T(8,128)(2,1)S(1)} %add.20), channel_id=1, source_target_pairs={{0,2},{1,3},{2,0},{3,1},{4,6},{5,7},{6,4},{7,5},{8,10},{9,11},{10,... | collective-permute-start | bytes 393224 | tf_op jit(solution)/shard_map/ppermute | solution.py:494
  15.6 9.3 %collective-permute-start.9 = (bf16[2,8,16,256]{3,2,1,0:T(8,128)(2,1)S(1)}, bf16[2,8,16,256]{3,2,1,0:T(8,128)(2,1)S(1)}, u32[]{:S(2)}, u32[]{:S(2)}) collective-permute-start(bf16[2,8,16,256]{3,2,1,0:T(8,128)(2,1)S(1)} %add.22), channel_id=1, source_target_pairs={{0,2},{1,3},{2,0},{3,1},{4,6},{5,7},{6,4},{7,5},{8,10},{9,11},{10,... | collective-permute-start | bytes 393224 | tf_op jit(solution)/shard_map/ppermute | solution.py:494
  16.7 1.4 %copy-start.2 = (f32[8,4,256]{2,1,0:T(4,128)S(1)}, f32[8,4,256]{2,1,0:T(4,128)}, u32[]{:S(2)}) copy-start(f32[8,4,256]{2,1,0:T(4,128)} %refs_3_.3) | copy-start | bytes 98308
  16.7 1.4 %collective-permute-start.3 = (f32[4,56,128]{2,1,0:T(8,128)S(1)}, f32[4,56,128]{2,1,0:T(8,128)S(1)}, u32[]{:S(2)}, u32[]{:S(2)}) collective-permute-start(f32[4,56,128]{2,1,0:T(8,128)S(1)} %pad_maximum_fusion.2.refs_0_), channel_id=1, source_target_pairs={{0,4},{4,0},{8,12},{12,8},{16,20},{20,16},{24,28},{28,24},{1,5},{5... | collective-permute-start | bytes 344072 | tf_op jit(solution)/shard_map/ppermute | solution.py:494
  19.1 10.4 %collective-permute-start.4 = (f32[8,16,256]{2,1,0:T(8,128)S(1)}, f32[8,16,256]{2,1,0:T(8,128)S(1)}, u32[]{:S(2)}, u32[]{:S(2)}) collective-permute-start(f32[8,16,256]{2,1,0:T(8,128)S(1)} %get-tuple-element.16.refs_2_), channel_id=1, source_target_pairs={{0,1},{1,0},{2,3},{3,2},{4,5},{5,4},{6,7},{7,6},{8,9},{9,8},{10,11... | collective-permute-start | bytes 393224 | tf_op jit(solution)/shard_map/ppermute | solution.py:494
  25.9 11.7 %collective-permute-start.16 = (f32[2,256,128]{2,1,0:T(8,128)S(1)}, f32[2,256,128]{2,1,0:T(8,128)S(1)}, u32[]{:S(2)}, u32[]{:S(2)}) collective-permute-start(f32[2,256,128]{2,1,0:T(8,128)S(1)} %products.1.refs_4_), channel_id=1, source_target_pairs={{0,24},{4,28},{8,16},{12,20},{16,8},{20,12},{24,0},{28,4},{1,25},{... | collective-permute-start | bytes 786440 | tf_op jit(solution)/shard_map/ppermute | solution.py:494
  28.6 11.0 %collective-permute-start.15 = (f32[2,256,128]{2,1,0:T(8,128)S(1)}, f32[2,256,128]{2,1,0:T(8,128)S(1)}, u32[]{:S(2)}, u32[]{:S(2)}) collective-permute-start(f32[2,256,128]{2,1,0:T(8,128)S(1)} %products.1.refs_4_), channel_id=1, source_target_pairs={{0,16},{4,20},{8,24},{12,28},{16,0},{20,4},{24,8},{28,12},{1,17},{... | collective-permute-start | bytes 786440 | tf_op jit(solution)/shard_map/ppermute | solution.py:494
  29.1 10.7 %collective-permute-start.14 = (f32[2,256,128]{2,1,0:T(8,128)S(1)}, f32[2,256,128]{2,1,0:T(8,128)S(1)}, u32[]{:S(2)}, u32[]{:S(2)}) collective-permute-start(f32[2,256,128]{2,1,0:T(8,128)S(1)} %products.1.refs_4_), channel_id=1, source_target_pairs={{0,8},{4,12},{8,0},{12,4},{16,24},{20,28},{24,16},{28,20},{1,9},{5... | collective-permute-start | bytes 786440 | tf_op jit(solution)/shard_map/ppermute | solution.py:494
  29.5 7.3 %collective-permute-start.5 = (f32[8,16,256]{2,1,0:T(8,128)S(1)}, f32[8,16,256]{2,1,0:T(8,128)S(1)}, u32[]{:S(2)}, u32[]{:S(2)}) collective-permute-start(f32[8,16,256]{2,1,0:T(8,128)S(1)} %add.18), channel_id=1, source_target_pairs={{0,2},{1,3},{2,0},{3,1},{4,6},{5,7},{6,4},{7,5},{8,10},{9,11},{10,... | collective-permute-start | bytes 393224 | tf_op jit(solution)/shard_map/ppermute | solution.py:494
  40.0 11.7 %collective-permute-start.17 = (f32[4,2,256,128]{3,2,1,0:T(8,128)S(1)}, f32[4,2,256,128]{3,2,1,0:T(8,128)S(1)}, u32[]{:S(2)}, u32[]{:S(2)}) collective-permute-start(f32[4,2,256,128]{3,2,1,0:T(8,128)S(1)} %keep.1), channel_id=1, source_target_pairs={{0,4},{4,0},{8,12},{12,8},{16,20},{20,16},{24,28},{28,24},{1,5},{5... | collective-permute-start | bytes 3145736 | tf_op jit(solution)/shard_map/ppermute | solution.py:494
  40.0 7.3 %collective-permute-start.12 = (f32[2,128,128]{2,1,0:T(8,128)S(1)}, f32[2,128,128]{2,1,0:T(8,128)S(1)}, u32[]{:S(2)}, u32[]{:S(2)}) collective-permute-start(f32[2,128,128]{2,1,0:T(8,128)S(1)} %targets.1.refs_1_), channel_id=1, source_target_pairs={{0,24},{4,28},{8,16},{12,20},{16,8},{20,12},{24,0},{28,4},{1,25},{... | collective-permute-start | bytes 393224 | tf_op jit(solution)/shard_map/ppermute | solution.py:494
  41.7 8.0 %collective-permute-start.11 = (f32[2,128,128]{2,1,0:T(8,128)S(1)}, f32[2,128,128]{2,1,0:T(8,128)S(1)}, u32[]{:S(2)}, u32[]{:S(2)}) collective-permute-start(f32[2,128,128]{2,1,0:T(8,128)S(1)} %targets.1.refs_1_), channel_id=1, source_target_pairs={{0,16},{4,20},{8,24},{12,28},{16,0},{20,4},{24,8},{28,12},{1,17},{... | collective-permute-start | bytes 393224 | tf_op jit(solution)/shard_map/ppermute | solution.py:494
  43.1 6.6 %collective-permute-start.10 = (f32[2,128,128]{2,1,0:T(8,128)S(1)}, f32[2,128,128]{2,1,0:T(8,128)S(1)}, u32[]{:S(2)}, u32[]{:S(2)}) collective-permute-start(f32[2,128,128]{2,1,0:T(8,128)S(1)} %targets.1.refs_1_), channel_id=1, source_target_pairs={{0,8},{4,12},{8,0},{12,4},{16,24},{20,28},{24,16},{28,20},{1,9},{5... | collective-permute-start | bytes 393224 | tf_op jit(solution)/shard_map/ppermute | solution.py:494
  49.7 0.9 %copy-start.1 = (f32[32,8,64]{2,1,0:T(8,128)S(1)}, f32[32,8,64]{2,1,0:T(8,128)}, u32[]{:S(2)}) copy-start(f32[32,8,64]{2,1,0:T(8,128)} %refs_0_.4) | copy-start | bytes 196612
  49.7 2.0 %collective-permute-start.13 = (f32[4,2,128,128]{3,2,1,0:T(8,128)S(1)}, f32[4,2,128,128]{3,2,1,0:T(8,128)S(1)}, u32[]{:S(2)}, u32[]{:S(2)}) collective-permute-start(f32[4,2,128,128]{3,2,1,0:T(8,128)S(1)} %pad_maximum_fusion.1), channel_id=1, source_target_pairs={{0,4},{4,0},{8,12},{12,8},{16,20},{20,16},{24,28},{28,24},{1,5},{5... | collective-permute-start | bytes 1572872 | tf_op jit(solution)/shard_map/ppermute | solution.py:494
  51.7 0.7 %copy-start.3 = (s32[32]{0:T(128)S(1)}, s32[32]{0:T(128)}, u32[]{:S(2)}) copy-start(s32[32]{0:T(128)} %refs_0_.5) | copy-start | bytes 388
  51.7 0.7 %copy-start.4 = (s32[32]{0:T(128)S(1)}, s32[32]{0:T(128)}, u32[]{:S(2)}) copy-start(s32[32]{0:T(128)} %refs_1_.3) | copy-start | bytes 388
  51.7 0.7 %copy-start.5 = (s32[32]{0:T(128)S(1)}, s32[32]{0:T(128)}, u32[]{:S(2)}) copy-start(s32[32]{0:T(128)} %refs_2_.5) | copy-start | bytes 388

commit v4 on v3

--- a/solution.py
+++ b/solution.py
@@ -149,9 +149,14 @@
     return value
 
 
-def lookup_kernel(near_ref, far_ref, hots_ref, turned_ref, part_ref, ends_ref, start_ref, table, *, width, owned, tiles):
+def lookup_kernel(
+    order_ref, counts_ref, damping_ref, offs_ref, near_ref, far_ref, hots_ref, turned_ref, part_ref, ends_ref, start_ref,
+    gains_ref, table, *, width, owned, tiles,
+):
     half = near_ref.shape[0]
     chunks = 2 * half * tiles
+    comp = lax.broadcasted_iota(jnp.int32, offs_ref.shape[1:], 0)
+    gains_ref[...] = offs_ref[...] + jnp.where((comp == 0) | (comp == 6), 1.0, 0.0)[None]
     base = lax.axis_index("bl").astype(jnp.int32) * width
     fill_table([near_ref, far_ref], table, width)
     start = table[owned * 8 : (owned + SOLVED) * 8, :]
@@ -266,11 +271,9 @@
                     out += 2
 
 
-def own_kernel(offs_ref, first_ref, *refs):
-    *solved_refs, res_ref, own_ref, gains_ref = refs
+def own_kernel(first_ref, *refs):
+    *solved_refs, res_ref, own_ref = refs
     channels = res_ref.shape[1]
-    comp = lax.broadcasted_iota(jnp.int32, offs_ref.shape[1:], 0)
-    gains_ref[...] = offs_ref[...] + jnp.where((comp == 0) | (comp == 6), 1.0, 0.0)[None]
     lane = lax.axis_index("dir")
 
     def select(value):
@@ -501,14 +504,15 @@
     return sums
 
 
-def chip_blocks(block, axis):
+def chip_blocks(block, axis, parts_out=False):
     chips = lax.axis_size(axis) // 2
     if chips <= 4:
-        return jnp.stack([block] + [exchange(block, axis, 2 * j) for j in range(1, chips)])
+        blocks = [block] + [exchange(block, axis, 2 * j) for j in range(1, chips)]
+        return (jnp.stack(blocks), blocks[1]) if parts_out else jnp.stack(blocks)
     parts = block[None]
     while parts.shape[0] < chips:
         parts = jnp.concatenate([parts, exchange(parts, axis, 2 * parts.shape[0])], axis=0)
-    return parts
+    return (parts, parts) if parts_out else parts
 
 
 def on_device(visibilities, coherencies, gain_offsets, stations, solve_order, counts, damping):
@@ -572,7 +576,7 @@
         width=width,
     )
     chunks = groups * tiles
-    hots, turned, hot_part, ends, start = call(
+    hots, turned, hot_part, ends, start, start_own = call(
         lookup_kernel,
         "lookup",
         [
@@ -581,9 +585,10 @@
             ((8, 256 * chunks), jnp.int32),
             ((SOLVED, 2, chunks * 8, 128), F32),
             ((SOLVED * 8, count), F32),
+            (gain_offsets.shape, F32),
         ],
-        [],
-        blocks,
+        [solve_order, counts, damping],
+        [gain_offsets] + blocks,
         [table],
         width=width,
         owned=owned,
@@ -592,12 +597,12 @@
     )
     partials = butterfly_sums(part, "dir")
     first = partials[-1]
-    res, own, start_own = call(
+    res, own = call(
         own_kernel,
         "own_channels",
-        [(visibilities.shape, F32), ((SOLVED, 8, channels, baselines), F32), (gain_offsets.shape, F32)],
+        [(visibilities.shape, F32), ((SOLVED, 8, channels, baselines), F32)],
         [],
-        [gain_offsets, first, *shared],
+        [first, *shared],
     )
     moved, solved = [], []
     flat = lambda near: [near.reshape(-1, 128), exchange(near, "bl", 1).reshape(-1, 128)]
@@ -617,9 +622,10 @@
             high=high,
             after=[value, hots],
         )
+        near, near_x = chip_blocks(value, "bl", True)
         [kx_near] = call(keep_kernel, "keep", [(kx_near.shape, F32)], [], [kx_near], after=[value])
         products = flat(kx_near)
-        targets = flat(chip_blocks(value, "bl"))
+        targets = flat(near)
         last = high == SOLVED
         moved_shape = ((high - low, M_ROWS, chunks, 128), F32)
         outs = call(

time: 62.4 us -> 61.2 us (0.981)
  local copies, waits for them, and re-layouts: 1.45 us -> 0.04 us
    unnamed x14, local copies, waits for them, and re-layouts: 1.45 us -> 0.04 us
  transfers between devices with their start and end apart: 18 -> 18, of which waited for: 10 -> 10; matrix products, arithmetic and copies ran while one was open for 3% -> 3% of each run, Pallas kernels for 6% -> 7%
where the time goes in v4:
time: 61.2 us; the launch traced here: 60.6 us
  waiting for transfers between devices  22.6 us (37%)
  starting transfers between devices  19.5 us (32%)
  Pallas kernels  15.5 us (25%)
  other arithmetic  2.1 us (3%)
  between operations  0.84 us (1%)
    ppermute x18, waiting for transfers between devices, exchange(): lax.ppermute(block, axis, [(i, i ^ mask) for i in range(lax.axis_size(axi...  22.6 us
    ppermute x18, starting transfers between devices, exchange(): lax.ppermute(block, axis, [(i, i ^ mask) for i in range(lax.axis_size(axi...  19.5 us
    pallas_call x7, Pallas kernels, call(): pl.pallas_call(body, out_shape=[jax.ShapeDtypeStruct(*shape) for shape in...  13.1 us
    pallas_call x1, Pallas kernels, on_device(): pl.pallas_call(functools.partial(prep_kernel, owned=owned, per=per), out_...  2.42 us
    add x6, other arithmetic, butterfly_sums(): sums.append(sums[-1] + exchange(sums[-1], axis, 1 << len(sums) - 1))  1.98 us
  transfers between devices with their start and end apart: 18, of which 10 were waited for; matrix products, arithmetic and copies ran while one was open for 3% of the time, Pallas kernels for 7%

profile of v4, /device:TPU:0, one launch (start us, length us, event | category | flops | bytes accessed | tf_op | source)
XLA Modules:
  0.0 60.6 jit_solution(2023766472658446619)
XLA Ops:
  0.6 2.4 %prepare.1 = (f32[56,128]{1,0:T(8,128)}, bf16[2,8,16,256]{3,2,1,0:T(8,128)(2,1)}, bf16[2,8,16,256]{3,2,1,0:T(8,128)(2,1)}) custom-call(s32[32]{0:T(128)} %refs_0_.5, s32[2,256]{1,0:T(2,128)} %stations_ref.1, f32[32,8,64]{2,1,0:T(8,128)} %refs_3_.5, bf16[8,8,16,256]{3,2,1,0:T(8,128)(2,1)} %refs_2_.5, bf16[8,8,16,256]{3,2,1,0:T(8,128)(2,1)} %refs_2_.5, ...), custom_call_target="tpu_custom_call" | custom-call | tf_op jit(solution)/shard_map/prepare/pallas_call | solution.py:551
  3.1 3.0 %collective-permute-start.6 = (bf16[2,8,16,256]{3,2,1,0:T(8,128)(2,1)}, bf16[2,8,16,256]{3,2,1,0:T(8,128)(2,1)S(1)}, u32[]{:S(2)}, u32[]{:S(2)}) collective-permute-start(bf16[2,8,16,256]{3,2,1,0:T(8,128)(2,1)} %get-tuple-element.22), channel_id=1, source_target_pairs={{0,1},{1,0},{2,3},{3,2},{4,5},{5,4},{6,7},{7,6},{8,9},{9,8},{10,11... | collective-permute-start | bytes 393224 | tf_op jit(solution)/shard_map/ppermute | solution.py:497
  6.1 2.8 %collective-permute-start.2 = (f32[56,128]{1,0:T(8,128)}, f32[56,128]{1,0:T(8,128)S(1)}, u32[]{:S(2)}, u32[]{:S(2)}) collective-permute-start(f32[56,128]{1,0:T(8,128)} %get-tuple-element.15), channel_id=1, source_target_pairs={{0,24},{4,28},{8,16},{12,20},{16,8},{20,12},{24,0},{28,4},{1,25},{... | collective-permute-start | bytes 86024 | tf_op jit(solution)/shard_map/ppermute | solution.py:497
  9.0 0.5 collective-permute-start.1
  9.5 0.1 collective-permute-start
  9.6 1.0 %collective-permute-done.6 = bf16[2,8,16,256]{3,2,1,0:T(8,128)(2,1)S(1)} collective-permute-done((bf16[2,8,16,256]{3,2,1,0:T(8,128)(2,1)}, bf16[2,8,16,256]{3,2,1,0:T(8,128)(2,1)S(1)}, u32[]{:S(2)}, u32[]{:S(2)}) %collective-permute-start.6) | collective-permute-done | bytes 131104 | tf_op jit(solution)/shard_map/ppermute | solution.py:497
  10.6 0.9 %add.20 = bf16[2,8,16,256]{3,2,1,0:T(8,128)(2,1)S(1)} add(bf16[2,8,16,256]{3,2,1,0:T(8,128)(2,1)} %get-tuple-element.22, bf16[2,8,16,256]{3,2,1,0:T(8,128)(2,1)S(1)} %collective-permute-done.6) | non-fusion elementwise | flops 65536 | bytes 393216 | tf_op jit(solution)/shard_map/add | solution.py:503
  11.6 3.1 %collective-permute-start.7 = (bf16[2,8,16,256]{3,2,1,0:T(8,128)(2,1)S(1)}, bf16[2,8,16,256]{3,2,1,0:T(8,128)(2,1)S(1)}, u32[]{:S(2)}, u32[]{:S(2)}) collective-permute-start(bf16[2,8,16,256]{3,2,1,0:T(8,128)(2,1)S(1)} %add.20), channel_id=1, source_target_pairs={{0,2},{1,3},{2,0},{3,1},{4,6},{5,7},{6,4},{7,5},{8,10},{9,11},{10,... | collective-permute-start | bytes 393224 | tf_op jit(solution)/shard_map/ppermute | solution.py:497
  14.7 0.9 %add.22 = bf16[2,8,16,256]{3,2,1,0:T(8,128)(2,1)S(1)} add(bf16[2,8,16,256]{3,2,1,0:T(8,128)(2,1)} %get-tuple-element.23, bf16[2,8,16,256]{3,2,1,0:T(8,128)(2,1)S(1)} %collective-permute-done.8) | non-fusion elementwise | flops 65536 | bytes 393216 | tf_op jit(solution)/shard_map/add | solution.py:503
  15.6 1.0 %collective-permute-start.9 = (bf16[2,8,16,256]{3,2,1,0:T(8,128)(2,1)S(1)}, bf16[2,8,16,256]{3,2,1,0:T(8,128)(2,1)S(1)}, u32[]{:S(2)}, u32[]{:S(2)}) collective-permute-start(bf16[2,8,16,256]{3,2,1,0:T(8,128)(2,1)S(1)} %add.22), channel_id=1, source_target_pairs={{0,2},{1,3},{2,0},{3,1},{4,6},{5,7},{6,4},{7,5},{8,10},{9,11},{10,... | collective-permute-start | bytes 393224 | tf_op jit(solution)/shard_map/ppermute | solution.py:497
  16.8 1.3 %collective-permute-done.3.refs_1_.refs_5_ = f32[4,56,128]{2,1,0:T(8,128)S(1)} collective-permute-done((f32[4,56,128]{2,1,0:T(8,128)S(1)}, f32[4,56,128]{2,1,0:T(8,128)S(1)}, u32[]{:S(2)}, u32[]{:S(2)}) %collective-permute-start.3) | collective-permute-done | bytes 114720 | tf_op jit(solution)/shard_map/ppermute | solution.py:497
  18.1 1.0 %first_model.1 = (f32[8,16,256]{2,1,0:T(8,128)S(1)}, f32[32,512]{1,0:T(8,128)S(1)}) custom-call(f32[4,56,128]{2,1,0:T(8,128)S(1)} %pad_maximum_fusion.2.refs_0_.refs_4_, f32[4,56,128]{2,1,0:T(8,128)S(1)} %collective-permute-done.3.refs_1_.refs_5_, bf16[8,8,16,256]{3,2,1,0:T(8,128)(2,1)S(1)} %copy-done, f32[8,4,256]{2,1,0:T(4,128)S(1)} %copy-done.2), custom_call_target="tpu_custom_call" | custom-call | tf_op jit(solution)/shard_map/first_model/pallas_call | solution.py:533
  19.1 1.4 %collective-permute-start.4 = (f32[8,16,256]{2,1,0:T(8,128)S(1)}, f32[8,16,256]{2,1,0:T(8,128)S(1)}, u32[]{:S(2)}, u32[]{:S(2)}) collective-permute-start(f32[8,16,256]{2,1,0:T(8,128)S(1)} %get-tuple-element.16.refs_6_.refs_2_), channel_id=1, source_target_pairs={{0,1},{1,0},{2,3},{3,2},{4,5},{5,4},{6,7},{7,6},{8,9},{9,8},{10,11... | collective-permute-start | bytes 393224 | tf_op jit(solution)/shard_map/ppermute | solution.py:497
  20.4 2.8 %collective-permute-done.7 = bf16[2,8,16,256]{3,2,1,0:T(8,128)(2,1)S(1)} collective-permute-done((bf16[2,8,16,256]{3,2,1,0:T(8,128)(2,1)S(1)}, bf16[2,8,16,256]{3,2,1,0:T(8,128)(2,1)S(1)}, u32[]{:S(2)}, u32[]{:S(2)}) %collective-permute-start.7) | collective-permute-done | bytes 131104 | tf_op jit(solution)/shard_map/ppermute | solution.py:497
  23.3 1.7 %collective-permute-done.9 = bf16[2,8,16,256]{3,2,1,0:T(8,128)(2,1)S(1)} collective-permute-done((bf16[2,8,16,256]{3,2,1,0:T(8,128)(2,1)S(1)}, bf16[2,8,16,256]{3,2,1,0:T(8,128)(2,1)S(1)}, u32[]{:S(2)}, u32[]{:S(2)}) %collective-permute-start.9) | collective-permute-done | bytes 131104 | tf_op jit(solution)/shard_map/ppermute | solution.py:497
  25.0 0.9 %products.1.refs_4_ = f32[2,256,128]{2,1,0:T(8,128)S(1)} custom-call(bf16[2,8,16,256]{3,2,1,0:T(8,128)(2,1)S(1)} %add.21.refs_1_.refs_0_.refs_2_, bf16[2,8,16,256]{3,2,1,0:T(8,128)(2,1)S(1)} %add.23.refs_2_.refs_1_.refs_3_, f32[8,16,256]{2,1,0:T(8,128)S(1)} %get-tuple-element.16.refs_6_.refs_2_), custom_call_target="tpu_custom_call" | custom-call | tf_op jit(solution)/shard_map/products/pallas_call | solution.py:533
  25.9 2.7 %collective-permute-start.16 = (f32[2,256,128]{2,1,0:T(8,128)S(1)}, f32[2,256,128]{2,1,0:T(8,128)S(1)}, u32[]{:S(2)}, u32[]{:S(2)}) collective-permute-start(f32[2,256,128]{2,1,0:T(8,128)S(1)} %products.1.refs_4_), channel_id=1, source_target_pairs={{0,24},{4,28},{8,16},{12,20},{16,8},{20,12},{24,0},{28,4},{1,25},{... | collective-permute-start | bytes 786440 | tf_op jit(solution)/shard_map/ppermute | solution.py:497
  28.7 0.5 collective-permute-start.15
  29.2 0.3 collective-permute-start.14
  29.6 1.4 %lookup.1 = (bf16[128,4096]{1,0:T(8,128)(2,1)S(1)}, bf16[4096,128]{1,0:T(8,128)(2,1)S(1)}, s32[8,4096]{1,0:T(8,128)S(1)}, f32[4,2,128,128]{3,2,1,0:T(8,128)S(1)}...) custom-call(s32[32]{0:T(128)S(1)} %copy-done.3, s32[32]{0:T(128)S(1)} %copy-done.4, s32[32]{0:T(128)S(1)} %copy-done.5, ...), custom_call_target="tpu_custom_call" | custom-call | tf_op jit(solution)/shard_map/lookup/pallas_call | solution.py:533
  31.0 5.8 %collective-permute-done.5 = f32[8,16,256]{2,1,0:T(8,128)S(1)} collective-permute-done((f32[8,16,256]{2,1,0:T(8,128)S(1)}, f32[8,16,256]{2,1,0:T(8,128)S(1)}, u32[]{:S(2)}, u32[]{:S(2)}) %collective-permute-start.5) | collective-permute-done | bytes 131104 | tf_op jit(solution)/shard_map/ppermute | solution.py:497
  36.9 0.7 %targets.1.refs_1_ = f32[2,128,128]{2,1,0:T(8,128)S(1)} custom-call(f32[8,16,256]{2,1,0:T(8,128)S(1)} %add.19.refs_0_, f32[32,512]{1,0:T(8,128)S(1)} %get-tuple-element.26.refs_1_, bf16[2,8,16,256]{3,2,1,0:T(8,128)(2,1)S(1)} %add.21.refs_1_.refs_0_.refs_2_, bf16[2,8,16,256]{3,2,1,0:T(8,128)(2,1)S(1)} %add.23.refs_2_.refs_1_.refs_3_, ...), custom_call_target="tpu_custom_call" | custom-call | tf_op jit(solution)/shard_map/targets/pallas_call | solution.py:533
  37.6 2.0 %collective-permute-done.15 = f32[2,256,128]{2,1,0:T(8,128)S(1)} collective-permute-done((f32[2,256,128]{2,1,0:T(8,128)S(1)}, f32[2,256,128]{2,1,0:T(8,128)S(1)}, u32[]{:S(2)}, u32[]{:S(2)}) %collective-permute-start.15) | collective-permute-done | bytes 262176 | tf_op jit(solution)/shard_map/ppermute | solution.py:497
  39.7 0.2 collective-permute-done.14
  40.1 1.6 %collective-permute-start.12 = (f32[2,128,128]{2,1,0:T(8,128)S(1)}, f32[2,128,128]{2,1,0:T(8,128)S(1)}, u32[]{:S(2)}, u32[]{:S(2)}) collective-permute-start(f32[2,128,128]{2,1,0:T(8,128)S(1)} %targets.1.refs_1_), channel_id=1, source_target_pairs={{0,24},{4,28},{8,16},{12,20},{16,8},{20,12},{24,0},{28,4},{1,25},{... | collective-permute-start | bytes 393224 | tf_op jit(solution)/shard_map/ppermute | solution.py:497
  41.7 1.4 %collective-permute-start.11 = (f32[2,128,128]{2,1,0:T(8,128)S(1)}, f32[2,128,128]{2,1,0:T(8,128)S(1)}, u32[]{:S(2)}, u32[]{:S(2)}) collective-permute-start(f32[2,128,128]{2,1,0:T(8,128)S(1)} %targets.1.refs_1_), channel_id=1, source_target_pairs={{0,16},{4,20},{8,24},{12,28},{16,0},{20,4},{24,8},{28,12},{1,17},{... | collective-permute-start | bytes 393224 | tf_op jit(solution)/shard_map/ppermute | solution.py:497
  43.1 0.5 collective-permute-start.10
  43.6 3.8 %collective-permute-done.12 = f32[2,128,128]{2,1,0:T(8,128)S(1)} collective-permute-done((f32[2,128,128]{2,1,0:T(8,128)S(1)}, f32[2,128,128]{2,1,0:T(8,128)S(1)}, u32[]{:S(2)}, u32[]{:S(2)}) %collective-permute-start.12) | collective-permute-done | bytes 131104 | tf_op jit(solution)/shard_map/ppermute | solution.py:497
  47.4 2.3 %collective-permute-done.11 = f32[2,128,128]{2,1,0:T(8,128)S(1)} collective-permute-done((f32[2,128,128]{2,1,0:T(8,128)S(1)}, f32[2,128,128]{2,1,0:T(8,128)S(1)}, u32[]{:S(2)}, u32[]{:S(2)}) %collective-permute-start.11) | collective-permute-done | bytes 131104 | tf_op jit(solution)/shard_map/ppermute | solution.py:497
  49.7 0.1 collective-permute-start.13
  50.0 1.8 %collective-permute-done.13 = f32[4,2,128,128]{3,2,1,0:T(8,128)S(1)} collective-permute-done((f32[4,2,128,128]{3,2,1,0:T(8,128)S(1)}, f32[4,2,128,128]{3,2,1,0:T(8,128)S(1)}, u32[]{:S(2)}, u32[]{:S(2)}) %collective-permute-start.13) | collective-permute-done | bytes 524320 | tf_op jit(solution)/shard_map/ppermute | solution.py:497
  51.7 8.9 %sweep.1 = (f32[32,8,64]{2,1,0:T(8,128)}, f32[8,4,256]{2,1,0:T(4,128)}) custom-call(s32[32]{0:T(128)S(1)} %copy-done.3, s32[32]{0:T(128)S(1)} %copy-done.4, s32[32]{0:T(128)S(1)} %copy-done.5, bf16[128,4096]{1,0:T(8,128)(2,1)S(1)} %get-tuple-element.17.refs_5_.refs_3_, bf16[4096,128]{1,0:T(8,128)(2,1)S(1)} %get-tuple-element.18.refs_4_, ...), custom_call_target="tpu_custom_call" | custom-call | tf_op jit(solution)/shard_map/sweep/pallas_call | solution.py:533
  (35 shorter events, 0.7 us)
Async XLA Ops:
  3.1 15.0 %copy-start = (bf16[8,8,16,256]{3,2,1,0:T(8,128)(2,1)S(1)}, bf16[8,8,16,256]{3,2,1,0:T(8,128)(2,1)}, u32[]{:S(2)}) copy-start(bf16[8,8,16,256]{3,2,1,0:T(8,128)(2,1)} %refs_2_.5) | copy-start | bytes 1572868
  3.1 7.6 %collective-permute-start.6 = (bf16[2,8,16,256]{3,2,1,0:T(8,128)(2,1)}, bf16[2,8,16,256]{3,2,1,0:T(8,128)(2,1)S(1)}, u32[]{:S(2)}, u32[]{:S(2)}) collective-permute-start(bf16[2,8,16,256]{3,2,1,0:T(8,128)(2,1)} %get-tuple-element.22), channel_id=1, source_target_pairs={{0,1},{1,0},{2,3},{3,2},{4,5},{5,4},{6,7},{7,6},{8,9},{9,8},{10,11... | collective-permute-start | bytes 393224 | tf_op jit(solution)/shard_map/ppermute | solution.py:497
  6.1 8.6 %collective-permute-start.8 = (bf16[2,8,16,256]{3,2,1,0:T(8,128)(2,1)}, bf16[2,8,16,256]{3,2,1,0:T(8,128)(2,1)S(1)}, u32[]{:S(2)}, u32[]{:S(2)}) collective-permute-start(bf16[2,8,16,256]{3,2,1,0:T(8,128)(2,1)} %get-tuple-element.23), channel_id=1, source_target_pairs={{0,1},{1,0},{2,3},{3,2},{4,5},{5,4},{6,7},{7,6},{8,9},{9,8},{10,11... | collective-permute-start | bytes 393224 | tf_op jit(solution)/shard_map/ppermute | solution.py:497
  6.1 10.5 %collective-permute-start.2 = (f32[56,128]{1,0:T(8,128)}, f32[56,128]{1,0:T(8,128)S(1)}, u32[]{:S(2)}, u32[]{:S(2)}) collective-permute-start(f32[56,128]{1,0:T(8,128)} %get-tuple-element.15), channel_id=1, source_target_pairs={{0,24},{4,28},{8,16},{12,20},{16,8},{20,12},{24,0},{28,4},{1,25},{... | collective-permute-start | bytes 86024 | tf_op jit(solution)/shard_map/ppermute | solution.py:497
  9.0 7.7 %collective-permute-start.1 = (f32[56,128]{1,0:T(8,128)}, f32[56,128]{1,0:T(8,128)S(1)}, u32[]{:S(2)}, u32[]{:S(2)}) collective-permute-start(f32[56,128]{1,0:T(8,128)} %get-tuple-element.15), channel_id=1, source_target_pairs={{0,16},{4,20},{8,24},{12,28},{16,0},{20,4},{24,8},{28,12},{1,17},{... | collective-permute-start | bytes 86024 | tf_op jit(solution)/shard_map/ppermute | solution.py:497
  9.5 7.2 %collective-permute-start = (f32[56,128]{1,0:T(8,128)}, f32[56,128]{1,0:T(8,128)S(1)}, u32[]{:S(2)}, u32[]{:S(2)}) collective-permute-start(f32[56,128]{1,0:T(8,128)} %get-tuple-element.15), channel_id=1, source_target_pairs={{0,8},{4,12},{8,0},{12,4},{16,24},{20,28},{24,16},{28,20},{1,9},{5... | collective-permute-start | bytes 86024 | tf_op jit(solution)/shard_map/ppermute | solution.py:497
  11.6 5.1 %copy-start.6 = (f32[56,128]{1,0:T(8,128)S(1)}, f32[56,128]{1,0:T(8,128)}, u32[]{:S(2)}) copy-start(f32[56,128]{1,0:T(8,128)} %get-tuple-element.15) | copy-start | bytes 86020
  11.6 11.7 %collective-permute-start.7 = (bf16[2,8,16,256]{3,2,1,0:T(8,128)(2,1)S(1)}, bf16[2,8,16,256]{3,2,1,0:T(8,128)(2,1)S(1)}, u32[]{:S(2)}, u32[]{:S(2)}) collective-permute-start(bf16[2,8,16,256]{3,2,1,0:T(8,128)(2,1)S(1)} %add.20), channel_id=1, source_target_pairs={{0,2},{1,3},{2,0},{3,1},{4,6},{5,7},{6,4},{7,5},{8,10},{9,11},{10,... | collective-permute-start | bytes 393224 | tf_op jit(solution)/shard_map/ppermute | solution.py:497
  15.6 9.3 %collective-permute-start.9 = (bf16[2,8,16,256]{3,2,1,0:T(8,128)(2,1)S(1)}, bf16[2,8,16,256]{3,2,1,0:T(8,128)(2,1)S(1)}, u32[]{:S(2)}, u32[]{:S(2)}) collective-permute-start(bf16[2,8,16,256]{3,2,1,0:T(8,128)(2,1)S(1)} %add.22), channel_id=1, source_target_pairs={{0,2},{1,3},{2,0},{3,1},{4,6},{5,7},{6,4},{7,5},{8,10},{9,11},{10,... | collective-permute-start | bytes 393224 | tf_op jit(solution)/shard_map/ppermute | solution.py:497
  16.7 1.4 %copy-start.2 = (f32[8,4,256]{2,1,0:T(4,128)S(1)}, f32[8,4,256]{2,1,0:T(4,128)}, u32[]{:S(2)}) copy-start(f32[8,4,256]{2,1,0:T(4,128)} %refs_3_.4) | copy-start | bytes 98308
  16.7 1.4 %collective-permute-start.3 = (f32[4,56,128]{2,1,0:T(8,128)S(1)}, f32[4,56,128]{2,1,0:T(8,128)S(1)}, u32[]{:S(2)}, u32[]{:S(2)}) collective-permute-start(f32[4,56,128]{2,1,0:T(8,128)S(1)} %pad_maximum_fusion.2.refs_0_.refs_4_), channel_id=1, source_target_pairs={{0,4},{4,0},{8,12},{12,8},{16,20},{20,16},{24,28},{28,24},{1,5},{5... | collective-permute-start | bytes 344072 | tf_op jit(solution)/shard_map/ppermute | solution.py:497
  19.1 10.4 %collective-permute-start.4 = (f32[8,16,256]{2,1,0:T(8,128)S(1)}, f32[8,16,256]{2,1,0:T(8,128)S(1)}, u32[]{:S(2)}, u32[]{:S(2)}) collective-permute-start(f32[8,16,256]{2,1,0:T(8,128)S(1)} %get-tuple-element.16.refs_6_.refs_2_), channel_id=1, source_target_pairs={{0,1},{1,0},{2,3},{3,2},{4,5},{5,4},{6,7},{7,6},{8,9},{9,8},{10,11... | collective-permute-start | bytes 393224 | tf_op jit(solution)/shard_map/ppermute | solution.py:497
  25.9 3.7 %copy-start.1 = (f32[32,8,64]{2,1,0:T(8,128)S(1)}, f32[32,8,64]{2,1,0:T(8,128)}, u32[]{:S(2)}) copy-start(f32[32,8,64]{2,1,0:T(8,128)} %refs_3_.5) | copy-start | bytes 196612
  25.9 3.7 %copy-start.3 = (s32[32]{0:T(128)S(1)}, s32[32]{0:T(128)}, u32[]{:S(2)}) copy-start(s32[32]{0:T(128)} %refs_0_.5) | copy-start | bytes 388
  25.9 3.7 %copy-start.4 = (s32[32]{0:T(128)S(1)}, s32[32]{0:T(128)}, u32[]{:S(2)}) copy-start(s32[32]{0:T(128)} %refs_1_.5) | copy-start | bytes 388
  25.9 3.7 %copy-start.5 = (s32[32]{0:T(128)S(1)}, s32[32]{0:T(128)}, u32[]{:S(2)}) copy-start(s32[32]{0:T(128)} %refs_2_.7) | copy-start | bytes 388
  25.9 11.7 %collective-permute-start.16 = (f32[2,256,128]{2,1,0:T(8,128)S(1)}, f32[2,256,128]{2,1,0:T(8,128)S(1)}, u32[]{:S(2)}, u32[]{:S(2)}) collective-permute-start(f32[2,256,128]{2,1,0:T(8,128)S(1)} %products.1.refs_4_), channel_id=1, source_target_pairs={{0,24},{4,28},{8,16},{12,20},{16,8},{20,12},{24,0},{28,4},{1,25},{... | collective-permute-start | bytes 786440 | tf_op jit(solution)/shard_map/ppermute | solution.py:497
  28.7 11.0 %collective-permute-start.15 = (f32[2,256,128]{2,1,0:T(8,128)S(1)}, f32[2,256,128]{2,1,0:T(8,128)S(1)}, u32[]{:S(2)}, u32[]{:S(2)}) collective-permute-start(f32[2,256,128]{2,1,0:T(8,128)S(1)} %products.1.refs_4_), channel_id=1, source_target_pairs={{0,16},{4,20},{8,24},{12,28},{16,0},{20,4},{24,8},{28,12},{1,17},{... | collective-permute-start | bytes 786440 | tf_op jit(solution)/shard_map/ppermute | solution.py:497
  29.2 10.7 %collective-permute-start.14 = (f32[2,256,128]{2,1,0:T(8,128)S(1)}, f32[2,256,128]{2,1,0:T(8,128)S(1)}, u32[]{:S(2)}, u32[]{:S(2)}) collective-permute-start(f32[2,256,128]{2,1,0:T(8,128)S(1)} %products.1.refs_4_), channel_id=1, source_target_pairs={{0,8},{4,12},{8,0},{12,4},{16,24},{20,28},{24,16},{28,20},{1,9},{5... | collective-permute-start | bytes 786440 | tf_op jit(solution)/shard_map/ppermute | solution.py:497
  29.5 7.3 %collective-permute-start.5 = (f32[8,16,256]{2,1,0:T(8,128)S(1)}, f32[8,16,256]{2,1,0:T(8,128)S(1)}, u32[]{:S(2)}, u32[]{:S(2)}) collective-permute-start(f32[8,16,256]{2,1,0:T(8,128)S(1)} %add.18), channel_id=1, source_target_pairs={{0,2},{1,3},{2,0},{3,1},{4,6},{5,7},{6,4},{7,5},{8,10},{9,11},{10,... | collective-permute-start | bytes 393224 | tf_op jit(solution)/shard_map/ppermute | solution.py:497
  40.0 11.7 %collective-permute-start.17 = (f32[4,2,256,128]{3,2,1,0:T(8,128)S(1)}, f32[4,2,256,128]{3,2,1,0:T(8,128)S(1)}, u32[]{:S(2)}, u32[]{:S(2)}) collective-permute-start(f32[4,2,256,128]{3,2,1,0:T(8,128)S(1)} %keep.1), channel_id=1, source_target_pairs={{0,4},{4,0},{8,12},{12,8},{16,20},{20,16},{24,28},{28,24},{1,5},{5... | collective-permute-start | bytes 3145736 | tf_op jit(solution)/shard_map/ppermute | solution.py:497
  40.1 7.3 %collective-permute-start.12 = (f32[2,128,128]{2,1,0:T(8,128)S(1)}, f32[2,128,128]{2,1,0:T(8,128)S(1)}, u32[]{:S(2)}, u32[]{:S(2)}) collective-permute-start(f32[2,128,128]{2,1,0:T(8,128)S(1)} %targets.1.refs_1_), channel_id=1, source_target_pairs={{0,24},{4,28},{8,16},{12,20},{16,8},{20,12},{24,0},{28,4},{1,25},{... | collective-permute-start | bytes 393224 | tf_op jit(solution)/shard_map/ppermute | solution.py:497
  41.7 8.0 %collective-permute-start.11 = (f32[2,128,128]{2,1,0:T(8,128)S(1)}, f32[2,128,128]{2,1,0:T(8,128)S(1)}, u32[]{:S(2)}, u32[]{:S(2)}) collective-permute-start(f32[2,128,128]{2,1,0:T(8,128)S(1)} %targets.1.refs_1_), channel_id=1, source_target_pairs={{0,16},{4,20},{8,24},{12,28},{16,0},{20,4},{24,8},{28,12},{1,17},{... | collective-permute-start | bytes 393224 | tf_op jit(solution)/shard_map/ppermute | solution.py:497
  43.1 6.6 %collective-permute-start.10 = (f32[2,128,128]{2,1,0:T(8,128)S(1)}, f32[2,128,128]{2,1,0:T(8,128)S(1)}, u32[]{:S(2)}, u32[]{:S(2)}) collective-permute-start(f32[2,128,128]{2,1,0:T(8,128)S(1)} %targets.1.refs_1_), channel_id=1, source_target_pairs={{0,8},{4,12},{8,0},{12,4},{16,24},{20,28},{24,16},{28,20},{1,9},{5... | collective-permute-start | bytes 393224 | tf_op jit(solution)/shard_map/ppermute | solution.py:497
  49.7 2.0 %collective-permute-start.13 = (f32[4,2,128,128]{3,2,1,0:T(8,128)S(1)}, f32[4,2,128,128]{3,2,1,0:T(8,128)S(1)}, u32[]{:S(2)}, u32[]{:S(2)}) collective-permute-start(f32[4,2,128,128]{3,2,1,0:T(8,128)S(1)} %pad_maximum_fusion.1), channel_id=1, source_target_pairs={{0,4},{4,0},{8,12},{12,8},{16,20},{20,16},{24,28},{28,24},{1,5},{5... | collective-permute-start | bytes 1572872 | tf_op jit(solution)/shard_map/ppermute | solution.py:497

commit v5 on v4

--- a/solution.py
+++ b/solution.py
@@ -107,8 +107,10 @@
         ref[i - low] = jnp.where(mine, coher_refs[i][0], jnp.zeros_like(coher_refs[i][0]))
 
 
-def keep_kernel(one_ref, out_ref):
-    out_ref[...] = one_ref[...]
+def keep_kernel(one_ref, *out_refs):
+    each = one_ref.shape[0] // len(out_refs)
+    for n, out_ref in enumerate(out_refs):
+        out_ref[...] = one_ref[n * each : (n + 1) * each]
 
 
 def fill_table(blocks, table, width):
@@ -136,10 +138,8 @@
     return [jnp.concatenate([rows[end * tiles + t : end * tiles + t + 1] for t in range(tiles)], axis=1) for end in (0, 1)]
 
 
-def fetch_columns(rows, hots, part, at):
-    count = rows.shape[0]
-    parts = rows.shape[1] // 128
-    wide = jnp.concatenate([rows[:, w * 128 : w * 128 + 128] for w in range(parts)], axis=0)
+def fetch_columns(wide, parts, hots, part, at):
+    count = wide.shape[0] // parts
     out = jnp.dot(split_rows(wide), hots[:, at], preferred_element_type=F32)
     out = out[: parts * count] + out[parts * count :]
     which = jnp.concatenate([part[:, at]] * (count // 8), axis=0)
@@ -160,7 +160,11 @@
     base = lax.axis_index("bl").astype(jnp.int32) * width
     fill_table([near_ref, far_ref], table, width)
     start = table[owned * 8 : (owned + SOLVED) * 8, :]
-    start_ref[...] = start
+    parts = start.shape[1] // 128
+    columns = [start[:, w * 128 : w * 128 + 128] for w in range(parts)]
+    for i in range(SOLVED):
+        start_ref[i] = jnp.concatenate([column[i * 8 : i * 8 + 8] for column in columns], axis=0)
+    wide = jnp.concatenate(columns, axis=0)
     pairs = [block_stations(ref.at[j], tiles, base) for ref in (near_ref, far_ref) for j in range(half)]
     step = min(8, chunks)
     for end in (0, 1):
@@ -173,7 +177,7 @@
             hots_ref[:, at] = hot.astype(BF16)
             turned_ref[at, :] = jnp.transpose(hot).astype(BF16)
             part_ref[:, at] = jnp.broadcast_to(here >> 7, (8, step * 128))
-            out = fetch_columns(start, hots_ref, part_ref, at)
+            out = fetch_columns(wide, parts, hots_ref, part_ref, at)
             for i in range(SOLVED):
                 for t in range(step):
                     ends_ref[i, end, (first + t) * 8 : (first + t) * 8 + 8, :] = out[i * 8 : i * 8 + 8, t * 128 : t * 128 + 128]
@@ -212,8 +216,33 @@
             part_ref[c, :, at] = jnp.concatenate([jnp.where(lane == x, y + vis, y) for x, y in enumerate(lanes)], axis=0)
 
 
-def summed(values):
-    return jnp.sum(values, axis=0, keepdims=True)
+class RowSums:
+    def __init__(self, ref, half):
+        self.ref, self.half, self.row, self.waiting = ref, half, 0, []
+
+    def put(self, *arrays):
+        for array in arrays:
+            rows = [array[at : at + 8] for at in range(0, array.shape[0], 8)]
+            self.waiting.append(functools.reduce(lambda x, y: x + y, rows))
+            if len(self.waiting) == 8:
+                self.ref[self.half, self.row : self.row + 8, :] = self.merged(self.waiting)
+                self.row, self.waiting = self.row + 8, []
+
+    @staticmethod
+    def merged(parts):
+        row = lax.broadcasted_iota(jnp.int32, parts[0].shape, 0)
+        low = (row & 4) == 0
+        parts = [
+            jnp.where(low, x, y) + pltpu.roll(jnp.where(low, y, x), 4, 0) for x, y in zip(parts[:4], parts[4:])
+        ]
+        for step in (2, 1):
+            low = (row & step) == 0
+            half = len(parts) // 2
+            parts = [
+                jnp.where(low, x + pltpu.roll(x, 8 - step, 0), y + pltpu.roll(y, step, 0))
+                for x, y in zip(parts[:half], parts[half:])
+            ]
+        return parts[0]
 
 
 def pair_list(low, high):
@@ -230,7 +259,7 @@
     baselines = first_ref.shape[2]
     for half in range(baselines // 128):
         at = pl.ds(half * 128, 128)
-        out = 0
+        sums = RowSums(out_ref, half)
         for i in range(low, high):
             coher = load_coher(solved_refs, i, at)
             gain_p, gain_q = [
@@ -241,34 +270,23 @@
             target = [(first_ref[2 * e, :, at] + model[e][0], first_ref[2 * e + 1, :, at] + model[e][1]) for e in range(4)]
             for u in range(4):
                 for v in range(4):
-                    value = mul_conj(target[u], coher[v])
-                    out_ref[half, out : out + 1, :] = summed(value[0])
-                    out_ref[half, out + 1 : out + 2, :] = summed(value[1])
-                    out += 2
+                    sums.put(*mul_conj(target[u], coher[v]))
 
 
 def product_kernel(*refs, low, high):
     *solved_refs, out_ref = refs
     for half in range(out_ref.shape[0]):
         at = pl.ds(half * 128, 128)
-        out = 0
+        sums = RowSums(out_ref, half)
         for i in range(low, high):
             coher = load_coher(solved_refs, i, at)
             for u, v in GRAM:
-                value = mul_conj(coher[u], coher[v])
-                out_ref[half, out : out + 1, :] = summed(value[0])
-                out += 1
-                if u != v:
-                    out_ref[half, out : out + 1, :] = summed(value[1])
-                    out += 1
+                sums.put(*mul_conj(coher[u], coher[v])[: 1 + (u != v)])
         for m, i in pair_list(low, high):
             coher, other = load_coher(solved_refs, i, at), load_coher(solved_refs, m, at)
             for u in range(4):
                 for v in range(4):
-                    value = mul_conj(other[u], coher[v])
-                    out_ref[half, out : out + 1, :] = summed(value[0])
-                    out_ref[half, out + 1 : out + 2, :] = summed(value[1])
-                    out += 2
+                    sums.put(*mul_conj(other[u], coher[v]))
 
 
 def own_kernel(first_ref, *refs):
@@ -294,8 +312,8 @@
     hots, turned, part, begin, start_ref, res_ref, own_ref = refs[:7]
     targets, refs = refs[7:9], refs[9:]
     pair, refs = refs[:2], refs[2:]
-    ends, values, state, m_now, k_now = refs[-5:]
-    refs = refs[:-5]
+    ends, values, state, sums, m_now, k_now = refs[-6:]
+    refs = refs[:-6]
     stages = [stage for stage in TARGETS if stage[1] <= low]
     earlier_moved = {m: (refs[s], m - stage[0]) for s, stage in enumerate(stages) for m in range(*stage)}
     refs = refs[len(stages) :]
@@ -305,7 +323,7 @@
     else:
         solved_ref, moved, out_ref = refs
     chunks = hots.shape[1] // 256
-    parts = start_ref.shape[1] // 128
+    parts = start_ref.shape[1] // 8
 
     def rows_at(pair, row):
         stride = pair[0].shape[0] // (chunks // 2)
@@ -316,7 +334,7 @@
         for end in (0, 1):
             for first in range(0, chunks if only is None else only, step):
                 at = pl.ds((end * chunks + first) * 128, step * 128)
-                out = fetch_columns(gain_now, hots, part, at)
+                out = fetch_columns(gain_now, parts, hots, part, at)
                 for t in range(step):
                     ends[end, (first + t) * 8 : (first + t) * 8 + 8, :] = out[:, t * 128 : t * 128 + 128]
 
@@ -415,15 +433,16 @@
         which = jnp.concatenate([part[...]] * 2, axis=0)
         wide = [split_rows(jnp.where(which == w, rows, jnp.zeros_like(rows))) for w in range(parts)]
         acc = jnp.dot(jnp.concatenate(wide, axis=0), turned[...], preferred_element_type=F32)
-        return jnp.concatenate([acc[w * 32 : w * 32 + 16] + acc[w * 32 + 16 : w * 32 + 32] for w in range(parts)], axis=1)
-
-    def solve(sums, gain_now, damp):
-        numer = sums[:8] + damp * gain_now
-        numer = as_matrix([numer[c : c + 1] for c in range(8)])
-        diag_a = sums[8:9] + damp
-        diag_d = sums[9:10] + damp
-        cross_r = sums[10:11]
-        cross_i = sums[11:12]
+        for w in range(parts):
+            sums[w * 16 : w * 16 + 16, :] = acc[w * 32 : w * 32 + 16] + acc[w * 32 + 16 : w * 32 + 32]
+
+    def solve(damp):
+        total_rows = [sums[pl.ds(c, parts, stride=16), :] for c in range(12)]
+        now = [state[pl.ds(c, parts, stride=8), :] for c in range(8)]
+        numer = as_matrix([total_rows[c] + damp * now[c] for c in range(8)])
+        diag_a = total_rows[8] + damp
+        diag_d = total_rows[9] + damp
+        cross_r, cross_i = total_rows[10:]
         scale = 1.0 / (diag_a * diag_d - cross_r * cross_r - cross_i * cross_i)
         rows = []
         for r in (0, 1):
@@ -432,7 +451,8 @@
             high = mul(x, (cross_r, cross_i))
             rows += [x[0] * diag_d - low[0], x[1] * diag_d - low[1]]
             rows += [y[0] * diag_a - high[0], y[1] * diag_a - high[1]]
-        return jnp.concatenate([value * scale for value in rows], axis=0)
+        for c in range(8):
+            state[pl.ds(c, parts, stride=8), :] = rows[c] * scale
 
     def add_change(i):
         for tile in range(tiles):
@@ -453,18 +473,19 @@
         gains_ref[...] = start_own[...]
         for i in range(low):
             ref, place = earlier_gains[i]
-            gains_ref[order_ref[i]] = ref[place, :, :width]
+            gains_ref[order_ref[i]] = ref[place, :8, :width]
     values[...] = jnp.zeros(values.shape, F32)
     for i in range(low, high):
         which = order_ref[i]
         damp = damping_ref[which].astype(F32) * factor
-        state[...] = start_ref[i * 8 : i * 8 + 8, :]
+        state[...] = start_ref[i]
         ends[...] = begin[i]
         prepare(i)
 
         def one_round():
             normal_terms()
-            state[...] = solve(station_sums(), state[...], damp)
+            station_sums()
+            solve(damp)
 
         def more(r, carry):
             one_round()
@@ -475,7 +496,7 @@
         one_round()
         fetch(state[...], tiles if i + 1 == SOLVED else None)
         if last:
-            gains_ref[which] = state[:, :width]
+            gains_ref[which] = state[:8, :width]
         else:
             solved_ref[i - low] = state[...]
         add_change(i)
@@ -584,7 +605,7 @@
             ((256 * chunks, 128), BF16),
             ((8, 256 * chunks), jnp.int32),
             ((SOLVED, 2, chunks * 8, 128), F32),
-            ((SOLVED * 8, count), F32),
+            ((SOLVED, count // 16, 128), F32),
             (gain_offsets.shape, F32),
         ],
         [solve_order, counts, damping],
@@ -623,8 +644,11 @@
             after=[value, hots],
         )
         near, near_x = chip_blocks(value, "bl", True)
-        [kx_near] = call(keep_kernel, "keep", [(kx_near.shape, F32)], [], [kx_near], after=[value])
-        products = flat(kx_near)
+        count_pieces = min(2, kx_near.shape[0])
+        shape = (kx_near.shape[0] // count_pieces,) + kx_near.shape[1:]
+        kept = call(keep_kernel, "keep", [(shape, F32)] * count_pieces, [], [kx_near], after=[value])
+        crossed = jnp.concatenate([exchange(piece, "bl", 1) for piece in kept], axis=0)
+        products = [kx_near.reshape(-1, 128), crossed.reshape(-1, 128)]
         targets = flat(near)
         last = high == SOLVED
         moved_shape = ((high - low, M_ROWS, chunks, 128), F32)
@@ -633,7 +657,7 @@
             "sweep",
             [(gain_offsets.shape, F32), (visibilities.shape, F32)]
             if last
-            else [((high - low, 8, count), F32), moved_shape, (visibilities.shape, F32)],
+            else [((high - low, count // 16, 128), F32), moved_shape, (visibilities.shape, F32)],
             [solve_order, counts, damping],
             [hots, turned, hot_part, ends, start, res, own]
             + targets
@@ -644,7 +668,8 @@
             + [
                 ((2, chunks * 8, 128), F32),
                 ((2, chunks * 16, 128), F32),
-                ((8, count), F32),
+                ((count // 16, 128), F32),
+                ((count // 8, 128), F32),
                 ((M_ROWS, chunks, 128), F32),
                 ((K_ROWS, chunks, 128), F32),
             ],

time: 61.2 us -> 56.7 us (0.926)
  waiting for transfers between devices: 22.6 us -> 19.1 us
  Pallas kernels: 15.5 us -> 13.5 us
    ppermute x18 -> x19, waiting for transfers between devices: 22.6 us -> 19.1 us  [exchange(): lax.ppermute(block, axis, [(i, i ^ mask) for i in range(lax.axis_size(axi...]
    pallas_call x7, Pallas kernels: 13.1 us -> 11.1 us  [call(): pl.pallas_call(body, out_shape=[jax.ShapeDtypeStruct(*shape) for shape in...]
    ppermute x18 -> x19, starting transfers between devices: 19.5 us -> 20 us  [exchange(): lax.ppermute(block, axis, [(i, i ^ mask) for i in range(lax.axis_size(axi...]
  transfers between devices with their start and end apart: 18 -> 19, of which waited for: 10 -> 10; matrix products, arithmetic and copies ran while one was open for 3% -> 4% of each run, Pallas kernels for 7% -> 7%
where the time goes in v5:
time: 56.7 us; the launch traced here: 55.7 us
  starting transfers between devices  20 us (35%)
  waiting for transfers between devices  19.1 us (34%)
  Pallas kernels  13.5 us (24%)
  other arithmetic  2.18 us (4%)
  between operations  0.87 us (2%)
    ppermute x19, starting transfers between devices, exchange(): lax.ppermute(block, axis, [(i, i ^ mask) for i in range(lax.axis_size(axi...  20 us
    ppermute x19, waiting for transfers between devices, exchange(): lax.ppermute(block, axis, [(i, i ^ mask) for i in range(lax.axis_size(axi...  19.1 us
    pallas_call x7, Pallas kernels, call(): pl.pallas_call(body, out_shape=[jax.ShapeDtypeStruct(*shape) for shape in...  11.1 us
    pallas_call x1, Pallas kernels, on_device(): pl.pallas_call(functools.partial(prep_kernel, owned=owned, per=per), out_...  2.41 us
    add x6, other arithmetic, butterfly_sums(): sums.append(sums[-1] + exchange(sums[-1], axis, 1 << len(sums) - 1))  1.99 us
  transfers between devices with their start and end apart: 19, of which 10 were waited for; matrix products, arithmetic and copies ran while one was open for 4% of the time, Pallas kernels for 7%

profile of v5, /device:TPU:0, one launch (start us, length us, event | category | flops | bytes accessed | tf_op | source)
XLA Modules:
  0.0 55.7 jit_solution(15143232867024237644)
XLA Ops:
  0.6 2.4 %prepare.1 = (f32[56,128]{1,0:T(8,128)}, bf16[2,8,16,256]{3,2,1,0:T(8,128)(2,1)}, bf16[2,8,16,256]{3,2,1,0:T(8,128)(2,1)}) custom-call(s32[32]{0:T(128)} %refs_0_.5, s32[2,256]{1,0:T(2,128)} %stations_ref.1, f32[32,8,64]{2,1,0:T(8,128)} %refs_3_.5, bf16[8,8,16,256]{3,2,1,0:T(8,128)(2,1)} %refs_2_.5, bf16[8,8,16,256]{3,2,1,0:T(8,128)(2,1)} %refs_2_.5, ...), custom_call_target="tpu_custom_call" | custom-call | tf_op jit(solution)/shard_map/prepare/pallas_call | solution.py:572
  3.0 3.0 %collective-permute-start.6 = (bf16[2,8,16,256]{3,2,1,0:T(8,128)(2,1)}, bf16[2,8,16,256]{3,2,1,0:T(8,128)(2,1)S(1)}, u32[]{:S(2)}, u32[]{:S(2)}) collective-permute-start(bf16[2,8,16,256]{3,2,1,0:T(8,128)(2,1)} %get-tuple-element.24), channel_id=1, source_target_pairs={{0,1},{1,0},{2,3},{3,2},{4,5},{5,4},{6,7},{7,6},{8,9},{9,8},{10,11... | collective-permute-start | bytes 393224 | tf_op jit(solution)/shard_map/ppermute | solution.py:518
  6.1 1.9 %collective-permute-start = (f32[56,128]{1,0:T(8,128)}, f32[56,128]{1,0:T(8,128)S(1)}, u32[]{:S(2)}, u32[]{:S(2)}) collective-permute-start(f32[56,128]{1,0:T(8,128)} %get-tuple-element.17), channel_id=1, source_target_pairs={{0,8},{4,12},{8,0},{12,4},{16,24},{20,28},{24,16},{28,20},{1,9},{5... | collective-permute-start | bytes 86024 | tf_op jit(solution)/shard_map/ppermute | solution.py:518
  8.0 1.5 %collective-permute-start.1 = (f32[56,128]{1,0:T(8,128)}, f32[56,128]{1,0:T(8,128)S(1)}, u32[]{:S(2)}, u32[]{:S(2)}) collective-permute-start(f32[56,128]{1,0:T(8,128)} %get-tuple-element.17), channel_id=1, source_target_pairs={{0,16},{4,20},{8,24},{12,28},{16,0},{20,4},{24,8},{28,12},{1,17},{... | collective-permute-start | bytes 86024 | tf_op jit(solution)/shard_map/ppermute | solution.py:518
  9.6 1.0 %collective-permute-done.6 = bf16[2,8,16,256]{3,2,1,0:T(8,128)(2,1)S(1)} collective-permute-done((bf16[2,8,16,256]{3,2,1,0:T(8,128)(2,1)}, bf16[2,8,16,256]{3,2,1,0:T(8,128)(2,1)S(1)}, u32[]{:S(2)}, u32[]{:S(2)}) %collective-permute-start.6) | collective-permute-done | bytes 131104 | tf_op jit(solution)/shard_map/ppermute | solution.py:518
  10.6 0.9 %add.20 = bf16[2,8,16,256]{3,2,1,0:T(8,128)(2,1)S(1)} add(bf16[2,8,16,256]{3,2,1,0:T(8,128)(2,1)} %get-tuple-element.24, bf16[2,8,16,256]{3,2,1,0:T(8,128)(2,1)S(1)} %collective-permute-done.6) | non-fusion elementwise | flops 65536 | bytes 393216 | tf_op jit(solution)/shard_map/add | solution.py:524
  11.6 3.1 %collective-permute-start.7 = (bf16[2,8,16,256]{3,2,1,0:T(8,128)(2,1)S(1)}, bf16[2,8,16,256]{3,2,1,0:T(8,128)(2,1)S(1)}, u32[]{:S(2)}, u32[]{:S(2)}) collective-permute-start(bf16[2,8,16,256]{3,2,1,0:T(8,128)(2,1)S(1)} %add.20), channel_id=1, source_target_pairs={{0,2},{1,3},{2,0},{3,1},{4,6},{5,7},{6,4},{7,5},{8,10},{9,11},{10,... | collective-permute-start | bytes 393224 | tf_op jit(solution)/shard_map/ppermute | solution.py:518
  14.7 0.9 %add.22 = bf16[2,8,16,256]{3,2,1,0:T(8,128)(2,1)S(1)} add(bf16[2,8,16,256]{3,2,1,0:T(8,128)(2,1)} %get-tuple-element.25, bf16[2,8,16,256]{3,2,1,0:T(8,128)(2,1)S(1)} %collective-permute-done.8) | non-fusion elementwise | flops 65536 | bytes 393216 | tf_op jit(solution)/shard_map/add | solution.py:524
  15.6 1.0 %collective-permute-start.9 = (bf16[2,8,16,256]{3,2,1,0:T(8,128)(2,1)S(1)}, bf16[2,8,16,256]{3,2,1,0:T(8,128)(2,1)S(1)}, u32[]{:S(2)}, u32[]{:S(2)}) collective-permute-start(bf16[2,8,16,256]{3,2,1,0:T(8,128)(2,1)S(1)} %add.22), channel_id=1, source_target_pairs={{0,2},{1,3},{2,0},{3,1},{4,6},{5,7},{6,4},{7,5},{8,10},{9,11},{10,... | collective-permute-start | bytes 393224 | tf_op jit(solution)/shard_map/ppermute | solution.py:518
  16.8 1.3 %collective-permute-done.3.refs_1_.refs_5_ = f32[4,56,128]{2,1,0:T(8,128)S(1)} collective-permute-done((f32[4,56,128]{2,1,0:T(8,128)S(1)}, f32[4,56,128]{2,1,0:T(8,128)S(1)}, u32[]{:S(2)}, u32[]{:S(2)}) %collective-permute-start.3) | collective-permute-done | bytes 114720 | tf_op jit(solution)/shard_map/ppermute | solution.py:518
  18.1 1.0 %first_model.1 = (f32[8,16,256]{2,1,0:T(8,128)S(1)}, f32[32,512]{1,0:T(8,128)S(1)}) custom-call(f32[4,56,128]{2,1,0:T(8,128)S(1)} %pad_maximum_fusion.3.refs_0_.refs_4_, f32[4,56,128]{2,1,0:T(8,128)S(1)} %collective-permute-done.3.refs_1_.refs_5_, bf16[8,8,16,256]{3,2,1,0:T(8,128)(2,1)S(1)} %copy-done, f32[8,4,256]{2,1,0:T(4,128)S(1)} %copy-done.2), custom_call_target="tpu_custom_call" | custom-call | tf_op jit(solution)/shard_map/first_model/pallas_call | solution.py:554
  19.1 1.4 %collective-permute-start.4 = (f32[8,16,256]{2,1,0:T(8,128)S(1)}, f32[8,16,256]{2,1,0:T(8,128)S(1)}, u32[]{:S(2)}, u32[]{:S(2)}) collective-permute-start(f32[8,16,256]{2,1,0:T(8,128)S(1)} %get-tuple-element.18.refs_6_.refs_2_), channel_id=1, source_target_pairs={{0,1},{1,0},{2,3},{3,2},{4,5},{5,4},{6,7},{7,6},{8,9},{9,8},{10,11... | collective-permute-start | bytes 393224 | tf_op jit(solution)/shard_map/ppermute | solution.py:518
  20.4 2.8 %collective-permute-done.7 = bf16[2,8,16,256]{3,2,1,0:T(8,128)(2,1)S(1)} collective-permute-done((bf16[2,8,16,256]{3,2,1,0:T(8,128)(2,1)S(1)}, bf16[2,8,16,256]{3,2,1,0:T(8,128)(2,1)S(1)}, u32[]{:S(2)}, u32[]{:S(2)}) %collective-permute-start.7) | collective-permute-done | bytes 131104 | tf_op jit(solution)/shard_map/ppermute | solution.py:518
  23.2 1.7 %collective-permute-done.9 = bf16[2,8,16,256]{3,2,1,0:T(8,128)(2,1)S(1)} collective-permute-done((bf16[2,8,16,256]{3,2,1,0:T(8,128)(2,1)S(1)}, bf16[2,8,16,256]{3,2,1,0:T(8,128)(2,1)S(1)}, u32[]{:S(2)}, u32[]{:S(2)}) %collective-permute-start.9) | collective-permute-done | bytes 131104 | tf_op jit(solution)/shard_map/ppermute | solution.py:518
  24.9 0.8 %products.1.refs_4_ = f32[2,256,128]{2,1,0:T(8,128)S(1)} custom-call(bf16[2,8,16,256]{3,2,1,0:T(8,128)(2,1)S(1)} %add.21.refs_1_.refs_0_.refs_2_, bf16[2,8,16,256]{3,2,1,0:T(8,128)(2,1)S(1)} %add.23.refs_2_.refs_1_.refs_3_, f32[8,16,256]{2,1,0:T(8,128)S(1)} %get-tuple-element.18.refs_6_.refs_2_), custom_call_target="tpu_custom_call" | custom-call | tf_op jit(solution)/shard_map/products/pallas_call | solution.py:554
  25.8 1.7 %collective-permute-start.14 = (f32[2,256,128]{2,1,0:T(8,128)S(1)}, f32[2,256,128]{2,1,0:T(8,128)S(1)}, u32[]{:S(2)}, u32[]{:S(2)}) collective-permute-start(f32[2,256,128]{2,1,0:T(8,128)S(1)} %products.1.refs_4_), channel_id=1, source_target_pairs={{0,8},{4,12},{8,0},{12,4},{16,24},{20,28},{24,16},{28,20},{1,9},{5... | collective-permute-start | bytes 786440 | tf_op jit(solution)/shard_map/ppermute | solution.py:518
  27.5 1.5 %collective-permute-start.15 = (f32[2,256,128]{2,1,0:T(8,128)S(1)}, f32[2,256,128]{2,1,0:T(8,128)S(1)}, u32[]{:S(2)}, u32[]{:S(2)}) collective-permute-start(f32[2,256,128]{2,1,0:T(8,128)S(1)} %products.1.refs_4_), channel_id=1, source_target_pairs={{0,16},{4,20},{8,24},{12,28},{16,0},{20,4},{24,8},{28,12},{1,17},{... | collective-permute-start | bytes 786440 | tf_op jit(solution)/shard_map/ppermute | solution.py:518
  29.1 0.3 collective-permute-start.16
  29.5 1.4 %lookup.1 = (bf16[128,4096]{1,0:T(8,128)(2,1)S(1)}, bf16[4096,128]{1,0:T(8,128)(2,1)S(1)}, s32[8,4096]{1,0:T(8,128)S(1)}, f32[4,2,128,128]{3,2,1,0:T(8,128)S(1)}...) custom-call(s32[32]{0:T(128)S(1)} %copy-done.3, s32[32]{0:T(128)S(1)} %copy-done.4, s32[32]{0:T(128)S(1)} %copy-done.5, ...), custom_call_target="tpu_custom_call" | custom-call | tf_op jit(solution)/shard_map/lookup/pallas_call | solution.py:554
  30.9 5.8 %collective-permute-done.5 = f32[8,16,256]{2,1,0:T(8,128)S(1)} collective-permute-done((f32[8,16,256]{2,1,0:T(8,128)S(1)}, f32[8,16,256]{2,1,0:T(8,128)S(1)}, u32[]{:S(2)}, u32[]{:S(2)}) %collective-permute-start.5) | collective-permute-done | bytes 131104 | tf_op jit(solution)/shard_map/ppermute | solution.py:518
  36.7 0.6 %targets.1.refs_1_ = f32[2,128,128]{2,1,0:T(8,128)S(1)} custom-call(f32[8,16,256]{2,1,0:T(8,128)S(1)} %add.19.refs_0_, f32[32,512]{1,0:T(8,128)S(1)} %get-tuple-element.28.refs_1_, bf16[2,8,16,256]{3,2,1,0:T(8,128)(2,1)S(1)} %add.21.refs_1_.refs_0_.refs_2_, bf16[2,8,16,256]{3,2,1,0:T(8,128)(2,1)S(1)} %add.23.refs_2_.refs_1_.refs_3_, ...), custom_call_target="tpu_custom_call" | custom-call | tf_op jit(solution)/shard_map/targets/pallas_call | solution.py:554
  37.4 1.7 %collective-permute-start.10 = (f32[2,128,128]{2,1,0:T(8,128)S(1)}, f32[2,128,128]{2,1,0:T(8,128)S(1)}, u32[]{:S(2)}, u32[]{:S(2)}) collective-permute-start(f32[2,128,128]{2,1,0:T(8,128)S(1)} %targets.1.refs_1_), channel_id=1, source_target_pairs={{0,8},{4,12},{8,0},{12,4},{16,24},{20,28},{24,16},{28,20},{1,9},{5... | collective-permute-start | bytes 393224 | tf_op jit(solution)/shard_map/ppermute | solution.py:518
  39.1 1.5 %collective-permute-start.11 = (f32[2,128,128]{2,1,0:T(8,128)S(1)}, f32[2,128,128]{2,1,0:T(8,128)S(1)}, u32[]{:S(2)}, u32[]{:S(2)}) collective-permute-start(f32[2,128,128]{2,1,0:T(8,128)S(1)} %targets.1.refs_1_), channel_id=1, source_target_pairs={{0,16},{4,20},{8,24},{12,28},{16,0},{20,4},{24,8},{28,12},{1,17},{... | collective-permute-start | bytes 393224 | tf_op jit(solution)/shard_map/ppermute | solution.py:518
  40.7 0.3 collective-permute-start.12
  41.0 0.4 collective-permute-done.16
  41.6 0.5 collective-permute-start.18
  42.1 0.8 %collective-permute-done.10 = f32[2,128,128]{2,1,0:T(8,128)S(1)} collective-permute-done((f32[2,128,128]{2,1,0:T(8,128)S(1)}, f32[2,128,128]{2,1,0:T(8,128)S(1)}, u32[]{:S(2)}, u32[]{:S(2)}) %collective-permute-start.10) | collective-permute-done | bytes 131104 | tf_op jit(solution)/shard_map/ppermute | solution.py:518
  42.9 1.3 %collective-permute-done.11 = f32[2,128,128]{2,1,0:T(8,128)S(1)} collective-permute-done((f32[2,128,128]{2,1,0:T(8,128)S(1)}, f32[2,128,128]{2,1,0:T(8,128)S(1)}, u32[]{:S(2)}, u32[]{:S(2)}) %collective-permute-start.11) | collective-permute-done | bytes 131104 | tf_op jit(solution)/shard_map/ppermute | solution.py:518
  44.1 2.4 %collective-permute-done.12 = f32[2,128,128]{2,1,0:T(8,128)S(1)} collective-permute-done((f32[2,128,128]{2,1,0:T(8,128)S(1)}, f32[2,128,128]{2,1,0:T(8,128)S(1)}, u32[]{:S(2)}, u32[]{:S(2)}) %collective-permute-start.12) | collective-permute-done | bytes 131104 | tf_op jit(solution)/shard_map/ppermute | solution.py:518
  46.7 0.1 own_channels.1
  46.9 1.7 %collective-permute-done.13 = f32[4,2,128,128]{3,2,1,0:T(8,128)S(1)} collective-permute-done((f32[4,2,128,128]{3,2,1,0:T(8,128)S(1)}, f32[4,2,128,128]{3,2,1,0:T(8,128)S(1)}, u32[]{:S(2)}, u32[]{:S(2)}) %collective-permute-start.13) | collective-permute-done | bytes 524320 | tf_op jit(solution)/shard_map/ppermute | solution.py:518
  48.6 7.1 %sweep.1 = (f32[32,8,64]{2,1,0:T(8,128)}, f32[8,4,256]{2,1,0:T(4,128)}) custom-call(s32[32]{0:T(128)S(1)} %copy-done.3, s32[32]{0:T(128)S(1)} %copy-done.4, s32[32]{0:T(128)S(1)} %copy-done.5, bf16[128,4096]{1,0:T(8,128)(2,1)S(1)} %get-tuple-element.19.refs_5_.refs_3_, bf16[4096,128]{1,0:T(8,128)(2,1)S(1)} %get-tuple-element.20.refs_4_, ...), custom_call_target="tpu_custom_call" | custom-call | tf_op jit(solution)/shard_map/sweep/pallas_call | solution.py:554
  (38 shorter events, 0.9 us)
Async XLA Ops:
  3.0 15.0 %copy-start = (bf16[8,8,16,256]{3,2,1,0:T(8,128)(2,1)S(1)}, bf16[8,8,16,256]{3,2,1,0:T(8,128)(2,1)}, u32[]{:S(2)}) copy-start(bf16[8,8,16,256]{3,2,1,0:T(8,128)(2,1)} %refs_2_.5) | copy-start | bytes 1572868
  3.0 7.6 %collective-permute-start.6 = (bf16[2,8,16,256]{3,2,1,0:T(8,128)(2,1)}, bf16[2,8,16,256]{3,2,1,0:T(8,128)(2,1)S(1)}, u32[]{:S(2)}, u32[]{:S(2)}) collective-permute-start(bf16[2,8,16,256]{3,2,1,0:T(8,128)(2,1)} %get-tuple-element.24), channel_id=1, source_target_pairs={{0,1},{1,0},{2,3},{3,2},{4,5},{5,4},{6,7},{7,6},{8,9},{9,8},{10,11... | collective-permute-start | bytes 393224 | tf_op jit(solution)/shard_map/ppermute | solution.py:518
  6.1 8.6 %collective-permute-start.8 = (bf16[2,8,16,256]{3,2,1,0:T(8,128)(2,1)}, bf16[2,8,16,256]{3,2,1,0:T(8,128)(2,1)S(1)}, u32[]{:S(2)}, u32[]{:S(2)}) collective-permute-start(bf16[2,8,16,256]{3,2,1,0:T(8,128)(2,1)} %get-tuple-element.25), channel_id=1, source_target_pairs={{0,1},{1,0},{2,3},{3,2},{4,5},{5,4},{6,7},{7,6},{8,9},{9,8},{10,11... | collective-permute-start | bytes 393224 | tf_op jit(solution)/shard_map/ppermute | solution.py:518
  6.1 10.5 %collective-permute-start = (f32[56,128]{1,0:T(8,128)}, f32[56,128]{1,0:T(8,128)S(1)}, u32[]{:S(2)}, u32[]{:S(2)}) collective-permute-start(f32[56,128]{1,0:T(8,128)} %get-tuple-element.17), channel_id=1, source_target_pairs={{0,8},{4,12},{8,0},{12,4},{16,24},{20,28},{24,16},{28,20},{1,9},{5... | collective-permute-start | bytes 86024 | tf_op jit(solution)/shard_map/ppermute | solution.py:518
  8.0 8.6 %collective-permute-start.1 = (f32[56,128]{1,0:T(8,128)}, f32[56,128]{1,0:T(8,128)S(1)}, u32[]{:S(2)}, u32[]{:S(2)}) collective-permute-start(f32[56,128]{1,0:T(8,128)} %get-tuple-element.17), channel_id=1, source_target_pairs={{0,16},{4,20},{8,24},{12,28},{16,0},{20,4},{24,8},{28,12},{1,17},{... | collective-permute-start | bytes 86024 | tf_op jit(solution)/shard_map/ppermute | solution.py:518
  9.5 7.1 %collective-permute-start.2 = (f32[56,128]{1,0:T(8,128)}, f32[56,128]{1,0:T(8,128)S(1)}, u32[]{:S(2)}, u32[]{:S(2)}) collective-permute-start(f32[56,128]{1,0:T(8,128)} %get-tuple-element.17), channel_id=1, source_target_pairs={{0,24},{4,28},{8,16},{12,20},{16,8},{20,12},{24,0},{28,4},{1,25},{... | collective-permute-start | bytes 86024 | tf_op jit(solution)/shard_map/ppermute | solution.py:518
  11.5 5.1 %copy-start.6 = (f32[56,128]{1,0:T(8,128)S(1)}, f32[56,128]{1,0:T(8,128)}, u32[]{:S(2)}) copy-start(f32[56,128]{1,0:T(8,128)} %get-tuple-element.17) | copy-start | bytes 86020
  11.6 11.7 %collective-permute-start.7 = (bf16[2,8,16,256]{3,2,1,0:T(8,128)(2,1)S(1)}, bf16[2,8,16,256]{3,2,1,0:T(8,128)(2,1)S(1)}, u32[]{:S(2)}, u32[]{:S(2)}) collective-permute-start(bf16[2,8,16,256]{3,2,1,0:T(8,128)(2,1)S(1)} %add.20), channel_id=1, source_target_pairs={{0,2},{1,3},{2,0},{3,1},{4,6},{5,7},{6,4},{7,5},{8,10},{9,11},{10,... | collective-permute-start | bytes 393224 | tf_op jit(solution)/shard_map/ppermute | solution.py:518
  15.6 9.3 %collective-permute-start.9 = (bf16[2,8,16,256]{3,2,1,0:T(8,128)(2,1)S(1)}, bf16[2,8,16,256]{3,2,1,0:T(8,128)(2,1)S(1)}, u32[]{:S(2)}, u32[]{:S(2)}) collective-permute-start(bf16[2,8,16,256]{3,2,1,0:T(8,128)(2,1)S(1)} %add.22), channel_id=1, source_target_pairs={{0,2},{1,3},{2,0},{3,1},{4,6},{5,7},{6,4},{7,5},{8,10},{9,11},{10,... | collective-permute-start | bytes 393224 | tf_op jit(solution)/shard_map/ppermute | solution.py:518
  16.6 1.4 %copy-start.2 = (f32[8,4,256]{2,1,0:T(4,128)S(1)}, f32[8,4,256]{2,1,0:T(4,128)}, u32[]{:S(2)}) copy-start(f32[8,4,256]{2,1,0:T(4,128)} %refs_3_.4) | copy-start | bytes 98308
  16.7 1.4 %collective-permute-start.3 = (f32[4,56,128]{2,1,0:T(8,128)S(1)}, f32[4,56,128]{2,1,0:T(8,128)S(1)}, u32[]{:S(2)}, u32[]{:S(2)}) collective-permute-start(f32[4,56,128]{2,1,0:T(8,128)S(1)} %pad_maximum_fusion.3.refs_0_.refs_4_), channel_id=1, source_target_pairs={{0,4},{4,0},{8,12},{12,8},{16,20},{20,16},{24,28},{28,24},{1,5},{5... | collective-permute-start | bytes 344072 | tf_op jit(solution)/shard_map/ppermute | solution.py:518
  19.1 10.3 %collective-permute-start.4 = (f32[8,16,256]{2,1,0:T(8,128)S(1)}, f32[8,16,256]{2,1,0:T(8,128)S(1)}, u32[]{:S(2)}, u32[]{:S(2)}) collective-permute-start(f32[8,16,256]{2,1,0:T(8,128)S(1)} %get-tuple-element.18.refs_6_.refs_2_), channel_id=1, source_target_pairs={{0,1},{1,0},{2,3},{3,2},{4,5},{5,4},{6,7},{7,6},{8,9},{9,8},{10,11... | collective-permute-start | bytes 393224 | tf_op jit(solution)/shard_map/ppermute | solution.py:518
  25.7 3.7 %copy-start.1 = (f32[32,8,64]{2,1,0:T(8,128)S(1)}, f32[32,8,64]{2,1,0:T(8,128)}, u32[]{:S(2)}) copy-start(f32[32,8,64]{2,1,0:T(8,128)} %refs_3_.5) | copy-start | bytes 196612
  25.8 3.7 %copy-start.3 = (s32[32]{0:T(128)S(1)}, s32[32]{0:T(128)}, u32[]{:S(2)}) copy-start(s32[32]{0:T(128)} %refs_0_.5) | copy-start | bytes 388
  25.8 3.7 %copy-start.4 = (s32[32]{0:T(128)S(1)}, s32[32]{0:T(128)}, u32[]{:S(2)}) copy-start(s32[32]{0:T(128)} %refs_1_.5) | copy-start | bytes 388
  25.8 3.7 %copy-start.5 = (s32[32]{0:T(128)S(1)}, s32[32]{0:T(128)}, u32[]{:S(2)}) copy-start(s32[32]{0:T(128)} %refs_2_.7) | copy-start | bytes 388
  25.8 14.9 %collective-permute-start.14 = (f32[2,256,128]{2,1,0:T(8,128)S(1)}, f32[2,256,128]{2,1,0:T(8,128)S(1)}, u32[]{:S(2)}, u32[]{:S(2)}) collective-permute-start(f32[2,256,128]{2,1,0:T(8,128)S(1)} %products.1.refs_4_), channel_id=1, source_target_pairs={{0,8},{4,12},{8,0},{12,4},{16,24},{20,28},{24,16},{28,20},{1,9},{5... | collective-permute-start | bytes 786440 | tf_op jit(solution)/shard_map/ppermute | solution.py:518
  27.5 13.4 %collective-permute-start.15 = (f32[2,256,128]{2,1,0:T(8,128)S(1)}, f32[2,256,128]{2,1,0:T(8,128)S(1)}, u32[]{:S(2)}, u32[]{:S(2)}) collective-permute-start(f32[2,256,128]{2,1,0:T(8,128)S(1)} %products.1.refs_4_), channel_id=1, source_target_pairs={{0,16},{4,20},{8,24},{12,28},{16,0},{20,4},{24,8},{28,12},{1,17},{... | collective-permute-start | bytes 786440 | tf_op jit(solution)/shard_map/ppermute | solution.py:518
  29.1 12.3 %collective-permute-start.16 = (f32[2,256,128]{2,1,0:T(8,128)S(1)}, f32[2,256,128]{2,1,0:T(8,128)S(1)}, u32[]{:S(2)}, u32[]{:S(2)}) collective-permute-start(f32[2,256,128]{2,1,0:T(8,128)S(1)} %products.1.refs_4_), channel_id=1, source_target_pairs={{0,24},{4,28},{8,16},{12,20},{16,8},{20,12},{24,0},{28,4},{1,25},{... | collective-permute-start | bytes 786440 | tf_op jit(solution)/shard_map/ppermute | solution.py:518
  29.4 7.3 %collective-permute-start.5 = (f32[8,16,256]{2,1,0:T(8,128)S(1)}, f32[8,16,256]{2,1,0:T(8,128)S(1)}, u32[]{:S(2)}, u32[]{:S(2)}) collective-permute-start(f32[8,16,256]{2,1,0:T(8,128)S(1)} %add.18), channel_id=1, source_target_pairs={{0,2},{1,3},{2,0},{3,1},{4,6},{5,7},{6,4},{7,5},{8,10},{9,11},{10,... | collective-permute-start | bytes 393224 | tf_op jit(solution)/shard_map/ppermute | solution.py:518
  37.4 5.5 %collective-permute-start.10 = (f32[2,128,128]{2,1,0:T(8,128)S(1)}, f32[2,128,128]{2,1,0:T(8,128)S(1)}, u32[]{:S(2)}, u32[]{:S(2)}) collective-permute-start(f32[2,128,128]{2,1,0:T(8,128)S(1)} %targets.1.refs_1_), channel_id=1, source_target_pairs={{0,8},{4,12},{8,0},{12,4},{16,24},{20,28},{24,16},{28,20},{1,9},{5... | collective-permute-start | bytes 393224 | tf_op jit(solution)/shard_map/ppermute | solution.py:518
  39.1 5.0 %collective-permute-start.11 = (f32[2,128,128]{2,1,0:T(8,128)S(1)}, f32[2,128,128]{2,1,0:T(8,128)S(1)}, u32[]{:S(2)}, u32[]{:S(2)}) collective-permute-start(f32[2,128,128]{2,1,0:T(8,128)S(1)} %targets.1.refs_1_), channel_id=1, source_target_pairs={{0,16},{4,20},{8,24},{12,28},{16,0},{20,4},{24,8},{28,12},{1,17},{... | collective-permute-start | bytes 393224 | tf_op jit(solution)/shard_map/ppermute | solution.py:518
  40.7 5.9 %collective-permute-start.12 = (f32[2,128,128]{2,1,0:T(8,128)S(1)}, f32[2,128,128]{2,1,0:T(8,128)S(1)}, u32[]{:S(2)}, u32[]{:S(2)}) collective-permute-start(f32[2,128,128]{2,1,0:T(8,128)S(1)} %targets.1.refs_1_), channel_id=1, source_target_pairs={{0,24},{4,28},{8,16},{12,20},{16,8},{20,12},{24,0},{28,4},{1,25},{... | collective-permute-start | bytes 393224 | tf_op jit(solution)/shard_map/ppermute | solution.py:518
  41.5 5.3 %collective-permute-start.17 = (f32[2,2,256,128]{3,2,1,0:T(8,128)S(1)}, f32[2,2,256,128]{3,2,1,0:T(8,128)S(1)}, u32[]{:S(2)}, u32[]{:S(2)}) collective-permute-start(f32[2,2,256,128]{3,2,1,0:T(8,128)S(1)} %get-tuple-element.29), channel_id=1, source_target_pairs={{0,4},{4,0},{8,12},{12,8},{16,20},{20,16},{24,28},{28,24},{1,5},{5... | collective-permute-start | bytes 1572872 | tf_op jit(solution)/shard_map/ppermute | solution.py:518
  41.6 5.2 %collective-permute-start.18 = (f32[2,2,256,128]{3,2,1,0:T(8,128)S(1)}, f32[2,2,256,128]{3,2,1,0:T(8,128)S(1)}, u32[]{:S(2)}, u32[]{:S(2)}) collective-permute-start(f32[2,2,256,128]{3,2,1,0:T(8,128)S(1)} %get-tuple-element.30), channel_id=1, source_target_pairs={{0,4},{4,0},{8,12},{12,8},{16,20},{20,16},{24,28},{28,24},{1,5},{5... | collective-permute-start | bytes 1572872 | tf_op jit(solution)/shard_map/ppermute | solution.py:518
  46.6 2.0 %collective-permute-start.13 = (f32[4,2,128,128]{3,2,1,0:T(8,128)S(1)}, f32[4,2,128,128]{3,2,1,0:T(8,128)S(1)}, u32[]{:S(2)}, u32[]{:S(2)}) collective-permute-start(f32[4,2,128,128]{3,2,1,0:T(8,128)S(1)} %pad_maximum_fusion.2), channel_id=1, source_target_pairs={{0,4},{4,0},{8,12},{12,8},{16,20},{20,16},{24,28},{28,24},{1,5},{5... | collective-permute-start | bytes 1572872 | tf_op jit(solution)/shard_map/ppermute | solution.py:518

commit v6 on v5

--- a/solution.py
+++ b/solution.py
@@ -217,15 +217,18 @@
 
 
 class RowSums:
-    def __init__(self, ref, half):
-        self.ref, self.half, self.row, self.waiting = ref, half, 0, []
+    def __init__(self, ref, half, plus=None):
+        self.ref, self.half, self.row, self.waiting, self.plus = ref, half, 0, [], plus
 
     def put(self, *arrays):
         for array in arrays:
             rows = [array[at : at + 8] for at in range(0, array.shape[0], 8)]
             self.waiting.append(functools.reduce(lambda x, y: x + y, rows))
             if len(self.waiting) == 8:
-                self.ref[self.half, self.row : self.row + 8, :] = self.merged(self.waiting)
+                value = self.merged(self.waiting)
+                if self.plus is not None:
+                    value += self.plus[self.half, self.row : self.row + 8, :]
+                self.ref[self.half, self.row : self.row + 8, :] = value
                 self.row, self.waiting = self.row + 8, []
 
     @staticmethod
@@ -254,9 +257,9 @@
     return as_matrix([ref[i - low, c, :, at].astype(F32) for c in range(8)])
 
 
-def target_kernel(first_ref, begin_ref, *refs, low, high):
+def own_target_kernel(begin_ref, *refs, low, high):
     *solved_refs, out_ref = refs
-    baselines = first_ref.shape[2]
+    baselines = begin_ref.shape[1] // 2
     for half in range(baselines // 128):
         at = pl.ds(half * 128, 128)
         sums = RowSums(out_ref, half)
@@ -267,7 +270,19 @@
                 for end in (0, 1)
             ]
             model = apply_gains(gain_p, coher, gain_q)
-            target = [(first_ref[2 * e, :, at] + model[e][0], first_ref[2 * e + 1, :, at] + model[e][1]) for e in range(4)]
+            for u in range(4):
+                for v in range(4):
+                    sums.put(*mul_conj(model[u], coher[v]))
+
+
+def target_kernel(first_ref, plus_ref, *refs, low, high):
+    *solved_refs, out_ref = refs
+    for half in range(first_ref.shape[2] // 128):
+        at = pl.ds(half * 128, 128)
+        sums = RowSums(out_ref, half, plus_ref)
+        target = [(first_ref[2 * e, :, at], first_ref[2 * e + 1, :, at]) for e in range(4)]
+        for i in range(low, high):
+            coher = load_coher(solved_refs, i, at)
             for u in range(4):
                 for v in range(4):
                     sums.put(*mul_conj(target[u], coher[v]))
@@ -633,12 +648,22 @@
     )
     kx_near = chip_blocks(value, "bl")
     for low, high in TARGETS:
+        [plus] = call(
+            own_target_kernel,
+            "own_targets",
+            [((tiles, (high - low) * M_ROWS, 128), F32)],
+            [],
+            [begin] + shared,
+            low=low,
+            high=high,
+            after=[value],
+        )
         [value] = call(
             target_kernel,
             "targets",
             [((tiles, (high - low) * M_ROWS, 128), F32)],
             [],
-            [first, begin] + shared,
+            [first, plus] + shared,
             low=low,
             high=high,
             after=[value, hots],

time: 56.7 us -> 56.6 us (level); the launches traced: 55.7 us -> 56.5 us
  Pallas kernels: 13.5 us -> 14.9 us
  waiting for transfers between devices: 19.1 us -> 18.5 us
    pallas_call x7 -> x8, Pallas kernels: 11.1 us -> 12.5 us  [call(): pl.pallas_call(body, out_shape=[jax.ShapeDtypeStruct(*shape) for shape in...]
    ppermute x19, waiting for transfers between devices: 19.1 us -> 18.5 us  [exchange(): lax.ppermute(block, axis, [(i, i ^ mask) for i in range(lax.axis_size(axi...]
  transfers between devices with their start and end apart: 19 -> 19, of which waited for: 10 -> 10; matrix products, arithmetic and copies ran while one was open for 4% -> 4% of each run, Pallas kernels for 7% -> 8%
where the time goes in v6:
time: 56.6 us; the launch traced here: 56.5 us
  starting transfers between devices  20 us (35%)
  waiting for transfers between devices  18.5 us (33%)
  Pallas kernels  14.9 us (26%)
  other arithmetic  2.2 us (4%)
  between operations  0.87 us (2%)
    ppermute x19, starting transfers between devices, exchange(): lax.ppermute(block, axis, [(i, i ^ mask) for i in range(lax.axis_size(axi...  20 us
    ppermute x19, waiting for transfers between devices, exchange(): lax.ppermute(block, axis, [(i, i ^ mask) for i in range(lax.axis_size(axi...  18.5 us
    pallas_call x8, Pallas kernels, call(): pl.pallas_call(body, out_shape=[jax.ShapeDtypeStruct(*shape) for shape in...  12.5 us
    pallas_call x1, Pallas kernels, on_device(): pl.pallas_call(functools.partial(prep_kernel, owned=owned, per=per), out_...  2.41 us
    add x6, other arithmetic, butterfly_sums(): sums.append(sums[-1] + exchange(sums[-1], axis, 1 << len(sums) - 1))  1.99 us
  transfers between devices with their start and end apart: 19, of which 10 were waited for; matrix products, arithmetic and copies ran while one was open for 4% of the time, Pallas kernels for 8%

profile of v6, /device:TPU:0, one launch (start us, length us, event | category | flops | bytes accessed | tf_op | source)
XLA Modules:
  0.0 56.5 jit_solution(15373528509081090467)
XLA Ops:
  0.6 2.4 %prepare.1 = (f32[56,128]{1,0:T(8,128)}, bf16[2,8,16,256]{3,2,1,0:T(8,128)(2,1)}, bf16[2,8,16,256]{3,2,1,0:T(8,128)(2,1)}) custom-call(s32[32]{0:T(128)} %refs_0_.5, s32[2,256]{1,0:T(2,128)} %stations_ref.1, f32[32,8,64]{2,1,0:T(8,128)} %refs_3_.5, bf16[8,8,16,256]{3,2,1,0:T(8,128)(2,1)} %refs_2_.5, bf16[8,8,16,256]{3,2,1,0:T(8,128)(2,1)} %refs_2_.5, ...), custom_call_target="tpu_custom_call" | custom-call | tf_op jit(solution)/shard_map/prepare/pallas_call | solution.py:587
  3.0 3.0 %collective-permute-start.6 = (bf16[2,8,16,256]{3,2,1,0:T(8,128)(2,1)}, bf16[2,8,16,256]{3,2,1,0:T(8,128)(2,1)S(1)}, u32[]{:S(2)}, u32[]{:S(2)}) collective-permute-start(bf16[2,8,16,256]{3,2,1,0:T(8,128)(2,1)} %get-tuple-element.24), channel_id=1, source_target_pairs={{0,1},{1,0},{2,3},{3,2},{4,5},{5,4},{6,7},{7,6},{8,9},{9,8},{10,11... | collective-permute-start | bytes 393224 | tf_op jit(solution)/shard_map/ppermute | solution.py:533
  6.1 1.9 %collective-permute-start = (f32[56,128]{1,0:T(8,128)}, f32[56,128]{1,0:T(8,128)S(1)}, u32[]{:S(2)}, u32[]{:S(2)}) collective-permute-start(f32[56,128]{1,0:T(8,128)} %get-tuple-element.17), channel_id=1, source_target_pairs={{0,8},{4,12},{8,0},{12,4},{16,24},{20,28},{24,16},{28,20},{1,9},{5... | collective-permute-start | bytes 86024 | tf_op jit(solution)/shard_map/ppermute | solution.py:533
  8.0 1.5 %collective-permute-start.1 = (f32[56,128]{1,0:T(8,128)}, f32[56,128]{1,0:T(8,128)S(1)}, u32[]{:S(2)}, u32[]{:S(2)}) collective-permute-start(f32[56,128]{1,0:T(8,128)} %get-tuple-element.17), channel_id=1, source_target_pairs={{0,16},{4,20},{8,24},{12,28},{16,0},{20,4},{24,8},{28,12},{1,17},{... | collective-permute-start | bytes 86024 | tf_op jit(solution)/shard_map/ppermute | solution.py:533
  9.6 1.0 %collective-permute-done.6 = bf16[2,8,16,256]{3,2,1,0:T(8,128)(2,1)S(1)} collective-permute-done((bf16[2,8,16,256]{3,2,1,0:T(8,128)(2,1)}, bf16[2,8,16,256]{3,2,1,0:T(8,128)(2,1)S(1)}, u32[]{:S(2)}, u32[]{:S(2)}) %collective-permute-start.6) | collective-permute-done | bytes 131104 | tf_op jit(solution)/shard_map/ppermute | solution.py:533
  10.6 0.9 %add.20 = bf16[2,8,16,256]{3,2,1,0:T(8,128)(2,1)S(1)} add(bf16[2,8,16,256]{3,2,1,0:T(8,128)(2,1)} %get-tuple-element.24, bf16[2,8,16,256]{3,2,1,0:T(8,128)(2,1)S(1)} %collective-permute-done.6) | non-fusion elementwise | flops 65536 | bytes 393216 | tf_op jit(solution)/shard_map/add | solution.py:539
  11.6 3.1 %collective-permute-start.7 = (bf16[2,8,16,256]{3,2,1,0:T(8,128)(2,1)S(1)}, bf16[2,8,16,256]{3,2,1,0:T(8,128)(2,1)S(1)}, u32[]{:S(2)}, u32[]{:S(2)}) collective-permute-start(bf16[2,8,16,256]{3,2,1,0:T(8,128)(2,1)S(1)} %add.20), channel_id=1, source_target_pairs={{0,2},{1,3},{2,0},{3,1},{4,6},{5,7},{6,4},{7,5},{8,10},{9,11},{10,... | collective-permute-start | bytes 393224 | tf_op jit(solution)/shard_map/ppermute | solution.py:533
  14.7 0.9 %add.22 = bf16[2,8,16,256]{3,2,1,0:T(8,128)(2,1)S(1)} add(bf16[2,8,16,256]{3,2,1,0:T(8,128)(2,1)} %get-tuple-element.25, bf16[2,8,16,256]{3,2,1,0:T(8,128)(2,1)S(1)} %collective-permute-done.8) | non-fusion elementwise | flops 65536 | bytes 393216 | tf_op jit(solution)/shard_map/add | solution.py:539
  15.6 1.0 %collective-permute-start.9 = (bf16[2,8,16,256]{3,2,1,0:T(8,128)(2,1)S(1)}, bf16[2,8,16,256]{3,2,1,0:T(8,128)(2,1)S(1)}, u32[]{:S(2)}, u32[]{:S(2)}) collective-permute-start(bf16[2,8,16,256]{3,2,1,0:T(8,128)(2,1)S(1)} %add.22), channel_id=1, source_target_pairs={{0,2},{1,3},{2,0},{3,1},{4,6},{5,7},{6,4},{7,5},{8,10},{9,11},{10,... | collective-permute-start | bytes 393224 | tf_op jit(solution)/shard_map/ppermute | solution.py:533
  16.8 1.3 %collective-permute-done.3.refs_1_.refs_5_ = f32[4,56,128]{2,1,0:T(8,128)S(1)} collective-permute-done((f32[4,56,128]{2,1,0:T(8,128)S(1)}, f32[4,56,128]{2,1,0:T(8,128)S(1)}, u32[]{:S(2)}, u32[]{:S(2)}) %collective-permute-start.3) | collective-permute-done | bytes 114720 | tf_op jit(solution)/shard_map/ppermute | solution.py:533
  18.1 1.0 %first_model.1 = (f32[8,16,256]{2,1,0:T(8,128)S(1)}, f32[32,512]{1,0:T(8,128)S(1)}) custom-call(f32[4,56,128]{2,1,0:T(8,128)S(1)} %pad_maximum_fusion.3.refs_0_.refs_4_, f32[4,56,128]{2,1,0:T(8,128)S(1)} %collective-permute-done.3.refs_1_.refs_5_, bf16[8,8,16,256]{3,2,1,0:T(8,128)(2,1)S(1)} %copy-done, f32[8,4,256]{2,1,0:T(4,128)S(1)} %copy-done.2), custom_call_target="tpu_custom_call" | custom-call | tf_op jit(solution)/shard_map/first_model/pallas_call | solution.py:569
  19.1 1.4 %collective-permute-start.4 = (f32[8,16,256]{2,1,0:T(8,128)S(1)}, f32[8,16,256]{2,1,0:T(8,128)S(1)}, u32[]{:S(2)}, u32[]{:S(2)}) collective-permute-start(f32[8,16,256]{2,1,0:T(8,128)S(1)} %get-tuple-element.18.refs_6_.refs_2_), channel_id=1, source_target_pairs={{0,1},{1,0},{2,3},{3,2},{4,5},{5,4},{6,7},{7,6},{8,9},{9,8},{10,11... | collective-permute-start | bytes 393224 | tf_op jit(solution)/shard_map/ppermute | solution.py:533
  20.4 2.8 %collective-permute-done.7 = bf16[2,8,16,256]{3,2,1,0:T(8,128)(2,1)S(1)} collective-permute-done((bf16[2,8,16,256]{3,2,1,0:T(8,128)(2,1)S(1)}, bf16[2,8,16,256]{3,2,1,0:T(8,128)(2,1)S(1)}, u32[]{:S(2)}, u32[]{:S(2)}) %collective-permute-start.7) | collective-permute-done | bytes 131104 | tf_op jit(solution)/shard_map/ppermute | solution.py:533
  23.2 1.7 %collective-permute-done.9 = bf16[2,8,16,256]{3,2,1,0:T(8,128)(2,1)S(1)} collective-permute-done((bf16[2,8,16,256]{3,2,1,0:T(8,128)(2,1)S(1)}, bf16[2,8,16,256]{3,2,1,0:T(8,128)(2,1)S(1)}, u32[]{:S(2)}, u32[]{:S(2)}) %collective-permute-start.9) | collective-permute-done | bytes 131104 | tf_op jit(solution)/shard_map/ppermute | solution.py:533
  24.9 0.8 %products.1.refs_3_.refs_4_ = f32[2,256,128]{2,1,0:T(8,128)S(1)} custom-call(bf16[2,8,16,256]{3,2,1,0:T(8,128)(2,1)S(1)} %add.21.refs_1_.refs_0_.refs_2_, bf16[2,8,16,256]{3,2,1,0:T(8,128)(2,1)S(1)} %add.23.refs_2_.refs_1_.refs_3_, f32[8,16,256]{2,1,0:T(8,128)S(1)} %get-tuple-element.18.refs_6_.refs_2_), custom_call_target="tpu_custom_call" | custom-call | tf_op jit(solution)/shard_map/products/pallas_call | solution.py:569
  25.8 1.7 %collective-permute-start.14 = (f32[2,256,128]{2,1,0:T(8,128)S(1)}, f32[2,256,128]{2,1,0:T(8,128)S(1)}, u32[]{:S(2)}, u32[]{:S(2)}) collective-permute-start(f32[2,256,128]{2,1,0:T(8,128)S(1)} %products.1.refs_3_.refs_4_), channel_id=1, source_target_pairs={{0,8},{4,12},{8,0},{12,4},{16,24},{20,28},{24,16},{28,20},{1,9},{5... | collective-permute-start | bytes 786440 | tf_op jit(solution)/shard_map/ppermute | solution.py:533
  27.5 1.5 %collective-permute-start.15 = (f32[2,256,128]{2,1,0:T(8,128)S(1)}, f32[2,256,128]{2,1,0:T(8,128)S(1)}, u32[]{:S(2)}, u32[]{:S(2)}) collective-permute-start(f32[2,256,128]{2,1,0:T(8,128)S(1)} %products.1.refs_3_.refs_4_), channel_id=1, source_target_pairs={{0,16},{4,20},{8,24},{12,28},{16,0},{20,4},{24,8},{28,12},{1,17},{... | collective-permute-start | bytes 786440 | tf_op jit(solution)/shard_map/ppermute | solution.py:533
  29.1 0.3 collective-permute-start.16
  29.5 1.4 %lookup.1 = (bf16[128,4096]{1,0:T(8,128)(2,1)S(1)}, bf16[4096,128]{1,0:T(8,128)(2,1)S(1)}, s32[8,4096]{1,0:T(8,128)S(1)}, f32[4,2,128,128]{3,2,1,0:T(8,128)S(1)}...) custom-call(s32[32]{0:T(128)S(1)} %copy-done.3, s32[32]{0:T(128)S(1)} %copy-done.4, s32[32]{0:T(128)S(1)} %copy-done.5, ...), custom_call_target="tpu_custom_call" | custom-call | tf_op jit(solution)/shard_map/lookup/pallas_call | solution.py:569
  30.9 0.6 %own_targets.1.refs_1_ = f32[2,128,128]{2,1,0:T(8,128)S(1)} custom-call(f32[32,512]{1,0:T(8,128)S(1)} %get-tuple-element.28.refs_0_, bf16[2,8,16,256]{3,2,1,0:T(8,128)(2,1)S(1)} %add.21.refs_1_.refs_0_.refs_2_, bf16[2,8,16,256]{3,2,1,0:T(8,128)(2,1)S(1)} %add.23.refs_2_.refs_1_.refs_3_, f32[2,256,128]{2,1,0:T(8,128)S(1)} %products.1.refs_3_.refs_4_), custom_call_target="tpu_custom_call" | custom-call | tf_op jit(solution)/shard_map/own_targets/pallas_call | solution.py:569
  31.5 5.2 %collective-permute-done.5 = f32[8,16,256]{2,1,0:T(8,128)S(1)} collective-permute-done((f32[8,16,256]{2,1,0:T(8,128)S(1)}, f32[8,16,256]{2,1,0:T(8,128)S(1)}, u32[]{:S(2)}, u32[]{:S(2)}) %collective-permute-start.5) | collective-permute-done | bytes 131104 | tf_op jit(solution)/shard_map/ppermute | solution.py:533
  36.7 0.4 targets.1.refs_1_
  37.1 1.7 %collective-permute-start.10 = (f32[2,128,128]{2,1,0:T(8,128)S(1)}, f32[2,128,128]{2,1,0:T(8,128)S(1)}, u32[]{:S(2)}, u32[]{:S(2)}) collective-permute-start(f32[2,128,128]{2,1,0:T(8,128)S(1)} %targets.1.refs_1_), channel_id=1, source_target_pairs={{0,8},{4,12},{8,0},{12,4},{16,24},{20,28},{24,16},{28,20},{1,9},{5... | collective-permute-start | bytes 393224 | tf_op jit(solution)/shard_map/ppermute | solution.py:533
  38.9 1.5 %collective-permute-start.11 = (f32[2,128,128]{2,1,0:T(8,128)S(1)}, f32[2,128,128]{2,1,0:T(8,128)S(1)}, u32[]{:S(2)}, u32[]{:S(2)}) collective-permute-start(f32[2,128,128]{2,1,0:T(8,128)S(1)} %targets.1.refs_1_), channel_id=1, source_target_pairs={{0,16},{4,20},{8,24},{12,28},{16,0},{20,4},{24,8},{28,12},{1,17},{... | collective-permute-start | bytes 393224 | tf_op jit(solution)/shard_map/ppermute | solution.py:533
  40.4 0.3 collective-permute-start.12
  40.7 0.9 %collective-permute-done.16 = f32[2,256,128]{2,1,0:T(8,128)S(1)} collective-permute-done((f32[2,256,128]{2,1,0:T(8,128)S(1)}, f32[2,256,128]{2,1,0:T(8,128)S(1)}, u32[]{:S(2)}, u32[]{:S(2)}) %collective-permute-start.16) | collective-permute-done | bytes 262176 | tf_op jit(solution)/shard_map/ppermute | solution.py:533
  41.8 0.5 collective-permute-start.18
  42.3 0.5 collective-permute-done.10
  42.9 1.3 %collective-permute-done.11 = f32[2,128,128]{2,1,0:T(8,128)S(1)} collective-permute-done((f32[2,128,128]{2,1,0:T(8,128)S(1)}, f32[2,128,128]{2,1,0:T(8,128)S(1)}, u32[]{:S(2)}, u32[]{:S(2)}) %collective-permute-start.11) | collective-permute-done | bytes 131104 | tf_op jit(solution)/shard_map/ppermute | solution.py:533
  44.2 2.1 %collective-permute-done.12 = f32[2,128,128]{2,1,0:T(8,128)S(1)} collective-permute-done((f32[2,128,128]{2,1,0:T(8,128)S(1)}, f32[2,128,128]{2,1,0:T(8,128)S(1)}, u32[]{:S(2)}, u32[]{:S(2)}) %collective-permute-start.12) | collective-permute-done | bytes 131104 | tf_op jit(solution)/shard_map/ppermute | solution.py:533
  46.6 1.7 %collective-permute-done.13 = f32[4,2,128,128]{3,2,1,0:T(8,128)S(1)} collective-permute-done((f32[4,2,128,128]{3,2,1,0:T(8,128)S(1)}, f32[4,2,128,128]{3,2,1,0:T(8,128)S(1)}, u32[]{:S(2)}, u32[]{:S(2)}) %collective-permute-start.13) | collective-permute-done | bytes 524320 | tf_op jit(solution)/shard_map/ppermute | solution.py:533
  48.3 8.1 %sweep.1 = (f32[32,8,64]{2,1,0:T(8,128)}, f32[8,4,256]{2,1,0:T(4,128)}) custom-call(s32[32]{0:T(128)S(1)} %copy-done.3, s32[32]{0:T(128)S(1)} %copy-done.4, s32[32]{0:T(128)S(1)} %copy-done.5, bf16[128,4096]{1,0:T(8,128)(2,1)S(1)} %get-tuple-element.19.refs_5_.refs_3_, bf16[4096,128]{1,0:T(8,128)(2,1)S(1)} %get-tuple-element.20.refs_4_, ...), custom_call_target="tpu_custom_call" | custom-call | tf_op jit(solution)/shard_map/sweep/pallas_call | solution.py:569
  (39 shorter events, 1.0 us)
Async XLA Ops:
  3.0 15.0 %copy-start = (bf16[8,8,16,256]{3,2,1,0:T(8,128)(2,1)S(1)}, bf16[8,8,16,256]{3,2,1,0:T(8,128)(2,1)}, u32[]{:S(2)}) copy-start(bf16[8,8,16,256]{3,2,1,0:T(8,128)(2,1)} %refs_2_.5) | copy-start | bytes 1572868
  3.0 7.6 %collective-permute-start.6 = (bf16[2,8,16,256]{3,2,1,0:T(8,128)(2,1)}, bf16[2,8,16,256]{3,2,1,0:T(8,128)(2,1)S(1)}, u32[]{:S(2)}, u32[]{:S(2)}) collective-permute-start(bf16[2,8,16,256]{3,2,1,0:T(8,128)(2,1)} %get-tuple-element.24), channel_id=1, source_target_pairs={{0,1},{1,0},{2,3},{3,2},{4,5},{5,4},{6,7},{7,6},{8,9},{9,8},{10,11... | collective-permute-start | bytes 393224 | tf_op jit(solution)/shard_map/ppermute | solution.py:533
  6.1 8.6 %collective-permute-start.8 = (bf16[2,8,16,256]{3,2,1,0:T(8,128)(2,1)}, bf16[2,8,16,256]{3,2,1,0:T(8,128)(2,1)S(1)}, u32[]{:S(2)}, u32[]{:S(2)}) collective-permute-start(bf16[2,8,16,256]{3,2,1,0:T(8,128)(2,1)} %get-tuple-element.25), channel_id=1, source_target_pairs={{0,1},{1,0},{2,3},{3,2},{4,5},{5,4},{6,7},{7,6},{8,9},{9,8},{10,11... | collective-permute-start | bytes 393224 | tf_op jit(solution)/shard_map/ppermute | solution.py:533
  6.1 10.5 %collective-permute-start = (f32[56,128]{1,0:T(8,128)}, f32[56,128]{1,0:T(8,128)S(1)}, u32[]{:S(2)}, u32[]{:S(2)}) collective-permute-start(f32[56,128]{1,0:T(8,128)} %get-tuple-element.17), channel_id=1, source_target_pairs={{0,8},{4,12},{8,0},{12,4},{16,24},{20,28},{24,16},{28,20},{1,9},{5... | collective-permute-start | bytes 86024 | tf_op jit(solution)/shard_map/ppermute | solution.py:533
  8.0 8.6 %collective-permute-start.1 = (f32[56,128]{1,0:T(8,128)}, f32[56,128]{1,0:T(8,128)S(1)}, u32[]{:S(2)}, u32[]{:S(2)}) collective-permute-start(f32[56,128]{1,0:T(8,128)} %get-tuple-element.17), channel_id=1, source_target_pairs={{0,16},{4,20},{8,24},{12,28},{16,0},{20,4},{24,8},{28,12},{1,17},{... | collective-permute-start | bytes 86024 | tf_op jit(solution)/shard_map/ppermute | solution.py:533
  9.5 7.1 %collective-permute-start.2 = (f32[56,128]{1,0:T(8,128)}, f32[56,128]{1,0:T(8,128)S(1)}, u32[]{:S(2)}, u32[]{:S(2)}) collective-permute-start(f32[56,128]{1,0:T(8,128)} %get-tuple-element.17), channel_id=1, source_target_pairs={{0,24},{4,28},{8,16},{12,20},{16,8},{20,12},{24,0},{28,4},{1,25},{... | collective-permute-start | bytes 86024 | tf_op jit(solution)/shard_map/ppermute | solution.py:533
  11.5 5.1 %copy-start.6 = (f32[56,128]{1,0:T(8,128)S(1)}, f32[56,128]{1,0:T(8,128)}, u32[]{:S(2)}) copy-start(f32[56,128]{1,0:T(8,128)} %get-tuple-element.17) | copy-start | bytes 86020
  11.6 11.7 %collective-permute-start.7 = (bf16[2,8,16,256]{3,2,1,0:T(8,128)(2,1)S(1)}, bf16[2,8,16,256]{3,2,1,0:T(8,128)(2,1)S(1)}, u32[]{:S(2)}, u32[]{:S(2)}) collective-permute-start(bf16[2,8,16,256]{3,2,1,0:T(8,128)(2,1)S(1)} %add.20), channel_id=1, source_target_pairs={{0,2},{1,3},{2,0},{3,1},{4,6},{5,7},{6,4},{7,5},{8,10},{9,11},{10,... | collective-permute-start | bytes 393224 | tf_op jit(solution)/shard_map/ppermute | solution.py:533
  15.6 9.3 %collective-permute-start.9 = (bf16[2,8,16,256]{3,2,1,0:T(8,128)(2,1)S(1)}, bf16[2,8,16,256]{3,2,1,0:T(8,128)(2,1)S(1)}, u32[]{:S(2)}, u32[]{:S(2)}) collective-permute-start(bf16[2,8,16,256]{3,2,1,0:T(8,128)(2,1)S(1)} %add.22), channel_id=1, source_target_pairs={{0,2},{1,3},{2,0},{3,1},{4,6},{5,7},{6,4},{7,5},{8,10},{9,11},{10,... | collective-permute-start | bytes 393224 | tf_op jit(solution)/shard_map/ppermute | solution.py:533
  16.6 1.4 %copy-start.2 = (f32[8,4,256]{2,1,0:T(4,128)S(1)}, f32[8,4,256]{2,1,0:T(4,128)}, u32[]{:S(2)}) copy-start(f32[8,4,256]{2,1,0:T(4,128)} %refs_3_.4) | copy-start | bytes 98308
  16.7 1.4 %collective-permute-start.3 = (f32[4,56,128]{2,1,0:T(8,128)S(1)}, f32[4,56,128]{2,1,0:T(8,128)S(1)}, u32[]{:S(2)}, u32[]{:S(2)}) collective-permute-start(f32[4,56,128]{2,1,0:T(8,128)S(1)} %pad_maximum_fusion.3.refs_0_.refs_4_), channel_id=1, source_target_pairs={{0,4},{4,0},{8,12},{12,8},{16,20},{20,16},{24,28},{28,24},{1,5},{5... | collective-permute-start | bytes 344072 | tf_op jit(solution)/shard_map/ppermute | solution.py:533
  19.1 10.3 %collective-permute-start.4 = (f32[8,16,256]{2,1,0:T(8,128)S(1)}, f32[8,16,256]{2,1,0:T(8,128)S(1)}, u32[]{:S(2)}, u32[]{:S(2)}) collective-permute-start(f32[8,16,256]{2,1,0:T(8,128)S(1)} %get-tuple-element.18.refs_6_.refs_2_), channel_id=1, source_target_pairs={{0,1},{1,0},{2,3},{3,2},{4,5},{5,4},{6,7},{7,6},{8,9},{9,8},{10,11... | collective-permute-start | bytes 393224 | tf_op jit(solution)/shard_map/ppermute | solution.py:533
  25.8 3.7 %copy-start.1 = (f32[32,8,64]{2,1,0:T(8,128)S(1)}, f32[32,8,64]{2,1,0:T(8,128)}, u32[]{:S(2)}) copy-start(f32[32,8,64]{2,1,0:T(8,128)} %refs_3_.5) | copy-start | bytes 196612
  25.8 3.7 %copy-start.3 = (s32[32]{0:T(128)S(1)}, s32[32]{0:T(128)}, u32[]{:S(2)}) copy-start(s32[32]{0:T(128)} %refs_0_.5) | copy-start | bytes 388
  25.8 3.7 %copy-start.4 = (s32[32]{0:T(128)S(1)}, s32[32]{0:T(128)}, u32[]{:S(2)}) copy-start(s32[32]{0:T(128)} %refs_1_.5) | copy-start | bytes 388
  25.8 3.7 %copy-start.5 = (s32[32]{0:T(128)S(1)}, s32[32]{0:T(128)}, u32[]{:S(2)}) copy-start(s32[32]{0:T(128)} %refs_2_.7) | copy-start | bytes 388
  25.8 14.6 %collective-permute-start.14 = (f32[2,256,128]{2,1,0:T(8,128)S(1)}, f32[2,256,128]{2,1,0:T(8,128)S(1)}, u32[]{:S(2)}, u32[]{:S(2)}) collective-permute-start(f32[2,256,128]{2,1,0:T(8,128)S(1)} %products.1.refs_3_.refs_4_), channel_id=1, source_target_pairs={{0,8},{4,12},{8,0},{12,4},{16,24},{20,28},{24,16},{28,20},{1,9},{5... | collective-permute-start | bytes 786440 | tf_op jit(solution)/shard_map/ppermute | solution.py:533
  27.5 13.2 %collective-permute-start.15 = (f32[2,256,128]{2,1,0:T(8,128)S(1)}, f32[2,256,128]{2,1,0:T(8,128)S(1)}, u32[]{:S(2)}, u32[]{:S(2)}) collective-permute-start(f32[2,256,128]{2,1,0:T(8,128)S(1)} %products.1.refs_3_.refs_4_), channel_id=1, source_target_pairs={{0,16},{4,20},{8,24},{12,28},{16,0},{20,4},{24,8},{28,12},{1,17},{... | collective-permute-start | bytes 786440 | tf_op jit(solution)/shard_map/ppermute | solution.py:533
  29.1 12.5 %collective-permute-start.16 = (f32[2,256,128]{2,1,0:T(8,128)S(1)}, f32[2,256,128]{2,1,0:T(8,128)S(1)}, u32[]{:S(2)}, u32[]{:S(2)}) collective-permute-start(f32[2,256,128]{2,1,0:T(8,128)S(1)} %products.1.refs_3_.refs_4_), channel_id=1, source_target_pairs={{0,24},{4,28},{8,16},{12,20},{16,8},{20,12},{24,0},{28,4},{1,25},{... | collective-permute-start | bytes 786440 | tf_op jit(solution)/shard_map/ppermute | solution.py:533
  29.4 7.3 %collective-permute-start.5 = (f32[8,16,256]{2,1,0:T(8,128)S(1)}, f32[8,16,256]{2,1,0:T(8,128)S(1)}, u32[]{:S(2)}, u32[]{:S(2)}) collective-permute-start(f32[8,16,256]{2,1,0:T(8,128)S(1)} %add.18), channel_id=1, source_target_pairs={{0,2},{1,3},{2,0},{3,1},{4,6},{5,7},{6,4},{7,5},{8,10},{9,11},{10,... | collective-permute-start | bytes 393224 | tf_op jit(solution)/shard_map/ppermute | solution.py:533
  37.1 5.7 %collective-permute-start.10 = (f32[2,128,128]{2,1,0:T(8,128)S(1)}, f32[2,128,128]{2,1,0:T(8,128)S(1)}, u32[]{:S(2)}, u32[]{:S(2)}) collective-permute-start(f32[2,128,128]{2,1,0:T(8,128)S(1)} %targets.1.refs_1_), channel_id=1, source_target_pairs={{0,8},{4,12},{8,0},{12,4},{16,24},{20,28},{24,16},{28,20},{1,9},{5... | collective-permute-start | bytes 393224 | tf_op jit(solution)/shard_map/ppermute | solution.py:533
  38.9 5.3 %collective-permute-start.11 = (f32[2,128,128]{2,1,0:T(8,128)S(1)}, f32[2,128,128]{2,1,0:T(8,128)S(1)}, u32[]{:S(2)}, u32[]{:S(2)}) collective-permute-start(f32[2,128,128]{2,1,0:T(8,128)S(1)} %targets.1.refs_1_), channel_id=1, source_target_pairs={{0,16},{4,20},{8,24},{12,28},{16,0},{20,4},{24,8},{28,12},{1,17},{... | collective-permute-start | bytes 393224 | tf_op jit(solution)/shard_map/ppermute | solution.py:533
  40.4 5.9 %collective-permute-start.12 = (f32[2,128,128]{2,1,0:T(8,128)S(1)}, f32[2,128,128]{2,1,0:T(8,128)S(1)}, u32[]{:S(2)}, u32[]{:S(2)}) collective-permute-start(f32[2,128,128]{2,1,0:T(8,128)S(1)} %targets.1.refs_1_), channel_id=1, source_target_pairs={{0,24},{4,28},{8,16},{12,20},{16,8},{20,12},{24,0},{28,4},{1,25},{... | collective-permute-start | bytes 393224 | tf_op jit(solution)/shard_map/ppermute | solution.py:533
  41.8 4.8 %collective-permute-start.17 = (f32[2,2,256,128]{3,2,1,0:T(8,128)S(1)}, f32[2,2,256,128]{3,2,1,0:T(8,128)S(1)}, u32[]{:S(2)}, u32[]{:S(2)}) collective-permute-start(f32[2,2,256,128]{3,2,1,0:T(8,128)S(1)} %get-tuple-element.29), channel_id=1, source_target_pairs={{0,4},{4,0},{8,12},{12,8},{16,20},{20,16},{24,28},{28,24},{1,5},{5... | collective-permute-start | bytes 1572872 | tf_op jit(solution)/shard_map/ppermute | solution.py:533
  41.8 4.7 %collective-permute-start.18 = (f32[2,2,256,128]{3,2,1,0:T(8,128)S(1)}, f32[2,2,256,128]{3,2,1,0:T(8,128)S(1)}, u32[]{:S(2)}, u32[]{:S(2)}) collective-permute-start(f32[2,2,256,128]{3,2,1,0:T(8,128)S(1)} %get-tuple-element.30), channel_id=1, source_target_pairs={{0,4},{4,0},{8,12},{12,8},{16,20},{20,16},{24,28},{28,24},{1,5},{5... | collective-permute-start | bytes 1572872 | tf_op jit(solution)/shard_map/ppermute | solution.py:533
  46.3 2.0 %collective-permute-start.13 = (f32[4,2,128,128]{3,2,1,0:T(8,128)S(1)}, f32[4,2,128,128]{3,2,1,0:T(8,128)S(1)}, u32[]{:S(2)}, u32[]{:S(2)}) collective-permute-start(f32[4,2,128,128]{3,2,1,0:T(8,128)S(1)} %pad_maximum_fusion.2), channel_id=1, source_target_pairs={{0,4},{4,0},{8,12},{12,8},{16,20},{20,16},{24,28},{28,24},{1,5},{5... | collective-permute-start | bytes 1572872 | tf_op jit(solution)/shard_map/ppermute | solution.py:533
